TPU v7x, 128 devices: a whole 4x4x4 slice. The times are simulated.
128 devices in a mesh: group: 32 (over y, z, core), tensor: 4 (over x).
Axes of the slice: x: 4, y: 4, z: 4, core: 2. Of those that a mesh axis runs over, the one named last changes fastest.
Arguments:
- queries: bfloat16 [4096, 8192], P('group', 'tensor'), may hold values from -256 to 256
- hidden_rows: bfloat16 [4096, 8192], P(('group', 'tensor')), may hold values from -6 to 6
- kv_weight: bfloat16 [2, 8192, 1024], P(None, None, 'tensor'), may hold values from -0.0625 to 0.0625
- cache_keys: bfloat16 [4096, 1024], P('group', 'tensor'), may hold values from -8 to 8
- cache_values: bfloat16 [4096, 1024], P('group', 'tensor'), may hold values from -6 to 6
- kv_blocks: int32 [32], replicated, may hold values from 1 to 4, 64 in all
Outputs:
- attended: bfloat16 [4096, 8192], P('group', 'tensor')
- new_keys: bfloat16 [4096, 1024], P('group', 'tensor')
- new_values: bfloat16 [4096, 1024], P('group', 'tensor')
Inputs may be any that keep to these rules, and one draw needn't show every extreme that they name: `kv_blocks`: they sum to 32 * 4 // 2 over the groups, and some group has 4.
All inputs are finite; a program needn't handle non-finite values.
Results may differ from a plain program's by a relative error of at most 0.009.
Values may be sent and summed in bfloat16 or wider, within the bound.
No kernel may reach another device: no remote copies, remote signals or barrier semaphores. Data moves between devices by JAX's collectives and lax.ppermute only.
A program may use at most 64 MiB of HBM per device.

v0:
```python
import math

import jax
import jax.numpy as jnp
from jax import lax
from jax.sharding import PartitionSpec as P

HEADS = 64
KV_HEADS = 8
HEAD_DIM = 128
BLOCK = 32


def rotate(key_proj, positions, head_dim):
    rows = key_proj.shape[0]
    half = head_dim // 2
    heads3 = key_proj.reshape(rows, -1, head_dim)
    freq = jnp.exp(jnp.arange(half, dtype=jnp.float32) * (-2.0 * math.log(500000.0) / head_dim))
    angle = positions.astype(jnp.float32)[:, None] * freq[None, :]
    cosine = jnp.cos(angle)[:, None, :]
    sine = jnp.sin(angle)[:, None, :]
    first = heads3[..., :half]
    second = heads3[..., half:]
    turned = jnp.concatenate([first * cosine - second * sine, second * cosine + first * sine], -1)
    return turned.reshape(rows, -1)


def shards(queries, hidden_rows, kv_weight, cache_keys, cache_values, kv_blocks):
    group = lax.axis_index("group")
    new_rows = hidden_rows.shape[0] * lax.axis_size("tensor")
    local_kv = kv_weight.shape[2]
    kv_local = local_kv // HEAD_DIM
    share = HEADS // KV_HEADS
    prefix_cap = cache_keys.shape[0]
    scale = 1.0 / math.sqrt(HEAD_DIM)
    piece = lax.all_gather(hidden_rows, "tensor", axis=0, tiled=True)
    joined = jnp.einsum("rd,kdc->rkc", piece, kv_weight, preferred_element_type=jnp.float32)
    projected = joined.reshape(piece.shape[0], 2 * local_kv)
    prefix_len = jnp.sum(kv_blocks) * BLOCK
    query_rows = group * new_rows + jnp.arange(new_rows, dtype=jnp.int32)
    new_keys = rotate(projected[:, :local_kv], prefix_len + query_rows, HEAD_DIM).astype(
        jnp.bfloat16
    )
    new_values = projected[:, local_kv:].astype(jnp.bfloat16)
    query_heads = queries.reshape(new_rows, kv_local, share, HEAD_DIM)
    group_ids = jnp.arange(kv_blocks.shape[0], dtype=jnp.int32)

    def block_terms(keys, values, visible):
        length = keys.shape[0]
        keys3 = keys.reshape(length, kv_local, HEAD_DIM)
        values3 = values.reshape(length, kv_local, HEAD_DIM)
        scores = (
            jnp.einsum("rksd,lkd->ksrl", query_heads, keys3, preferred_element_type=jnp.float32)
            * scale
        )
        top_block = jnp.max(jnp.where(visible, scores, -1e30), -1)
        weights = jnp.where(visible, jnp.exp(scores - top_block[..., None]), 0.0)
        numerator = jnp.einsum(
            "ksrl,lkd->ksrd",
            weights.astype(jnp.bfloat16),
            values3,
            preferred_element_type=jnp.float32,
        )
        return (top_block, numerator, jnp.sum(weights, -1))

    def absorb(carry, terms):
        highest, numerator, denominator = carry
        top_block, block_num, block_den = terms
        raised = jnp.maximum(highest, top_block)
        keep_old = jnp.exp(highest - raised)
        keep_new = jnp.exp(top_block - raised)
        return (
            raised,
            numerator * keep_old[..., None] + block_num * keep_new[..., None],
            denominator * keep_old + block_den * keep_new,
        )

    def cache_block(carry, keys, values, source):
        live_rows = jnp.sum(jnp.where(group_ids == source, kv_blocks, 0)) * BLOCK
        visible = jnp.broadcast_to(
            jnp.arange(prefix_cap, dtype=jnp.int32)[None, :] < live_rows, (new_rows, prefix_cap)
        )
        return absorb(carry, block_terms(keys, values, visible))

    def new_block(carry, keys, values, source):
        key_rows = source * new_rows + jnp.arange(new_rows, dtype=jnp.int32)
        visible = key_rows[None, :] <= query_rows[:, None]
        return absorb(carry, block_terms(keys, values, visible))

    init = (
        jnp.full((kv_local, share, new_rows), -1e30, jnp.float32),
        jnp.zeros((kv_local, share, new_rows, HEAD_DIM), jnp.float32),
        jnp.zeros((kv_local, share, new_rows), jnp.float32),
    )
    span = prefix_cap + new_rows
    joined_keys = jnp.concatenate([cache_keys, new_keys], 0)
    joined_values = jnp.concatenate([cache_values, new_values], 0)
    carry = init
    keys_all = lax.all_gather(joined_keys, "group", axis=0, tiled=True)
    values_all = lax.all_gather(joined_values, "group", axis=0, tiled=True)
    count = keys_all.shape[0] // span

    def visit(inner, item):
        key_item, value_item, offset = item
        inner = cache_block(inner, key_item[:prefix_cap], value_item[:prefix_cap], offset)
        inner = new_block(inner, key_item[prefix_cap:], value_item[prefix_cap:], offset)
        return (inner, None)

    carry, unused = lax.scan(
        visit,
        carry,
        (
            keys_all.reshape(count, span, local_kv),
            values_all.reshape(count, span, local_kv),
            jnp.arange(count, dtype=jnp.int32),
        ),
    )
    highest, numerator, denominator = carry
    attended = (numerator / denominator[..., None]).transpose(2, 0, 1, 3)
    attended = attended.reshape(new_rows, kv_local * share * HEAD_DIM).astype(jnp.bfloat16)
    return (attended, new_keys, new_values)


def solution(mesh):
    placed = (
        P("group", "tensor"),
        P(("group", "tensor"), None),
        P(None, None, "tensor"),
        P("group", "tensor"),
        P("group", "tensor"),
        P(),
    )
    return jax.shard_map(
        shards,
        mesh=mesh,
        in_specs=placed,
        out_specs=(P("group", "tensor"), P("group", "tensor"), P("group", "tensor")),
        check_vma=False,
    )
```

profile of v0, /device:TPU:25, one launch (start us, length us, event | category | flops | bytes accessed | tf_op | source)
XLA Modules:
  0.0 423.2 jit_solution(11416779646588892868)
XLA Ops:
  8.9 33.7 %all-gather.4.cloned.1.call-done = bf16[128,8192]{1,0:T(8,128)(2,1)} async-done(((bf16[32,8192]{1,0:T(8,128)(2,1)}), bf16[128,8192]{1,0:T(8,128)(2,1)}) %all-gather.4.cloned.1.call-update) | async-done | bytes 2097168 | tf_op jit(solution)/shard_map/all_gather | solution.py:36
  42.6 7.4 %fusion.26 = f32[128,2,256]{0,2,1:T(8,128)S(1)} fusion(bf16[2,8192,256]{2,1,0:T(8,128)(2,1)} %param.10, bf16[128,8192]{1,0:T(8,128)(2,1)} %all-gather.4.cloned.1.call-done), kind=kOutput, calls=%fused_computation.48 | convolution fusion | flops 1073741824 | bytes 10747904 | tf_op jit(solution)/shard_map/rd,kdc->rkc/dot_general | solution.py:37
  54.5 45.7 %all-gather.8.cloned.1.call-done = bf16[8192,256]{0,1:T(8,128)(2,1)} async-done(((bf16[256,256]{0,1:T(8,128)(2,1)}), bf16[8192,256]{0,1:T(8,128)(2,1)}) %all-gather.8.cloned.1.call-update) | async-done | bytes 4194320 | tf_op jit(solution)/shard_map/all_gather | solution.py:100
  100.2 4.7 %copy.50 = bf16[32,32,8,256]{3,2,0,1:T(8,128)(2,1)} copy(bf16[32,32,8,256]{3,2,1,0:T(8,128)(2,1)} %bitcast.78) | data formatting | bytes 8388608 | tf_op jit(solution)/shard_map/reshape | solution.py:114
  104.9 43.9 %all-gather.6.cloned.1.call-done = bf16[8192,256]{1,0:T(8,128)(2,1)} async-done(((bf16[256,256]{1,0:T(8,128)(2,1)}), bf16[8192,256]{1,0:T(8,128)(2,1)}) %all-gather.6.cloned.1.call-update) | async-done | bytes 4194320 | tf_op jit(solution)/shard_map/all_gather | solution.py:99
  148.9 266.2 %while.17 = (s32[]{:T(128)}, f32[2,8,128]{2,1,0:T(8,128)S(1)}, f32[2,8,128,128]{3,2,1,0:T(8,128)S(1)}, f32[2,8,128]{2,1,0:T(8,128)S(1)}, s32[32]{0:T(128)S(1)}, ...) while((s32[]{:T(128)}, f32[2,8,128]{2,1,0:T(8,128)S(1)}, ...), condition=%wide.region_7.8_spmd.clone.clone, body=%wide.region_1.7_spmd.clone.clone.sunk | while | flops 275026400 | bytes 12848116 | solution.py:109
  150.1 1.3 fusion.60
  155.5 1.1 fusion.63
  158.4 1.3 fusion.60
  163.8 1.1 fusion.63
  166.7 1.3 fusion.60
  172.1 1.1 fusion.63
  175.1 1.3 fusion.60
  180.4 1.1 fusion.63
  183.4 1.3 fusion.60
  188.8 1.1 fusion.63
  191.7 1.3 fusion.60
  197.1 1.1 fusion.63
  200.0 1.3 fusion.60
  205.4 1.1 fusion.63
  208.3 1.3 fusion.60
  213.7 1.1 fusion.63
  216.7 1.3 fusion.60
  222.0 1.1 fusion.63
  225.0 1.3 fusion.60
  230.4 1.1 fusion.63
  233.3 1.3 fusion.60
  238.7 1.1 fusion.63
  241.6 1.3 fusion.60
  247.0 1.1 fusion.63
  249.9 1.3 fusion.60
  255.3 1.1 fusion.63
  258.3 1.3 fusion.60
  263.6 1.1 fusion.63
  266.6 1.3 fusion.60
  272.0 1.1 fusion.63
  274.9 1.3 fusion.60
  280.3 1.1 fusion.63
  283.2 1.3 fusion.60
  288.6 1.1 fusion.63
  291.5 1.3 fusion.60
  296.9 1.1 fusion.63
  299.9 1.3 fusion.60
  305.2 1.1 fusion.63
  308.2 1.3 fusion.60
  313.6 1.1 fusion.63
  316.5 1.3 fusion.60
  321.9 1.1 fusion.63
  324.8 1.3 fusion.60
  330.2 1.1 fusion.63
  333.1 1.3 fusion.60
  338.5 1.1 fusion.63
  341.5 1.3 fusion.60
  346.8 1.1 fusion.63
  349.8 1.3 fusion.60
  355.2 1.1 fusion.63
  358.1 1.3 fusion.60
  363.5 1.1 fusion.63
  366.4 1.3 fusion.60
  374.7 1.3 fusion.60
  383.1 1.3 fusion.60
  391.4 1.3 fusion.60
  399.7 1.3 fusion.60
  408.0 1.3 fusion.60
  (490 shorter events, 155.2 us)
Async XLA Ops:
  7.2 35.4 %all-gather.4.cloned.1.call-start = ((), (), s32[]{:S(2)}) async-start(), calls=%async_computation | async-start | bytes 2621440 | tf_op jit(solution)/shard_map/all_gather | solution.py:36
  7.9 92.3 %all-gather.8.cloned.1.call-start = ((), (), s32[]{:S(2)}) async-start(), calls=%async_computation.2 | async-start | bytes 4325376 | tf_op jit(solution)/shard_map/all_gather | solution.py:100
  8.9 41.8 %copy-start.3 = (s32[32]{0:T(128)S(1)}, s32[32]{0:T(128)}, u32[]{:S(2)}) copy-start(s32[32]{0:T(128)} %param.13) | copy-start | bytes 388
  8.9 43.5 %copy-start.2 = (bf16[128,256]{1,0:T(8,128)(2,1)S(1)}, bf16[128,256]{1,0:T(8,128)(2,1)}, u32[]{:S(2)}) copy-start(bf16[128,256]{1,0:T(8,128)(2,1)} %param.11) | copy-start | bytes 196612
  8.9 44.3 %copy-start = (bf16[128,2048]{1,0:T(8,128)(2,1)S(1)}, bf16[128,2048]{1,0:T(8,128)(2,1)}, u32[]{:S(2)}) copy-start(bf16[128,2048]{1,0:T(8,128)(2,1)} %param.8) | copy-start | bytes 1572868
  50.7 98.2 %all-gather.6.cloned.1.call-start = ((), (), s32[]{:S(2)}) async-start(), calls=%async_computation.1 | async-start | bytes 4325376 | tf_op jit(solution)/shard_map/all_gather | solution.py:99
  52.5 52.5 %copy-start.1 = (bf16[128,256]{1,0:T(8,128)(2,1)}, bf16[128,256]{1,0:T(8,128)(2,1)S(1)}, u32[]{:S(2)}) copy-start(bf16[128,256]{1,0:T(8,128)(2,1)S(1)} %copy.34) | copy-start | bytes 196612
Sparse Core Ops, SparseCore 0:
  9.7 32.9 all-gather.3
  50.8 49.3 all-gather.7
  103.1 45.7 all-gather.5
where the time goes:
time: 429 us; the launch traced here: 423 us
  waiting for transfers between devices  124 us (29%)
  local copies, waits for them, and re-layouts  91.4 us (21%)
  matrix products  84.3 us (20%)
  other arithmetic  63 us (15%)
  loops' own time  45.9 us (11%)
  between operations  14.6 us (3%)
    dot_general x64, matrix products, block_terms(): jnp.einsum('ksrl,lkd->ksrd', weights.astype(jnp.bfloat16), values3, prefe...  53.3 us
    another operation x1, loops' own time, shards(): lax.scan(visit, carry, (keys_all.reshape(count, span, local_kv), values_a...  45.9 us
    all_gather x1, waiting for transfers between devices, shards(): values_all = lax.all_gather(joined_values, 'group', axis=0, tiled=True)  45.7 us
    all_gather x1, waiting for transfers between devices, shards(): keys_all = lax.all_gather(joined_keys, 'group', axis=0, tiled=True)  43.9 us
    reduce_sum x32, other arithmetic, cache_block(): live_rows = jnp.sum(jnp.where(group_ids == source, kv_blocks, 0)) * BLOCK  42.9 us
    all_gather x1, waiting for transfers between devices, shards(): piece = lax.all_gather(hidden_rows, 'tensor', axis=0, tiled=True)  33.7 us
    slice x32, local copies, waits for them, and re-layouts, visit(): value_item[prefix_cap:]  28.5 us
    slice x32, local copies, waits for them, and re-layouts, visit(): key_item[:prefix_cap]  28.5 us
  transfers between devices with their start and end apart: 3, of which 3 were waited for; matrix products, arithmetic and copies ran while one was open for 2% of the time, Pallas kernels for 0%

commit v1 on v0

v1 whole, which is shorter than its diff:
```python
import functools
import math

import jax
import jax.numpy as jnp
from jax import lax
from jax.experimental import pallas as pl
from jax.experimental.pallas import tpu as pltpu
from jax.sharding import PartitionSpec as P

HEAD_DIM = 128
BLOCK = 32
ROWS = 128
SHARE = 8
SIDE = 4
EXPONENT = math.log2(math.e) / math.sqrt(HEAD_DIM)
BACK = (0, 1, 3, 2)
VMEM = pl.BlockSpec(memory_space=pltpu.VMEM)
SMEM = pl.BlockSpec(memory_space=pltpu.SMEM)
F32 = jnp.float32
BF16 = jnp.bfloat16


def swap_cores():
    return [(i, i ^ 1) for i in range(2 * SIDE * SIDE)]


def along(phase, distance):
    pairs = []
    for y in range(SIDE):
        for z in range(SIDE):
            for core in range(2):
                if (core + phase) % 2 == 0:
                    to = (y, (z + distance) % SIDE)
                else:
                    to = ((y + distance) % SIDE, z)
                pairs.append(((y * SIDE + z) * 2 + core, (to[0] * SIDE + to[1]) * 2 + core))
    return pairs


def ring(distance):
    return [(x, (x + distance) % SIDE) for x in range(SIDE)]


def sender(info, piece, slot):
    core, y, z = info[0], info[1], info[2]
    first, second = BACK[slot], BACK[piece]
    dy = jnp.where(core == 0, second, first)
    dz = jnp.where(core == 0, first, second)
    return lax.rem(y - dy + SIDE, SIDE) * SIDE + lax.rem(z - dz + SIDE, SIDE)


def pack_kernel(info, keys, values, queries, mine, give, own_queries):
    core = info[0]
    width = SHARE * HEAD_DIM
    for which, target, target_queries, start in (
        (core, mine, own_queries, 0),
        (1 - core, give, give, 2 * ROWS),
    ):
        head = pl.ds(pl.multiple_of(which * HEAD_DIM, HEAD_DIM), HEAD_DIM)
        target[0:ROWS, :] = keys[:, head]
        target[ROWS : 2 * ROWS, :] = values[:, head]
        for h in range(SHARE):
            columns = pl.ds(pl.multiple_of(which * width + h * HEAD_DIM, HEAD_DIM), HEAD_DIM)
            target_queries[start + h * ROWS : start + (h + 1) * ROWS, :] = queries[:, columns]


def pack(info, keys, values, queries):
    return pl.pallas_call(
        pack_kernel,
        out_shape=(
            jax.ShapeDtypeStruct((2 * ROWS, HEAD_DIM), BF16),
            jax.ShapeDtypeStruct(((2 + SHARE) * ROWS, HEAD_DIM), BF16),
            jax.ShapeDtypeStruct((SHARE * ROWS, HEAD_DIM), BF16),
        ),
        in_specs=[SMEM, VMEM, VMEM, VMEM],
        out_specs=(VMEM, VMEM, VMEM),
        name="pack",
    )(info, keys, values, queries)


def project_kernel(info, *refs):
    pieces, (weight, cosine, sine) = refs[:7], refs[7:10]
    new_keys, new_values, mine, give, rows = refs[10:]
    core, x = info[0], info[3]
    size = pieces[1].shape[0]
    rows[pl.ds(pl.multiple_of(x * 2 * size, size), 2 * size), :] = pieces[0][...]
    for piece, back, half in zip(pieces[1:], (1, 3, 1, 3, 2, 2), (0, 1, 1, 0, 0, 1)):
        place = lax.rem(x - back + SIDE, SIDE) * 2 + half
        rows[pl.ds(pl.multiple_of(place * size, size), size), :] = piece[...]
    depth = weight.shape[1]
    step = 1024

    def add(i, totals):
        part = pl.ds(pl.multiple_of(i * step, step), step)
        block = rows[:, part]
        return tuple(
            total + jnp.dot(block, weight[k, part, :], preferred_element_type=F32)
            for k, total in enumerate(totals)
        )

    zero = jnp.zeros((ROWS, 2 * HEAD_DIM), F32)
    keys, values = lax.fori_loop(0, depth // step, add, (zero, zero))
    for h in range(2):
        head = slice(h * HEAD_DIM, (h + 1) * HEAD_DIM)
        key = keys[:, head]
        turned = key * cosine[...] + pltpu.roll(key, HEAD_DIM // 2, 1) * sine[...]
        new_keys[:, head] = turned.astype(BF16)
        new_values[:, head] = values[:, head].astype(BF16)
    for which, target in ((core, mine), (1 - core, give)):
        head = pl.ds(pl.multiple_of(which * HEAD_DIM, HEAD_DIM), HEAD_DIM)
        target[0:ROWS, :] = new_keys[:, head]
        target[ROWS : 2 * ROWS, :] = new_values[:, head]


def project(info, pieces, weight, cosine, sine):
    wide = jax.ShapeDtypeStruct((ROWS, 2 * HEAD_DIM), BF16)
    tall = jax.ShapeDtypeStruct((2 * ROWS, HEAD_DIM), BF16)
    return pl.pallas_call(
        project_kernel,
        out_shape=(wide, wide, tall, tall),
        in_specs=[SMEM] + [VMEM] * 10,
        out_specs=(VMEM,) * 4,
        scratch_shapes=[pltpu.VMEM((ROWS, weight.shape[1]), BF16)],
        compiler_params=pltpu.CompilerParams(vmem_limit_bytes=32 << 20),
        name="project",
    )(info, *pieces, weight, cosine, sine)


def absorb(query, turned_keys, values, state, visible=None):
    top, den, num = state
    scores = jnp.dot(query, turned_keys, preferred_element_type=F32)
    if visible is not None:
        scores = jnp.where(visible, scores, -1e30)
    raised = jnp.maximum(top, jnp.max(scores, axis=1, keepdims=True))
    weights = [
        jnp.exp2((scores[:, i : i + HEAD_DIM] - raised) * EXPONENT)
        for i in range(0, scores.shape[1], HEAD_DIM)
    ]
    keep = jnp.exp2((top - raised) * EXPONENT)
    den = den * keep + functools.reduce(lambda a, b: a + b, weights)
    rounded = jnp.concatenate([w.astype(BF16) for w in weights], 1)
    num = num * keep + jnp.dot(rounded, values, preferred_element_type=F32)
    return raised, den, num


def query_of(own_queries, received, head):
    row = pl.multiple_of(head * ROWS, ROWS)
    there = pl.multiple_of(head * ROWS + 2 * ROWS, ROWS)
    return jnp.concatenate([own_queries[pl.ds(row, ROWS), :], received[pl.ds(there, ROWS), :]], 0)


def cache_kernel(live_keys, info, kv_blocks, own_queries, received, *refs):
    pieces, states = refs[:4], refs[4:7]
    keys, values, turned = refs[7:]
    core = info[0]
    place = jnp.int32(0)
    for piece in range(SIDE):
        for slot in range(SIDE):
            chip = sender(info, piece, slot)
            for half in range(2):
                group = chip * 2 + (core if half == 0 else 1 - core)
                row = slot * 4 * ROWS + half * 2 * ROWS
                there = pl.ds(pl.multiple_of(place, BLOCK), ROWS)
                keys[there, :] = pieces[piece][row : row + ROWS, :]
                values[there, :] = pieces[piece][row + ROWS : row + 2 * ROWS, :]
                place = place + kv_blocks[group] * BLOCK
    for i in range(0, live_keys, 256):
        turned[:, i : i + 256] = keys[i : i + 256, :].T
    size = 2 * ROWS
    step = 512

    def one_head(head, _):
        query = query_of(own_queries, received, head)
        state = (
            jnp.full((size, HEAD_DIM), -1e30, F32),
            jnp.zeros((size, HEAD_DIM), F32),
            jnp.zeros((size, HEAD_DIM), F32),
        )
        for i in range(0, live_keys, step):
            state = absorb(query, turned[:, i : i + step], values[i : i + step, :], state)
        rows = pl.ds(pl.multiple_of(head * size, size), size)
        for ref, value in zip(states, state):
            ref[rows, :] = value
        return 0

    lax.fori_loop(0, SHARE, one_head, 0)


STATE = jax.ShapeDtypeStruct((2 * SHARE * ROWS, HEAD_DIM), F32)


def attend_cache(info, kv_blocks, own_queries, received, pieces, live_keys):
    return pl.pallas_call(
        functools.partial(cache_kernel, live_keys),
        out_shape=(STATE,) * 3,
        in_specs=[SMEM, SMEM] + [VMEM] * 6,
        out_specs=(VMEM,) * 3,
        scratch_shapes=[
            pltpu.VMEM((live_keys + ROWS, HEAD_DIM), BF16),
            pltpu.VMEM((live_keys + ROWS, HEAD_DIM), BF16),
            pltpu.VMEM((HEAD_DIM, live_keys), BF16),
        ],
        compiler_params=pltpu.CompilerParams(vmem_limit_bytes=24 << 20),
        name="attend_cache",
    )(info, kv_blocks, own_queries, received, *pieces)


def new_kernel(which, last, info, own_queries, received, *refs):
    count = len(which)
    pieces, states = refs[:count], refs[count : count + 3]
    outs, (turned,) = refs[count + 3 : -1], refs[-1:]
    core, me = info[0], info[1] * SIDE + info[2]
    size = 2 * ROWS
    if not last:
        for ref, old in zip(outs, states):
            ref[...] = old[...]
        states = outs

    def visit(ref, slot, visible):
        base = slot * 4 * ROWS
        keys = jnp.concatenate(
            [ref[base : base + ROWS, :], ref[base + 2 * ROWS : base + 3 * ROWS, :]], 0
        )
        turned[...] = keys.T

        def one_head(head, _):
            rows = pl.ds(pl.multiple_of(head * size, size), size)
            values = jnp.concatenate(
                [
                    ref[base + ROWS : base + 2 * ROWS, :],
                    ref[base + 3 * ROWS : base + 4 * ROWS, :],
                ],
                0,
            )
            state = absorb(
                query_of(own_queries, received, head),
                turned[...],
                values,
                tuple(s[rows, :] for s in states),
                visible() if visible else None,
            )
            for s, value in zip(states, state):
                s[rows, :] = value
            return 0

        lax.fori_loop(0, SHARE, one_head, 0)

    def causal():
        def position(axis):
            at = lax.broadcasted_iota(jnp.int32, (size, size), axis)
            return jnp.where(core == 0, at, lax.rem(at + ROWS, size))

        return position(1) <= position(0)

    for piece, ref in zip(which, pieces):
        for slot in range(SIDE):
            if piece == 0 and slot == 0:
                visit(ref, slot, causal)
                continue
            pl.when(sender(info, piece, slot) < me)(
                functools.partial(visit, ref, slot, None)
            )
    if last:
        here, there = outs

        for head in range(SHARE):
            rows = slice(head * size, (head + 1) * size)
            den = jnp.sum(states[1][rows, :], axis=1, keepdims=True)
            result = (states[2][rows, :] / den).astype(BF16)
            columns = slice(head * HEAD_DIM, (head + 1) * HEAD_DIM)
            here[:, columns] = result[:ROWS]
            there[:, columns] = result[ROWS:]


def attend_new(info, own_queries, received, which, pieces, states, last):
    out = jax.ShapeDtypeStruct((ROWS, SHARE * HEAD_DIM), BF16)
    aliases = {} if last else {3 + len(which) + i: i for i in range(3)}
    return pl.pallas_call(
        functools.partial(new_kernel, which, last),
        out_shape=(out, out) if last else (STATE,) * 3,
        in_specs=[SMEM] + [VMEM] * (2 + len(which) + 3),
        out_specs=(VMEM,) * (2 if last else 3),
        scratch_shapes=[pltpu.VMEM((HEAD_DIM, 2 * ROWS), BF16)],
        compiler_params=pltpu.CompilerParams(vmem_limit_bytes=24 << 20),
        name="attend_new_last" if last else "attend_new",
    )(info, own_queries, received, *pieces, *states)


def spread(block):
    first = [block] + [lax.ppermute(block, "group", along(0, d)) for d in (1, 3, 2)]
    joined = jnp.concatenate(first, 0)
    return [joined] + [lax.ppermute(joined, "group", along(1, d)) for d in (1, 3, 2)]


def shards(queries, hidden_rows, kv_weight, cache_keys, cache_values, kv_blocks):
    group = lax.axis_index("group")
    x = lax.axis_index("tensor")
    core, chip = lax.rem(group, 2), group // 2
    info = jnp.stack([core, chip // SIDE, lax.rem(chip, SIDE), x]).astype(jnp.int32)
    size = hidden_rows.shape[0] // 2
    upper, lower = hidden_rows[:size], hidden_rows[size:]
    upper_right = lax.ppermute(upper, "tensor", ring(1))
    lower_left = lax.ppermute(lower, "tensor", ring(3))
    lower_right = lax.ppermute(lower, "tensor", ring(1))
    upper_left = lax.ppermute(upper, "tensor", ring(3))
    upper_far = lax.ppermute(upper_right, "tensor", ring(1))
    lower_far = lax.ppermute(lower_left, "tensor", ring(3))

    mine, give, own_queries = pack(info, cache_keys, cache_values, queries)
    received = lax.ppermute(give, "group", swap_cores())
    cache = spread(jnp.concatenate([mine, received[: 2 * ROWS]], 0))
    live_keys = cache_keys.shape[0] * kv_blocks.shape[0] // 2
    states = attend_cache(info, kv_blocks, own_queries, received, cache, live_keys)

    half = HEAD_DIM // 2
    positions = jnp.sum(kv_blocks) * BLOCK + group * ROWS + jnp.arange(ROWS, dtype=jnp.int32)
    freq = jnp.exp(jnp.arange(half, dtype=F32) * (-2.0 * math.log(500000.0) / HEAD_DIM))
    angle = positions.astype(F32)[:, None] * freq[None, :]
    cosine, sine = jnp.cos(angle), jnp.sin(angle)
    new_keys, new_values, mine, give = project(
        info,
        (hidden_rows, upper_right, lower_left, lower_right, upper_left, upper_far, lower_far),
        kv_weight,
        jnp.concatenate([cosine, cosine], 1),
        jnp.concatenate([-sine, sine], 1),
    )
    new = spread(jnp.concatenate([mine, lax.ppermute(give, "group", swap_cores())], 0))
    states = attend_new(info, own_queries, received, (0,), new[:1], states, False)
    states = attend_new(info, own_queries, received, (1, 2), new[1:3], states, False)
    here, there = attend_new(info, own_queries, received, (3,), new[3:], states, True)
    other = lax.ppermute(there, "group", swap_cores())
    attended = jnp.where(
        core == 0, jnp.concatenate([here, other], 1), jnp.concatenate([other, here], 1)
    )
    return (attended, new_keys, new_values)


def solution(mesh):
    placed = (
        P("group", "tensor"),
        P(("group", "tensor"), None),
        P(None, None, "tensor"),
        P("group", "tensor"),
        P("group", "tensor"),
        P(),
    )
    return jax.shard_map(
        shards,
        mesh=mesh,
        in_specs=placed,
        out_specs=(P("group", "tensor"), P("group", "tensor"), P("group", "tensor")),
        check_vma=False,
    )
```

time: 429 us -> 132 us (0.31)
  the two profiles are of different devices: /device:TPU:25 before, /device:TPU:121 now
where the time goes in v1:
time: 132 us
  Pallas kernels  73.7 us (56%)
  waiting for transfers between devices  26.8 us (20%)
  starting transfers between devices  18.8 us (14%)
  local copies, waits for them, and re-layouts  7.11 us (5%)
  other arithmetic  4.06 us (3%)
  between operations  1.49 us (1%)
    pallas_call x3, Pallas kernels, attend_new(): pl.pallas_call(functools.partial(new_kernel, which, last), out_shape=(out...  55.8 us
    ppermute x6, waiting for transfers between devices, spread(): lax.ppermute(block, 'group', along(0, d))  12.8 us
    pallas_call x1, Pallas kernels, attend_cache(): pl.pallas_call(functools.partial(cache_kernel, live_keys), out_shape=(STA...  11.8 us
    unnamed x18, local copies, waits for them, and re-layouts  5.96 us
    ppermute x6, waiting for transfers between devices, spread(): lax.ppermute(joined, 'group', along(1, d))  5.47 us
    ppermute x6, starting transfers between devices, spread(): lax.ppermute(block, 'group', along(0, d))  4.96 us
    pallas_call x1, Pallas kernels, project(): pl.pallas_call(project_kernel, out_shape=(wide, wide, tall, tall), in_spe...  4.01 us
    ppermute x1, waiting for transfers between devices, shards(): upper_right = lax.ppermute(upper, 'tensor', ring(1))  3.9 us
  transfers between devices with their start and end apart: 21, of which 9 were waited for; matrix products, arithmetic and copies ran while one was open for 3% of the time, Pallas kernels for 45%

profile of v1, /device:TPU:121, one launch (start us, length us, event | category | flops | bytes accessed | tf_op | source)
XLA Modules:
  0.0 131.9 jit_solution(10421601976920511882)
XLA Ops:
  0.6 0.0 copy-start.5
  0.6 1.1 fusion.1
  1.7 2.5 %collective-permute-start.2 = (bf16[16,8192]{1,0:T(8,128)(2,1)S(1)}, bf16[16,8192]{1,0:T(8,128)(2,1)S(1)}, u32[]{:S(2)}, u32[]{:S(2)}) collective-permute-start(bf16[16,8192]{1,0:T(8,128)(2,1)S(1)} %get-tuple-element.39), channel_id=1, source_target_pairs={{0,3},{1,0},{2,1},{3,2},{4,7},{5,4},{6,5},{7,6},{8,11},{9,8},{10,9... | collective-permute-start | bytes 786440 | tf_op jit(solution)/shard_map/ppermute | solution.py:304
  4.3 0.0 collective-permute-start.3
  4.3 0.6 pad_add_fusion.info
  4.8 0.0 copy-start.4
  4.8 2.1 %pack.1 = (bf16[256,128]{1,0:T(8,128)(2,1)}, bf16[1280,128]{1,0:T(8,128)(2,1)}, bf16[1024,128]{1,0:T(8,128)(2,1)}) custom-call(s32[4]{0:T(128)} %pad_add_fusion.info, bf16[128,256]{1,0:T(8,128)(2,1)} %keys.1, bf16[128,256]{1,0:T(8,128)(2,1)} %values.1, bf16[128,2048]{1,0:T(8,128)(2,1)} %queries.1), custom_call_target="tpu_custom_call" | custom-call | tf_op jit(solution)/shard_map/pack/pallas_call | solution.py:69
  7.0 1.0 collective-permute-start
  7.9 0.5 collective-permute-start.1
  8.4 1.3 reduce_sum.9
  10.4 0.8 constant_dynamic-update-slice_fusion.11
  11.2 0.0 collective-permute-done.received
  11.2 0.9 pad_maximum_fusion
  12.1 0.1 collective-permute-start.14
  12.2 1.5 %collective-permute-start.15 = (bf16[512,128]{1,0:T(8,128)(2,1)S(1)}, bf16[512,128]{1,0:T(8,128)(2,1)S(1)}, u32[]{:S(2)}, u32[]{:S(2)}) collective-permute-start(bf16[512,128]{1,0:T(8,128)(2,1)S(1)} %pad_maximum_fusion), channel_id=1, source_target_pairs={{0,24},{4,100},{8,0},{12,108},{16,8},{20,116},{24,16},{28,124},{32... | collective-permute-start | bytes 393224 | tf_op jit(solution)/shard_map/ppermute | solution.py:291
  13.6 0.3 fusion
  13.9 0.1 pad_maximum_fusion.1
  14.0 3.9 %collective-permute-done.1.refs_1_ = bf16[16,8192]{1,0:T(8,128)(2,1)S(1)} collective-permute-done((bf16[16,8192]{1,0:T(8,128)(2,1)S(1)}, bf16[16,8192]{1,0:T(8,128)(2,1)S(1)}, u32[]{:S(2)}, u32[]{:S(2)}) %collective-permute-start.1) | collective-permute-done | bytes 262176 | tf_op jit(solution)/shard_map/ppermute | solution.py:303
  17.9 0.8 collective-permute-start.4
  18.8 0.0 collective-permute-done.2.refs_2_
  18.8 0.7 collective-permute-start.5
  19.4 0.0 collective-permute-done.14
  19.4 2.0 %collective-permute-start.6 = (bf16[16,8192]{1,0:T(8,128)(2,1)S(1)}, bf16[16,8192]{1,0:T(8,128)(2,1)S(1)}, u32[]{:S(2)}, u32[]{:S(2)}) collective-permute-start(bf16[16,8192]{1,0:T(8,128)(2,1)S(1)} %collective-permute-done.2.refs_2_), channel_id=1, source_target_pairs={{0,3},{1,0},{2,1},{3,2},{4,7},{5,4},{6,5},{7,6},{8,11},{9,8},{10,9... | collective-permute-start | bytes 786440 | tf_op jit(solution)/shard_map/ppermute | solution.py:308
  21.4 0.0 collective-permute-done.15
  21.4 1.0 collective-permute-start.16
  22.4 4.3 %collective-permute-done.16 = bf16[512,128]{1,0:T(8,128)(2,1)S(1)} collective-permute-done((bf16[512,128]{1,0:T(8,128)(2,1)S(1)}, bf16[512,128]{1,0:T(8,128)(2,1)S(1)}, u32[]{:S(2)}, u32[]{:S(2)}) %collective-permute-start.16) | collective-permute-done | bytes 131104 | tf_op jit(solution)/shard_map/ppermute | solution.py:291
  26.8 0.1 collective-permute-start.17
  26.9 0.0 collective-permute-done.3.refs_3_
  26.9 0.0 collective-permute-done.4.refs_4_
  26.9 0.0 collective-permute-done.5.refs_5_
  26.9 2.6 %collective-permute-done.6.refs_6_ = bf16[16,8192]{1,0:T(8,128)(2,1)S(1)} collective-permute-done((bf16[16,8192]{1,0:T(8,128)(2,1)S(1)}, bf16[16,8192]{1,0:T(8,128)(2,1)S(1)}, u32[]{:S(2)}, u32[]{:S(2)}) %collective-permute-start.6) | collective-permute-done | bytes 262176 | tf_op jit(solution)/shard_map/ppermute | solution.py:308
  29.5 3.4 %copy-done = bf16[2,8192,256]{2,1,0:T(8,128)(2,1)S(1)} copy-done((bf16[2,8192,256]{2,1,0:T(8,128)(2,1)S(1)}, bf16[2,8192,256]{2,1,0:T(8,128)(2,1)}, u32[]{:S(2)}) %copy-start) | copy-done | bytes 8388632
  32.9 1.0 copy-done.2
  33.9 0.6 copy-done.3
  34.5 4.0 %project.1 = (bf16[128,256]{1,0:T(8,128)(2,1)}, bf16[128,256]{1,0:T(8,128)(2,1)}, bf16[256,128]{1,0:T(8,128)(2,1)S(1)}, bf16[256,128]{1,0:T(8,128)(2,1)S(1)}) custom-call(s32[4]{0:T(128)S(1)} %copy-done.3, bf16[32,8192]{1,0:T(8,128)(2,1)S(1)} %copy-done.2, bf16[16,8192]{1,0:T(8,128)(2,1)S(1)} %collective-permute-done.1.refs_1_, ...), custom_call_target="tpu_custom_call" | custom-call | tf_op jit(solution)/shard_map/project/pallas_call | solution.py:119
  38.5 2.8 %collective-permute-start.7 = (bf16[256,128]{1,0:T(8,128)(2,1)S(1)}, bf16[256,128]{1,0:T(8,128)(2,1)S(1)}, u32[]{:S(2)}, u32[]{:S(2)}) collective-permute-start(bf16[256,128]{1,0:T(8,128)(2,1)S(1)} %get-tuple-element.24), channel_id=1, source_target_pairs={{0,4},{4,0},{8,12},{12,8},{16,20},{20,16},{24,28},{28,24},{32,36},... | collective-permute-start | bytes 196616 | tf_op jit(solution)/shard_map/ppermute | solution.py:328
  41.3 0.9 collective-permute-done.7
  42.2 0.1 collective-permute-start.8
  42.3 1.5 %collective-permute-start.9 = (bf16[512,128]{1,0:T(8,128)(2,1)S(1)}, bf16[512,128]{1,0:T(8,128)(2,1)S(1)}, u32[]{:S(2)}, u32[]{:S(2)}) collective-permute-start(bf16[512,128]{1,0:T(8,128)(2,1)S(1)} %get-tuple-element.43), channel_id=1, source_target_pairs={{0,24},{4,100},{8,0},{12,108},{16,8},{20,116},{24,16},{28,124},{32... | collective-permute-start | bytes 393224 | tf_op jit(solution)/shard_map/ppermute | solution.py:291
  43.8 0.1 collective-permute-start.18
  43.9 0.2 collective-permute-start.19
  44.1 2.4 %collective-permute-done.8 = bf16[512,128]{1,0:T(8,128)(2,1)S(1)} collective-permute-done((bf16[512,128]{1,0:T(8,128)(2,1)S(1)}, bf16[512,128]{1,0:T(8,128)(2,1)S(1)}, u32[]{:S(2)}, u32[]{:S(2)}) %collective-permute-start.8) | collective-permute-done | bytes 131104 | tf_op jit(solution)/shard_map/ppermute | solution.py:291
  46.4 1.0 collective-permute-start.10
  47.4 0.3 collective-permute-done.9
  47.7 5.8 %collective-permute-done.10 = bf16[512,128]{1,0:T(8,128)(2,1)S(1)} collective-permute-done((bf16[512,128]{1,0:T(8,128)(2,1)S(1)}, bf16[512,128]{1,0:T(8,128)(2,1)S(1)}, u32[]{:S(2)}, u32[]{:S(2)}) %collective-permute-start.10) | collective-permute-done | bytes 131104 | tf_op jit(solution)/shard_map/ppermute | solution.py:291
  53.5 0.1 collective-permute-start.12
  53.6 1.4 %collective-permute-start.13 = (bf16[2048,128]{1,0:T(8,128)(2,1)S(1)}, bf16[2048,128]{1,0:T(8,128)(2,1)S(1)}, u32[]{:S(2)}, u32[]{:S(2)}) collective-permute-start(bf16[2048,128]{1,0:T(8,128)(2,1)S(1)} %constant_dynamic-update-slice_fusion.2.refs_0_), channel_id=1, source_target_pairs={{0,96},{4,28},{8,104},{12,4},{16,112},{20,12},{24,120},{28,20},{32... | collective-permute-start | bytes 1572872 | tf_op jit(solution)/shard_map/ppermute | solution.py:293
  55.1 0.0 collective-permute-done.17.refs_1_
  55.1 0.6 collective-permute-start.11
  55.7 5.5 %collective-permute-done.18.refs_2_ = bf16[2048,128]{1,0:T(8,128)(2,1)S(1)} collective-permute-done((bf16[2048,128]{1,0:T(8,128)(2,1)S(1)}, bf16[2048,128]{1,0:T(8,128)(2,1)S(1)}, u32[]{:S(2)}, u32[]{:S(2)}) %collective-permute-start.18) | collective-permute-done | bytes 524320 | tf_op jit(solution)/shard_map/ppermute | solution.py:293
  61.2 0.0 collective-permute-done.19.refs_3_
  61.2 0.0 copy-done.5
  61.2 0.0 copy-done.1
  61.2 11.8 %attend_cache.1 = (f32[2048,128]{1,0:T(8,128)S(1)}, f32[2048,128]{1,0:T(8,128)S(1)}, f32[2048,128]{1,0:T(8,128)S(1)}) custom-call(s32[4]{0:T(128)S(1)} %copy-done.3, s32[32]{0:T(128)S(1)} %copy-done.5, bf16[1024,128]{1,0:T(8,128)(2,1)S(1)} %copy-done.1, bf16[1280,128]{1,0:T(8,128)(2,1)S(1)} %collective-permute-done.received, ...), custom_call_target="tpu_custom_call" | custom-call | tf_op jit(solution)/shard_map/attend_cache/pallas_call | solution.py:194
  73.0 0.0 copy-done.4
  73.0 14.0 %attend_new.2 = (f32[2048,128]{1,0:T(8,128)S(1)}, f32[2048,128]{1,0:T(8,128)S(1)}, f32[2048,128]{1,0:T(8,128)S(1)}) custom-call(s32[4]{0:T(128)S(1)} %copy-done.4, bf16[1024,128]{1,0:T(8,128)(2,1)S(1)} %copy-done.1, bf16[1280,128]{1,0:T(8,128)(2,1)S(1)} %collective-permute-done.received, bf16[2048,128]{1,0:T(8,128)(2,1)S(1)} %constant_dynamic-update-slice_fusion.2.refs_0_, ...), custom_call_target="tpu_custom_call" | custom-call | tf_op jit(solution)/shard_map/attend_new/pallas_call | solution.py:279
  87.0 0.0 collective-permute-done.12.refs_0_
  87.0 0.0 collective-permute-done.13.refs_1_
  87.0 27.6 %attend_new.3 = (f32[2048,128]{1,0:T(8,128)S(1)}, f32[2048,128]{1,0:T(8,128)S(1)}, f32[2048,128]{1,0:T(8,128)S(1)}) custom-call(s32[4]{0:T(128)S(1)} %copy-done.4, bf16[1024,128]{1,0:T(8,128)(2,1)S(1)} %copy-done.1, bf16[1280,128]{1,0:T(8,128)(2,1)S(1)} %collective-permute-done.received, bf16[2048,128]{1,0:T(8,128)(2,1)S(1)} %collective-permute-done.12.refs_0_, ...), custom_call_target="tpu_custom_call" | custom-call | tf_op jit(solution)/shard_map/attend_new/pallas_call | solution.py:279
  114.6 0.0 collective-permute-done.11.refs_0_
  114.6 14.2 %attend_new_last.1 = (bf16[128,1024]{1,0:T(8,128)(2,1)S(1)}, bf16[128,1024]{1,0:T(8,128)(2,1)S(1)}) custom-call(s32[4]{0:T(128)S(1)} %copy-done.4, bf16[1024,128]{1,0:T(8,128)(2,1)S(1)} %copy-done.1, bf16[1280,128]{1,0:T(8,128)(2,1)S(1)} %collective-permute-done.received, bf16[2048,128]{1,0:T(8,128)(2,1)S(1)} %collective-permute-done.11.refs_0_, ...), custom_call_target="tpu_custom_call" | custom-call | tf_op jit(solution)/shard_map/attend_new_last/pallas_call | solution.py:279
  128.8 1.0 collective-permute-start.20
  129.9 1.2 collective-permute-done.20
  131.0 0.9 maximum_select_fusion
  (15 shorter events, 0.2 us)
Async XLA Ops:
  0.6 60.5 %copy-start.5 = (s32[32]{0:T(128)S(1)}, s32[32]{0:T(128)}, u32[]{:S(2)}) copy-start(s32[32]{0:T(128)} %kv_blocks.1) | copy-start | bytes 388
  1.7 17.0 %collective-permute-start.2 = (bf16[16,8192]{1,0:T(8,128)(2,1)S(1)}, bf16[16,8192]{1,0:T(8,128)(2,1)S(1)}, u32[]{:S(2)}, u32[]{:S(2)}) collective-permute-start(bf16[16,8192]{1,0:T(8,128)(2,1)S(1)} %get-tuple-element.39), channel_id=1, source_target_pairs={{0,3},{1,0},{2,1},{3,2},{4,7},{5,4},{6,5},{7,6},{8,11},{9,8},{10,9... | collective-permute-start | bytes 786440 | tf_op jit(solution)/shard_map/ppermute | solution.py:304
  4.3 22.6 %collective-permute-start.3 = (bf16[16,8192]{1,0:T(8,128)(2,1)S(1)}, bf16[16,8192]{1,0:T(8,128)(2,1)S(1)}, u32[]{:S(2)}, u32[]{:S(2)}) collective-permute-start(bf16[16,8192]{1,0:T(8,128)(2,1)S(1)} %get-tuple-element.39), channel_id=1, source_target_pairs={{0,1},{1,2},{2,3},{3,0},{4,5},{5,6},{6,7},{7,4},{8,9},{9,10},{10,1... | collective-permute-start | bytes 786440 | tf_op jit(solution)/shard_map/ppermute | solution.py:305
  4.8 68.2 %copy-start.4 = (s32[4]{0:T(128)S(1)}, s32[4]{0:T(128)}, u32[]{:S(2)}) copy-start(s32[4]{0:T(128)} %pad_add_fusion.info) | copy-start | bytes 52
  7.0 54.2 %copy-start.1 = (bf16[1024,128]{1,0:T(8,128)(2,1)S(1)}, bf16[1024,128]{1,0:T(8,128)(2,1)}, u32[]{:S(2)}) copy-start(bf16[1024,128]{1,0:T(8,128)(2,1)} %get-tuple-element.21.own_queries) | copy-start | bytes 786436
  7.0 4.3 %collective-permute-start = (bf16[1280,128]{1,0:T(8,128)(2,1)}, bf16[1280,128]{1,0:T(8,128)(2,1)S(1)}, u32[]{:S(2)}, u32[]{:S(2)}) collective-permute-start(bf16[1280,128]{1,0:T(8,128)(2,1)} %get-tuple-element.22), channel_id=1, source_target_pairs={{0,4},{4,0},{8,12},{12,8},{16,20},{20,16},{24,28},{28,24},{32,36},... | collective-permute-start | bytes 983048 | tf_op jit(solution)/shard_map/ppermute | solution.py:311
  7.9 10.0 %collective-permute-start.1 = (bf16[16,8192]{1,0:T(8,128)(2,1)S(1)}, bf16[16,8192]{1,0:T(8,128)(2,1)S(1)}, u32[]{:S(2)}, u32[]{:S(2)}) collective-permute-start(bf16[16,8192]{1,0:T(8,128)(2,1)S(1)} %get-tuple-element.40), channel_id=1, source_target_pairs={{0,1},{1,2},{2,3},{3,0},{4,5},{5,6},{6,7},{7,4},{8,9},{9,10},{10,1... | collective-permute-start | bytes 786440 | tf_op jit(solution)/shard_map/ppermute | solution.py:303
  12.1 7.3 %collective-permute-start.14 = (bf16[512,128]{1,0:T(8,128)(2,1)S(1)}, bf16[512,128]{1,0:T(8,128)(2,1)S(1)}, u32[]{:S(2)}, u32[]{:S(2)}) collective-permute-start(bf16[512,128]{1,0:T(8,128)(2,1)S(1)} %pad_maximum_fusion), channel_id=1, source_target_pairs={{0,8},{4,36},{8,16},{12,44},{16,24},{20,52},{24,0},{28,60},{32,40}... | collective-permute-start | bytes 393224 | tf_op jit(solution)/shard_map/ppermute | solution.py:291
  12.2 9.3 %collective-permute-start.15 = (bf16[512,128]{1,0:T(8,128)(2,1)S(1)}, bf16[512,128]{1,0:T(8,128)(2,1)S(1)}, u32[]{:S(2)}, u32[]{:S(2)}) collective-permute-start(bf16[512,128]{1,0:T(8,128)(2,1)S(1)} %pad_maximum_fusion), channel_id=1, source_target_pairs={{0,24},{4,100},{8,0},{12,108},{16,8},{20,116},{24,16},{28,124},{32... | collective-permute-start | bytes 393224 | tf_op jit(solution)/shard_map/ppermute | solution.py:291
  17.9 8.9 %collective-permute-start.4 = (bf16[16,8192]{1,0:T(8,128)(2,1)S(1)}, bf16[16,8192]{1,0:T(8,128)(2,1)S(1)}, u32[]{:S(2)}, u32[]{:S(2)}) collective-permute-start(bf16[16,8192]{1,0:T(8,128)(2,1)S(1)} %get-tuple-element.40), channel_id=1, source_target_pairs={{0,3},{1,0},{2,1},{3,2},{4,7},{5,4},{6,5},{7,6},{8,11},{9,8},{10,9... | collective-permute-start | bytes 786440 | tf_op jit(solution)/shard_map/ppermute | solution.py:306
  18.8 8.1 %collective-permute-start.5 = (bf16[16,8192]{1,0:T(8,128)(2,1)S(1)}, bf16[16,8192]{1,0:T(8,128)(2,1)S(1)}, u32[]{:S(2)}, u32[]{:S(2)}) collective-permute-start(bf16[16,8192]{1,0:T(8,128)(2,1)S(1)} %collective-permute-done.1.refs_1_), channel_id=1, source_target_pairs={{0,1},{1,2},{2,3},{3,0},{4,5},{5,6},{6,7},{7,4},{8,9},{9,10},{10,1... | collective-permute-start | bytes 786440 | tf_op jit(solution)/shard_map/ppermute | solution.py:307
  19.4 10.1 %collective-permute-start.6 = (bf16[16,8192]{1,0:T(8,128)(2,1)S(1)}, bf16[16,8192]{1,0:T(8,128)(2,1)S(1)}, u32[]{:S(2)}, u32[]{:S(2)}) collective-permute-start(bf16[16,8192]{1,0:T(8,128)(2,1)S(1)} %collective-permute-done.2.refs_2_), channel_id=1, source_target_pairs={{0,3},{1,0},{2,1},{3,2},{4,7},{5,4},{6,5},{7,6},{8,11},{9,8},{10,9... | collective-permute-start | bytes 786440 | tf_op jit(solution)/shard_map/ppermute | solution.py:308
  21.4 5.3 %collective-permute-start.16 = (bf16[512,128]{1,0:T(8,128)(2,1)S(1)}, bf16[512,128]{1,0:T(8,128)(2,1)S(1)}, u32[]{:S(2)}, u32[]{:S(2)}) collective-permute-start(bf16[512,128]{1,0:T(8,128)(2,1)S(1)} %pad_maximum_fusion), channel_id=1, source_target_pairs={{0,16},{4,68},{8,24},{12,76},{16,0},{20,84},{24,8},{28,92},{32,48}... | collective-permute-start | bytes 393224 | tf_op jit(solution)/shard_map/ppermute | solution.py:291
  26.8 28.3 %collective-permute-start.17 = (bf16[2048,128]{1,0:T(8,128)(2,1)S(1)}, bf16[2048,128]{1,0:T(8,128)(2,1)S(1)}, u32[]{:S(2)}, u32[]{:S(2)}) collective-permute-start(bf16[2048,128]{1,0:T(8,128)(2,1)S(1)} %constant_dynamic-update-slice_fusion.7.refs_0_), channel_id=1, source_target_pairs={{0,32},{4,12},{8,40},{12,20},{16,48},{20,28},{24,56},{28,4},{32,64... | collective-permute-start | bytes 1572872 | tf_op jit(solution)/shard_map/ppermute | solution.py:293
  29.5 3.4 %copy-start = (bf16[2,8192,256]{2,1,0:T(8,128)(2,1)S(1)}, bf16[2,8192,256]{2,1,0:T(8,128)(2,1)}, u32[]{:S(2)}) copy-start(bf16[2,8192,256]{2,1,0:T(8,128)(2,1)} %refs_7_.1) | copy-start | bytes 25165828
  32.9 1.0 copy-start.2
  33.9 0.6 copy-start.3
  38.5 3.7 %collective-permute-start.7 = (bf16[256,128]{1,0:T(8,128)(2,1)S(1)}, bf16[256,128]{1,0:T(8,128)(2,1)S(1)}, u32[]{:S(2)}, u32[]{:S(2)}) collective-permute-start(bf16[256,128]{1,0:T(8,128)(2,1)S(1)} %get-tuple-element.24), channel_id=1, source_target_pairs={{0,4},{4,0},{8,12},{12,8},{16,20},{20,16},{24,28},{28,24},{32,36},... | collective-permute-start | bytes 196616 | tf_op jit(solution)/shard_map/ppermute | solution.py:328
  42.2 4.2 %collective-permute-start.8 = (bf16[512,128]{1,0:T(8,128)(2,1)S(1)}, bf16[512,128]{1,0:T(8,128)(2,1)S(1)}, u32[]{:S(2)}, u32[]{:S(2)}) collective-permute-start(bf16[512,128]{1,0:T(8,128)(2,1)S(1)} %get-tuple-element.43), channel_id=1, source_target_pairs={{0,8},{4,36},{8,16},{12,44},{16,24},{20,52},{24,0},{28,60},{32,40}... | collective-permute-start | bytes 393224 | tf_op jit(solution)/shard_map/ppermute | solution.py:291
  42.3 5.4 %collective-permute-start.9 = (bf16[512,128]{1,0:T(8,128)(2,1)S(1)}, bf16[512,128]{1,0:T(8,128)(2,1)S(1)}, u32[]{:S(2)}, u32[]{:S(2)}) collective-permute-start(bf16[512,128]{1,0:T(8,128)(2,1)S(1)} %get-tuple-element.43), channel_id=1, source_target_pairs={{0,24},{4,100},{8,0},{12,108},{16,8},{20,116},{24,16},{28,124},{32... | collective-permute-start | bytes 393224 | tf_op jit(solution)/shard_map/ppermute | solution.py:291
  43.8 17.4 %collective-permute-start.18 = (bf16[2048,128]{1,0:T(8,128)(2,1)S(1)}, bf16[2048,128]{1,0:T(8,128)(2,1)S(1)}, u32[]{:S(2)}, u32[]{:S(2)}) collective-permute-start(bf16[2048,128]{1,0:T(8,128)(2,1)S(1)} %constant_dynamic-update-slice_fusion.7.refs_0_), channel_id=1, source_target_pairs={{0,96},{4,28},{8,104},{12,4},{16,112},{20,12},{24,120},{28,20},{32... | collective-permute-start | bytes 1572872 | tf_op jit(solution)/shard_map/ppermute | solution.py:293
  43.9 17.3 %collective-permute-start.19 = (bf16[2048,128]{1,0:T(8,128)(2,1)S(1)}, bf16[2048,128]{1,0:T(8,128)(2,1)S(1)}, u32[]{:S(2)}, u32[]{:S(2)}) collective-permute-start(bf16[2048,128]{1,0:T(8,128)(2,1)S(1)} %constant_dynamic-update-slice_fusion.7.refs_0_), channel_id=1, source_target_pairs={{0,64},{4,20},{8,72},{12,28},{16,80},{20,4},{24,88},{28,12},{32,96... | collective-permute-start | bytes 1572872 | tf_op jit(solution)/shard_map/ppermute | solution.py:293
  46.4 7.1 %collective-permute-start.10 = (bf16[512,128]{1,0:T(8,128)(2,1)S(1)}, bf16[512,128]{1,0:T(8,128)(2,1)S(1)}, u32[]{:S(2)}, u32[]{:S(2)}) collective-permute-start(bf16[512,128]{1,0:T(8,128)(2,1)S(1)} %get-tuple-element.43), channel_id=1, source_target_pairs={{0,16},{4,68},{8,24},{12,76},{16,0},{20,84},{24,8},{28,92},{32,48}... | collective-permute-start | bytes 393224 | tf_op jit(solution)/shard_map/ppermute | solution.py:291
  53.5 33.5 %collective-permute-start.12 = (bf16[2048,128]{1,0:T(8,128)(2,1)S(1)}, bf16[2048,128]{1,0:T(8,128)(2,1)S(1)}, u32[]{:S(2)}, u32[]{:S(2)}) collective-permute-start(bf16[2048,128]{1,0:T(8,128)(2,1)S(1)} %constant_dynamic-update-slice_fusion.2.refs_0_), channel_id=1, source_target_pairs={{0,32},{4,12},{8,40},{12,20},{16,48},{20,28},{24,56},{28,4},{32,64... | collective-permute-start | bytes 1572872 | tf_op jit(solution)/shard_map/ppermute | solution.py:293
  53.6 33.4 %collective-permute-start.13 = (bf16[2048,128]{1,0:T(8,128)(2,1)S(1)}, bf16[2048,128]{1,0:T(8,128)(2,1)S(1)}, u32[]{:S(2)}, u32[]{:S(2)}) collective-permute-start(bf16[2048,128]{1,0:T(8,128)(2,1)S(1)} %constant_dynamic-update-slice_fusion.2.refs_0_), channel_id=1, source_target_pairs={{0,96},{4,28},{8,104},{12,4},{16,112},{20,12},{24,120},{28,20},{32... | collective-permute-start | bytes 1572872 | tf_op jit(solution)/shard_map/ppermute | solution.py:293
  55.1 59.5 %collective-permute-start.11 = (bf16[2048,128]{1,0:T(8,128)(2,1)S(1)}, bf16[2048,128]{1,0:T(8,128)(2,1)S(1)}, u32[]{:S(2)}, u32[]{:S(2)}) collective-permute-start(bf16[2048,128]{1,0:T(8,128)(2,1)S(1)} %constant_dynamic-update-slice_fusion.2.refs_0_), channel_id=1, source_target_pairs={{0,64},{4,20},{8,72},{12,28},{16,80},{20,4},{24,88},{28,12},{32,96... | collective-permute-start | bytes 1572872 | tf_op jit(solution)/shard_map/ppermute | solution.py:293
  128.8 2.2 %collective-permute-start.20 = (bf16[128,1024]{1,0:T(8,128)(2,1)S(1)}, bf16[128,1024]{1,0:T(8,128)(2,1)S(1)}, u32[]{:S(2)}, u32[]{:S(2)}) collective-permute-start(bf16[128,1024]{1,0:T(8,128)(2,1)S(1)} %get-tuple-element.36), channel_id=1, source_target_pairs={{0,4},{4,0},{8,12},{12,8},{16,20},{20,16},{24,28},{28,24},{32,36},... | collective-permute-start | bytes 786440 | tf_op jit(solution)/shard_map/ppermute | solution.py:332

commit v2 on v0

v2 whole, which is shorter than its diff:
```python
import functools
import math

import jax
import jax.numpy as jnp
from jax import lax
from jax.experimental import pallas as pl
from jax.experimental.pallas import tpu as pltpu
from jax.sharding import PartitionSpec as P

HEAD_DIM = 128
BLOCK = 32
ROWS = 128
SHARE = 8
SIDE = 4
EXPONENT = math.log2(math.e) / math.sqrt(HEAD_DIM)
ARRIVAL = (0, 1, 3, 2)
BACK = (0, 1, 3, 2)
VMEM = pl.BlockSpec(memory_space=pltpu.VMEM)
SMEM = pl.BlockSpec(memory_space=pltpu.SMEM)
F32 = jnp.float32
BF16 = jnp.bfloat16


def swap_cores():
    return [(i, i ^ 1) for i in range(2 * SIDE * SIDE)]


def along(phase, distance):
    pairs = []
    for y in range(SIDE):
        for z in range(SIDE):
            for core in range(2):
                if (core + phase) % 2 == 0:
                    to = (y, (z + distance) % SIDE)
                else:
                    to = ((y + distance) % SIDE, z)
                pairs.append(((y * SIDE + z) * 2 + core, (to[0] * SIDE + to[1]) * 2 + core))
    return pairs


def ring(distance):
    pairs = []
    for group in range(2 * SIDE * SIDE):
        for x in range(SIDE):
            to = (x + (distance if group % 2 == 0 else -distance)) % SIDE
            pairs.append((group * SIDE + x, group * SIDE + to))
    return pairs


def place():
    group = lax.axis_index("group")
    return lax.rem(group, 2), group // (2 * SIDE), lax.rem(group // 2, SIDE)


def sender(piece, slot):
    core, y, z = place()
    first, second = BACK[slot], BACK[piece]
    dy = jnp.where(core == 0, second, first)
    dz = jnp.where(core == 0, first, second)
    return lax.rem(y - dy + SIDE, SIDE) * SIDE + lax.rem(z - dz + SIDE, SIDE)


def cost(microseconds):
    return pl.CostEstimate(
        flops=int(microseconds * 1.1e9), bytes_accessed=int(microseconds * 3.5e6), transcendentals=0
    )


def heads_kernel(width, *refs):
    core, _, _ = place()
    arrays, (mine, give) = refs[:-2], refs[-2:]
    for which, target in ((core, mine), (1 - core, give)):
        at = 0
        for array in arrays:
            for i in range(0, width, HEAD_DIM):
                columns = pl.ds(pl.multiple_of(which * width + i, HEAD_DIM), HEAD_DIM)
                target[at : at + ROWS, :] = array[:, columns]
                at += ROWS


def heads(width, *arrays):
    rows = len(arrays) * width // HEAD_DIM * ROWS
    tall = jax.ShapeDtypeStruct((rows, HEAD_DIM), BF16)
    return pl.pallas_call(
        functools.partial(heads_kernel, width),
        out_shape=(tall, tall),
        in_specs=[VMEM] * len(arrays),
        out_specs=(VMEM,) * 2,
        compiler_params=pltpu.CompilerParams(vmem_limit_bytes=8 << 20),
        cost_estimate=cost(0.1),
        name="heads",
    )(*arrays)


def sent_from(step):
    core, _, _ = place()
    x = lax.axis_index("tensor")
    return lax.rem(jnp.where(core == 0, x - step, x + step) + SIDE, SIDE)


def near_kernel(*refs):
    pieces, weight, keys_out, values_out, held, rows, sems = refs[:3], *refs[3:]
    chunks = sems.shape[0]
    step = held.shape[1] // chunks

    def fetch(i):
        part = pl.ds(i * step, step)
        return pltpu.make_async_copy(weight.at[:, part, :], held.at[:, part, :], sems.at[i])

    for i in range(chunks):
        fetch(i).start()
    size = pieces[0].shape[0]
    for i, piece in enumerate(pieces):
        rows[i * size : (i + 1) * size, :] = piece[...]
    keys = jnp.zeros(keys_out.shape, F32)
    values = jnp.zeros(keys_out.shape, F32)
    for i in range(chunks):
        fetch(i).wait()
        part = slice(i * step, (i + 1) * step)
        keys += jnp.dot(rows[:, part], held[0, part, :], preferred_element_type=F32)
        values += jnp.dot(rows[:, part], held[1, part, :], preferred_element_type=F32)
    keys_out[...] = keys
    values_out[...] = values


def project_near(pieces, weight):
    count = sum(piece.shape[0] for piece in pieces)
    wide = jax.ShapeDtypeStruct((count, weight.shape[2]), F32)
    return pl.pallas_call(
        near_kernel,
        out_shape=(wide, wide, jax.ShapeDtypeStruct(weight.shape, BF16)),
        in_specs=[VMEM] * 3 + [pl.BlockSpec(memory_space=pltpu.HBM)],
        out_specs=(VMEM,) * 3,
        scratch_shapes=[
            pltpu.VMEM((count, weight.shape[1]), BF16),
            pltpu.SemaphoreType.DMA((8,)),
        ],
        compiler_params=pltpu.CompilerParams(vmem_limit_bytes=32 << 20),
        cost_estimate=cost(0.1),
        name="project_near",
    )(*pieces, weight)


def far_kernel(piece, near_keys, near_values, weight, cosine, sine, *refs):
    new_keys, new_values, mine, give = refs
    size = piece.shape[0]
    keys = jnp.zeros((size, weight.shape[2]), F32)
    values = jnp.zeros((size, weight.shape[2]), F32)
    step = 1024
    for i in range(0, piece.shape[1], step):
        part = slice(i, i + step)
        keys += jnp.dot(piece[:, part], weight[0, part, :], preferred_element_type=F32)
        values += jnp.dot(piece[:, part], weight[1, part, :], preferred_element_type=F32)
    for i, back in enumerate(ARRIVAL):
        at = pl.ds(pl.multiple_of(sent_from(back) * size, size), size)
        part = slice(i * size, (i + 1) * size)
        last = i == len(ARRIVAL) - 1
        for h in range(2):
            head = slice(h * HEAD_DIM, (h + 1) * HEAD_DIM)
            key = keys[:, head] if last else near_keys[part, head]
            turned = key * cosine[at, :] + pltpu.roll(key, HEAD_DIM // 2, 1) * sine[at, :]
            new_keys[at, head] = turned.astype(BF16)
        value = values if last else near_values[part, :]
        new_values[at, :] = value.astype(BF16)
    core, _, _ = place()
    for which, target in ((core, mine), (1 - core, give)):
        head = pl.ds(pl.multiple_of(which * HEAD_DIM, HEAD_DIM), HEAD_DIM)
        target[0:ROWS, :] = new_keys[:, head]
        target[ROWS : 2 * ROWS, :] = new_values[:, head]


def project_far(piece, near_keys, near_values, weight, cosine, sine):
    wide = jax.ShapeDtypeStruct((ROWS, 2 * HEAD_DIM), BF16)
    tall = jax.ShapeDtypeStruct((2 * ROWS, HEAD_DIM), BF16)
    return pl.pallas_call(
        far_kernel,
        out_shape=(wide, wide, tall, tall),
        in_specs=[VMEM] * 6,
        out_specs=(VMEM,) * 4,
        compiler_params=pltpu.CompilerParams(vmem_limit_bytes=24 << 20),
        cost_estimate=cost(0.1),
        name="project_far",
    )(piece, near_keys, near_values, weight, cosine, sine)


def absorb(query, turned_keys, values, state, visible=None):
    top, den, num = state
    scores = jnp.dot(query, turned_keys, preferred_element_type=F32)
    if visible is not None:
        scores = jnp.where(visible, scores, -1e30)
    raised = jnp.maximum(top, jnp.max(scores, axis=1, keepdims=True))
    weights = [
        jnp.exp2((scores[:, i : i + HEAD_DIM] - raised) * EXPONENT)
        for i in range(0, scores.shape[1], HEAD_DIM)
    ]
    keep = jnp.exp2((top - raised) * EXPONENT)
    den = den * keep + functools.reduce(lambda a, b: a + b, weights)
    rounded = jnp.concatenate([w.astype(BF16) for w in weights], 1)
    num = num * keep + jnp.dot(rounded, values, preferred_element_type=F32)
    return raised, den, num


TILE = 512


def tiles(own_queries, received):
    found = []
    for i in range(0, SHARE * ROWS, TILE):
        found.append((0, i, functools.partial(own_queries.__getitem__, slice(i, i + TILE))))
    for i in range(0, SHARE * ROWS, TILE):
        there = slice(i, i + TILE)
        found.append((1, SHARE * ROWS + i, functools.partial(received.__getitem__, there)))
    return found


STATE = jax.ShapeDtypeStruct((2 * SHARE * ROWS, HEAD_DIM), F32)


def cache_kernel(live_keys, kv_blocks, own_queries, received, *refs):
    pieces, states, (keys, values, turned) = refs[:4], refs[4:7], refs[7:]
    core, _, _ = place()
    at = jnp.int32(0)
    for piece in range(SIDE):
        for slot in range(SIDE):
            chip = sender(piece, slot)
            for half in range(2):
                group = chip * 2 + (core if half == 0 else 1 - core)
                row = slot * 4 * ROWS + half * 2 * ROWS
                there = pl.ds(pl.multiple_of(at, BLOCK), ROWS)
                keys[there, :] = pieces[piece][row : row + ROWS, :]
                values[there, :] = pieces[piece][row + ROWS : row + 2 * ROWS, :]
                at = at + kv_blocks[group] * BLOCK
    for i in range(0, live_keys, 256):
        turned[:, i : i + 256] = keys[i : i + 256, :].T
    for _, start, query in tiles(own_queries, received):
        zero = jnp.zeros((TILE, HEAD_DIM), F32)
        state = (jnp.full((TILE, HEAD_DIM), -1e30, F32), zero, zero)
        state = absorb(query(), turned[...], values[:live_keys, :], state)
        for ref, value in zip(states, state):
            ref[start : start + TILE, :] = value


def attend_cache(kv_blocks, own_queries, received, pieces, live_keys):
    held = pltpu.VMEM((live_keys + ROWS, HEAD_DIM), BF16)
    return pl.pallas_call(
        functools.partial(cache_kernel, live_keys),
        out_shape=(STATE,) * 3,
        in_specs=[SMEM] + [VMEM] * 6,
        out_specs=(VMEM,) * 3,
        scratch_shapes=[held, held, pltpu.VMEM((HEAD_DIM, live_keys), BF16)],
        compiler_params=pltpu.CompilerParams(vmem_limit_bytes=24 << 20),
        cost_estimate=cost(0.1),
        name="attend_cache",
    )(kv_blocks, own_queries, received, *pieces)


def new_kernel(which, last, own_queries, received, *refs):
    count = len(which)
    pieces, olds = refs[:count], refs[count : count + 3]
    outs, (turned, held), sums = refs[count + 3 :], refs[-5:-3], refs[-3:]
    core, y, z = place()
    size = 2 * ROWS
    if not last:
        sums = outs[:3]
    parts = tiles(own_queries, received)

    def visit(keys, values, sources, visible=None):
        for partner, start, query in parts:
            rows = slice(start, start + TILE)
            state = absorb(
                query(),
                keys,
                values,
                tuple(s[rows, :] for s in sources),
                visible(partner) if visible else None,
            )
            for s, value in zip(sums, state):
                s[rows, :] = value

    def block_of(ref, slot):
        base = slot * 4 * ROWS
        here = [slice(base + i * ROWS, base + (i + 1) * ROWS) for i in range(4)]
        keys = jnp.concatenate([ref[here[0], :], ref[here[2], :]], 0)
        return keys.T, jnp.concatenate([ref[here[1], :], ref[here[3], :]], 0)

    def causal(partner):
        shape = (TILE, size)
        row = lax.rem(lax.broadcasted_iota(jnp.int32, shape, 0), ROWS)
        row = row + jnp.where(core == partner, 0, ROWS)
        key = lax.broadcasted_iota(jnp.int32, shape, 1)
        key = jnp.where(core == 0, key, lax.rem(key + ROWS, size))
        return key <= row

    found = jnp.int32(0)
    for piece, ref in zip(which, pieces):
        for slot in range(SIDE):
            if piece == 0 and slot == 0:
                continue
            seen = sender(piece, slot) < y * SIDE + z

            def keep(ref=ref, slot=slot, found=found):
                there = pl.ds(pl.multiple_of(found * size, size), size)
                turned[:, there], held[there, :] = block_of(ref, slot)

            pl.when(seen)(keep)
            found = found + seen.astype(jnp.int32)

    def one(i, sources):
        there = pl.ds(pl.multiple_of(i * size, size), size)
        visit(turned[:, there], held[there, :], sources)

    def rest(first):
        def body(i, _):
            one(i, sums)
            return 0

        lax.fori_loop(first, found, body, 0)

    if which[0] == 0:
        visit(*block_of(pieces[0], 0), olds, causal)
        rest(0)
    else:

        @pl.when(found == 0)
        def _():
            for new, old in zip(sums, olds):
                new[...] = old[...]

        @pl.when(found > 0)
        def _():
            one(0, olds)
            rest(1)

    if last:
        here, there = outs[:2]
        for partner, target in ((0, here), (1, there)):
            for head in range(SHARE):
                start = (partner * SHARE + head) * ROWS
                rows = slice(start, start + ROWS)
                den = jnp.sum(sums[1][rows, :], axis=1, keepdims=True)
                columns = slice(head * HEAD_DIM, (head + 1) * HEAD_DIM)
                target[:, columns] = (sums[2][rows, :] / den).astype(BF16)


def attend_new(own_queries, received, which, pieces, states, last):
    out = jax.ShapeDtypeStruct((ROWS, SHARE * HEAD_DIM), BF16)
    blocks = SIDE * len(which)
    total = pltpu.VMEM(STATE.shape if last else (8, HEAD_DIM), F32)
    return pl.pallas_call(
        functools.partial(new_kernel, which, last),
        out_shape=(out, out) if last else (STATE,) * 3,
        in_specs=[VMEM] * (2 + len(which) + 3),
        out_specs=(VMEM,) * (2 if last else 3),
        scratch_shapes=[
            pltpu.VMEM((HEAD_DIM, 2 * ROWS * blocks), BF16),
            pltpu.VMEM((2 * ROWS * blocks, HEAD_DIM), BF16),
            total,
            total,
            total,
        ],
        compiler_params=pltpu.CompilerParams(vmem_limit_bytes=24 << 20),
        cost_estimate=cost(0.1),
        name="attend_new_last" if last else "attend_new",
    )(own_queries, received, *pieces, *states)


def after(value, *others):
    return lax.optimization_barrier((value, *others))[0]


def first_phase(block):
    return jnp.concatenate(
        [block] + [lax.ppermute(block, "group", along(0, d)) for d in (1, 3, 2)], 0
    )


def second_phase(joined):
    return [joined] + [lax.ppermute(joined, "group", along(1, d)) for d in (1, 3, 2)]


def swapped(block):
    return lax.ppermute(block, "group", swap_cores())


def shards(queries, hidden_rows, kv_weight, cache_keys, cache_values, kv_blocks):
    group = lax.axis_index("group")
    core = lax.rem(group, 2)
    both = ("group", "tensor")
    ahead = lax.ppermute(hidden_rows, both, ring(1))
    mine, give = heads(HEAD_DIM, cache_keys, cache_values)
    behind = lax.ppermute(after(hidden_rows, mine), both, ring(3))
    far = lax.ppermute(ahead, both, ring(1))
    cache = second_phase(first_phase(jnp.concatenate([mine, swapped(give)], 0)))

    live_keys = cache_keys.shape[0] * kv_blocks.shape[0] // 2
    half = HEAD_DIM // 2
    positions = live_keys + group * ROWS + jnp.arange(ROWS, dtype=jnp.int32)
    freq = jnp.exp(jnp.arange(half, dtype=F32) * (-2.0 * math.log(500000.0) / HEAD_DIM))
    angle = positions.astype(F32)[:, None] * freq[None, :]
    cosine, sine = jnp.cos(angle), jnp.sin(angle)
    near_keys, near_values, weight = project_near((hidden_rows, ahead, behind), kv_weight)
    own_queries, give_queries = heads(SHARE * HEAD_DIM, after(queries, near_keys))
    received = swapped(give_queries)
    new_keys, new_values, mine, give = project_far(
        after(far, received),
        near_keys,
        near_values,
        weight,
        jnp.concatenate([cosine, cosine], 1),
        jnp.concatenate([-sine, sine], 1),
    )
    joined = first_phase(jnp.concatenate([mine, swapped(give)], 0))
    new = second_phase(joined)
    states = attend_cache(kv_blocks, after(own_queries, joined), received, cache, live_keys)
    states = attend_new(own_queries, received, (0,), new[:1], states, False)
    states = attend_new(own_queries, received, (1, 2), new[1:3], states, False)
    here, there = attend_new(own_queries, received, (3,), new[3:], states, True)
    other = swapped(there)
    attended = jnp.where(
        core == 0, jnp.concatenate([here, other], 1), jnp.concatenate([other, here], 1)
    )
    return (attended, new_keys, new_values)


def solution(mesh):
    placed = (
        P("group", "tensor"),
        P(("group", "tensor"), None),
        P(None, None, "tensor"),
        P("group", "tensor"),
        P("group", "tensor"),
        P(),
    )
    return jax.shard_map(
        shards,
        mesh=mesh,
        in_specs=placed,
        out_specs=(P("group", "tensor"), P("group", "tensor"), P("group", "tensor")),
        check_vma=False,
    )
```

time: 429 us -> 82.2 us (0.19); the launches traced: 423 us -> 81 us
  waiting for transfers between devices: 124 us -> 17.8 us
  local copies, waits for them, and re-layouts: 91.4 us -> 6.29 us
  matrix products: 84.3 us -> 0 us
  other arithmetic: 63 us -> 1.34 us
  loops' own time: 45.9 us -> 0 us
  starting transfers between devices: 0.12 us -> 30 us
  Pallas kernels: 0 us -> 24.7 us
  between operations: 14.6 us -> 0.82 us
    all_gather x3 -> x0, waiting for transfers between devices: 123 us -> none  [the longest x1 45.7 us: shards(): values_all = lax.all_gather(joined_values, 'group', axis=0, tiled=True)]
    dot_general x129 -> x0, matrix products: 84.3 us -> none  [the longest x64 53.3 us: block_terms(): jnp.einsum('ksrl,lkd->ksrd', weights.astype(jnp.bfloat16), values3, prefe...]
    reduce_sum x97 -> x0, other arithmetic: 57.2 us -> none  [the longest x32 42.9 us: cache_block(): live_rows = jnp.sum(jnp.where(group_ids == source, kv_blocks, 0)) * BLOCK]
    slice x66 -> x0, local copies, waits for them, and re-layouts: 57 us -> none  [the longest x32 28.5 us: visit(): value_item[prefix_cap:]]
    another operation x1 -> x0, loops' own time: 45.9 us -> none  [shards(): lax.scan(visit, carry, (keys_all.reshape(count, span, local_kv), values_a...]
    ppermute x0 -> x19, starting transfers between devices: none -> 30 us  [the longest x4 12.7 us: swapped(): return lax.ppermute(block, 'group', swap_cores())]
    pallas_call x0 -> x8, Pallas kernels: none -> 24.7 us  [the longest x3 13.5 us: attend_new(): pl.pallas_call(functools.partial(new_kernel, which, last), out_shape=(out...]
    dynamic_slice x32 -> x0, local copies, waits for them, and re-layouts: 18.8 us -> none  [shards(): lax.scan(visit, carry, (keys_all.reshape(count, span, local_kv), values_a...]
  transfers between devices with their start and end apart: 3 -> 19, of which waited for: 3 -> 8; matrix products, arithmetic and copies ran while one was open for 2% -> 1% of each run, Pallas kernels for 0% -> 26%
where the time goes in v2:
time: 82.2 us; the launch traced here: 81 us
  starting transfers between devices  30 us (36%)
  Pallas kernels  24.7 us (30%)
  waiting for transfers between devices  17.8 us (22%)
  local copies, waits for them, and re-layouts  6.29 us (8%)
  other arithmetic  1.34 us (2%)
    pallas_call x3, Pallas kernels, attend_new(): pl.pallas_call(functools.partial(new_kernel, which, last), out_shape=(out...  13.5 us
    ppermute x4, starting transfers between devices, swapped(): return lax.ppermute(block, 'group', swap_cores())  12.7 us
    ppermute x6, waiting for transfers between devices, first_phase(): lax.ppermute(block, 'group', along(0, d))  7.64 us
    ppermute x6, starting transfers between devices, second_phase(): lax.ppermute(joined, 'group', along(1, d))  6.28 us
    pallas_call x1, Pallas kernels, attend_cache(): pl.pallas_call(functools.partial(cache_kernel, live_keys), out_shape=(STA...  6.27 us
    unnamed x18, local copies, waits for them, and re-layouts  6.21 us
    ppermute x6, starting transfers between devices, first_phase(): lax.ppermute(block, 'group', along(0, d))  5.08 us
    ppermute x1, waiting for transfers between devices, shards(): ahead = lax.ppermute(hidden_rows, both, ring(1))  5.04 us
  transfers between devices with their start and end apart: 19, of which 8 were waited for; matrix products, arithmetic and copies ran while one was open for 1% of the time, Pallas kernels for 26%

profile of v2, /device:TPU:25, one launch (start us, length us, event | category | flops | bytes accessed | tf_op | source)
XLA Modules:
  0.0 81.0 jit_solution(11364998372010863317)
XLA Ops:
  0.6 0.0 copy-start.2
  0.6 2.5 %collective-permute-start = (bf16[32,8192]{1,0:T(8,128)(2,1)}, bf16[32,8192]{1,0:T(8,128)(2,1)S(1)}, u32[]{:S(2)}, u32[]{:S(2)}) collective-permute-start(bf16[32,8192]{1,0:T(8,128)(2,1)} %refs_0_.3), channel_id=1, source_target_pairs={{0,1},{1,2},{2,3},{3,0},{4,7},{5,4},{6,5},{7,6},{8,9},{9,10},{10,1... | collective-permute-start | bytes 1572872 | tf_op jit(solution)/shard_map/ppermute | solution.py:390
  3.2 0.0 copy-start.4
  3.2 0.8 %copy-done.4 = bf16[128,256]{1,0:T(8,128)(2,1)S(1)} copy-done((bf16[128,256]{1,0:T(8,128)(2,1)S(1)}, bf16[128,256]{1,0:T(8,128)(2,1)}, u32[]{:S(2)}) %copy-start.4) | copy-done | bytes 65560
  4.0 0.0 copy-start.5
  4.0 0.8 %copy-done.5 = bf16[128,256]{1,0:T(8,128)(2,1)S(1)} copy-done((bf16[128,256]{1,0:T(8,128)(2,1)S(1)}, bf16[128,256]{1,0:T(8,128)(2,1)}, u32[]{:S(2)}) %copy-start.5) | copy-done | bytes 65560
  4.9 0.1 collective-permute-start.1
  5.0 1.4 %collective-permute-start.11 = (bf16[256,128]{1,0:T(8,128)(2,1)S(1)}, bf16[256,128]{1,0:T(8,128)(2,1)S(1)}, u32[]{:S(2)}, u32[]{:S(2)}) collective-permute-start(bf16[256,128]{1,0:T(8,128)(2,1)S(1)} %get-tuple-element.41), channel_id=1, source_target_pairs={{0,4},{4,0},{8,12},{12,8},{16,20},{20,16},{24,28},{28,24},{32,36},... | collective-permute-start | bytes 196616 | tf_op jit(solution)/shard_map/ppermute | solution.py:383
  6.4 0.3 fusion
  6.8 5.0 %collective-permute-done.refs_1_ = bf16[32,8192]{1,0:T(8,128)(2,1)S(1)} collective-permute-done((bf16[32,8192]{1,0:T(8,128)(2,1)}, bf16[32,8192]{1,0:T(8,128)(2,1)S(1)}, u32[]{:S(2)}, u32[]{:S(2)}) %collective-permute-start) | collective-permute-done | bytes 524320 | tf_op jit(solution)/shard_map/ppermute | solution.py:390
  11.8 3.3 %collective-permute-start.3 = (bf16[32,8192]{1,0:T(8,128)(2,1)S(1)}, bf16[32,8192]{1,0:T(8,128)(2,1)S(1)}, u32[]{:S(2)}, u32[]{:S(2)}) collective-permute-start(bf16[32,8192]{1,0:T(8,128)(2,1)S(1)} %collective-permute-done.refs_1_), channel_id=1, source_target_pairs={{0,1},{1,2},{2,3},{3,0},{4,7},{5,4},{6,5},{7,6},{8,9},{9,10},{10,1... | collective-permute-start | bytes 1572872 | tf_op jit(solution)/shard_map/ppermute | solution.py:393
  15.1 0.0 collective-permute-done.11
  15.1 0.1 collective-permute-start.12
  15.2 0.0 copy-start.3
  15.2 0.1 pad_maximum_fusion
  15.3 1.5 %collective-permute-start.13 = (bf16[512,128]{1,0:T(8,128)(2,1)S(1)}, bf16[512,128]{1,0:T(8,128)(2,1)S(1)}, u32[]{:S(2)}, u32[]{:S(2)}) collective-permute-start(bf16[512,128]{1,0:T(8,128)(2,1)S(1)} %get-tuple-element.55), channel_id=1, source_target_pairs={{0,24},{4,100},{8,0},{12,108},{16,8},{20,116},{24,16},{28,124},{32... | collective-permute-start | bytes 393224 | tf_op jit(solution)/shard_map/ppermute | solution.py:374
  16.8 1.0 %collective-permute-start.14 = (bf16[512,128]{1,0:T(8,128)(2,1)S(1)}, bf16[512,128]{1,0:T(8,128)(2,1)S(1)}, u32[]{:S(2)}, u32[]{:S(2)}) collective-permute-start(bf16[512,128]{1,0:T(8,128)(2,1)S(1)} %get-tuple-element.55), channel_id=1, source_target_pairs={{0,16},{4,68},{8,24},{12,76},{16,0},{20,84},{24,8},{28,92},{32,48}... | collective-permute-start | bytes 393224 | tf_op jit(solution)/shard_map/ppermute | solution.py:374
  17.8 0.0 collective-permute-done.1.refs_2_
  17.8 0.0 copy-start
  17.8 3.4 %copy-done = bf16[2,8192,256]{2,1,0:T(8,128)(2,1)S(1)} copy-done((bf16[2,8192,256]{2,1,0:T(8,128)(2,1)S(1)}, bf16[2,8192,256]{2,1,0:T(8,128)(2,1)}, u32[]{:S(2)}) %copy-start) | copy-done | bytes 8388632
  21.2 0.0 copy-start.1
  21.2 1.0 %copy-done.1 = bf16[32,8192]{1,0:T(8,128)(2,1)S(1)} copy-done((bf16[32,8192]{1,0:T(8,128)(2,1)S(1)}, bf16[32,8192]{1,0:T(8,128)(2,1)}, u32[]{:S(2)}) %copy-start.1) | copy-done | bytes 524312
  22.2 2.4 %project_near.1 = (f32[96,256]{1,0:T(8,128)S(1)}, f32[96,256]{1,0:T(8,128)S(1)}, bf16[2,8192,256]{2,1,0:T(8,128)(2,1)S(1)}) custom-call(bf16[32,8192]{1,0:T(8,128)(2,1)S(1)} %copy-done.1, bf16[32,8192]{1,0:T(8,128)(2,1)S(1)} %collective-permute-done.refs_1_, bf16[32,8192]{1,0:T(8,128)(2,1)S(1)} %collective-permute-done.1.refs_2_, ...), custom_call_target="tpu_custom_call" | custom-call | flops 110000000 | bytes 350000 | tf_op jit(solution)/shard_map/project_near/pallas_call | solution.py:130
  24.7 0.0 copy-done.2
  24.7 0.2 heads.3
  24.8 4.6 %collective-permute-start.2 = (bf16[1024,128]{1,0:T(8,128)(2,1)S(1)}, bf16[1024,128]{1,0:T(8,128)(2,1)S(1)}, u32[]{:S(2)}, u32[]{:S(2)}) collective-permute-start(bf16[1024,128]{1,0:T(8,128)(2,1)S(1)} %get-tuple-element.34), channel_id=1, source_target_pairs={{0,4},{4,0},{8,12},{12,8},{16,20},{20,16},{24,28},{28,24},{32,36},... | collective-permute-start | bytes 786440 | tf_op jit(solution)/shard_map/ppermute | solution.py:383
  29.4 0.0 collective-permute-done.12
  29.4 0.0 collective-permute-done.13
  29.5 0.0 collective-permute-done.14
  29.5 0.8 collective-permute-start.15
  30.3 0.3 collective-permute-done.2.received
  30.6 0.0 collective-permute-done.3.piece
  30.6 2.2 %project_far.1 = (bf16[128,256]{1,0:T(8,128)(2,1)}, bf16[128,256]{1,0:T(8,128)(2,1)}, bf16[256,128]{1,0:T(8,128)(2,1)S(1)}, bf16[256,128]{1,0:T(8,128)(2,1)S(1)}) custom-call(bf16[32,8192]{1,0:T(8,128)(2,1)S(1)} %collective-permute-done.3.piece, f32[96,256]{1,0:T(8,128)S(1)} %get-tuple-element.31.near_keys, f32[96,256]{1,0:T(8,128)S(1)} %get-tuple-element.36.near_values, ...), custom_call_target="tpu_custom_call" | custom-call | flops 110000000 | bytes 350000 | tf_op jit(solution)/shard_map/project_far/pallas_call | solution.py:176
  32.8 0.4 collective-permute-start.4
  33.2 0.9 %collective-permute-done.4 = bf16[256,128]{1,0:T(8,128)(2,1)S(1)} collective-permute-done((bf16[256,128]{1,0:T(8,128)(2,1)S(1)}, bf16[256,128]{1,0:T(8,128)(2,1)S(1)}, u32[]{:S(2)}, u32[]{:S(2)}) %collective-permute-start.4) | collective-permute-done | bytes 65568 | tf_op jit(solution)/shard_map/ppermute | solution.py:383
  34.1 0.3 collective-permute-start.5
  34.4 1.3 %collective-permute-start.6 = (bf16[512,128]{1,0:T(8,128)(2,1)S(1)}, bf16[512,128]{1,0:T(8,128)(2,1)S(1)}, u32[]{:S(2)}, u32[]{:S(2)}) collective-permute-start(bf16[512,128]{1,0:T(8,128)(2,1)S(1)} %get-tuple-element.59), channel_id=1, source_target_pairs={{0,24},{4,100},{8,0},{12,108},{16,8},{20,116},{24,16},{28,124},{32... | collective-permute-start | bytes 393224 | tf_op jit(solution)/shard_map/ppermute | solution.py:374
  35.7 1.7 %collective-permute-start.16 = (bf16[2048,128]{1,0:T(8,128)(2,1)S(1)}, bf16[2048,128]{1,0:T(8,128)(2,1)S(1)}, u32[]{:S(2)}, u32[]{:S(2)}) collective-permute-start(bf16[2048,128]{1,0:T(8,128)(2,1)S(1)} %constant_dynamic-update-slice_fusion.9.refs_0_), channel_id=1, source_target_pairs={{0,96},{4,28},{8,104},{12,4},{16,112},{20,12},{24,120},{28,20},{32... | collective-permute-start | bytes 1572872 | tf_op jit(solution)/shard_map/ppermute | solution.py:379
  37.3 0.9 %collective-permute-start.17 = (bf16[2048,128]{1,0:T(8,128)(2,1)S(1)}, bf16[2048,128]{1,0:T(8,128)(2,1)S(1)}, u32[]{:S(2)}, u32[]{:S(2)}) collective-permute-start(bf16[2048,128]{1,0:T(8,128)(2,1)S(1)} %constant_dynamic-update-slice_fusion.9.refs_0_), channel_id=1, source_target_pairs={{0,64},{4,20},{8,72},{12,28},{16,80},{20,4},{24,88},{28,12},{32,96... | collective-permute-start | bytes 1572872 | tf_op jit(solution)/shard_map/ppermute | solution.py:379
  38.2 1.6 %collective-permute-done.5 = bf16[512,128]{1,0:T(8,128)(2,1)S(1)} collective-permute-done((bf16[512,128]{1,0:T(8,128)(2,1)S(1)}, bf16[512,128]{1,0:T(8,128)(2,1)S(1)}, u32[]{:S(2)}, u32[]{:S(2)}) %collective-permute-start.5) | collective-permute-done | bytes 131104 | tf_op jit(solution)/shard_map/ppermute | solution.py:374
  39.8 1.0 %collective-permute-start.7 = (bf16[512,128]{1,0:T(8,128)(2,1)S(1)}, bf16[512,128]{1,0:T(8,128)(2,1)S(1)}, u32[]{:S(2)}, u32[]{:S(2)}) collective-permute-start(bf16[512,128]{1,0:T(8,128)(2,1)S(1)} %get-tuple-element.59), channel_id=1, source_target_pairs={{0,16},{4,68},{8,24},{12,76},{16,0},{20,84},{24,8},{28,92},{32,48}... | collective-permute-start | bytes 393224 | tf_op jit(solution)/shard_map/ppermute | solution.py:374
  40.8 0.0 collective-permute-done.6
  40.8 6.0 %collective-permute-done.7 = bf16[512,128]{1,0:T(8,128)(2,1)S(1)} collective-permute-done((bf16[512,128]{1,0:T(8,128)(2,1)S(1)}, bf16[512,128]{1,0:T(8,128)(2,1)S(1)}, u32[]{:S(2)}, u32[]{:S(2)}) %collective-permute-start.7) | collective-permute-done | bytes 131104 | tf_op jit(solution)/shard_map/ppermute | solution.py:374
  46.9 0.8 collective-permute-start.9
  47.7 1.9 %collective-permute-start.10 = (bf16[2048,128]{1,0:T(8,128)(2,1)S(1)}, bf16[2048,128]{1,0:T(8,128)(2,1)S(1)}, u32[]{:S(2)}, u32[]{:S(2)}) collective-permute-start(bf16[2048,128]{1,0:T(8,128)(2,1)S(1)} %constant_dynamic-update-slice_fusion.2.refs_0_), channel_id=1, source_target_pairs={{0,96},{4,28},{8,104},{12,4},{16,112},{20,12},{24,120},{28,20},{32... | collective-permute-start | bytes 1572872 | tf_op jit(solution)/shard_map/ppermute | solution.py:379
  49.6 0.0 collective-permute-done.15.refs_1_
  49.6 0.2 collective-permute-start.8
  49.8 2.0 %collective-permute-done.16.refs_2_ = bf16[2048,128]{1,0:T(8,128)(2,1)S(1)} collective-permute-done((bf16[2048,128]{1,0:T(8,128)(2,1)S(1)}, bf16[2048,128]{1,0:T(8,128)(2,1)S(1)}, u32[]{:S(2)}, u32[]{:S(2)}) %collective-permute-start.16) | collective-permute-done | bytes 524320 | tf_op jit(solution)/shard_map/ppermute | solution.py:379
  51.9 0.0 collective-permute-done.17.refs_3_
  51.9 0.0 copy-done.3
  51.9 6.3 %attend_cache.1 = (f32[2048,128]{1,0:T(8,128)S(1)}, f32[2048,128]{1,0:T(8,128)S(1)}, f32[2048,128]{1,0:T(8,128)S(1)}) custom-call(s32[32]{0:T(128)S(1)} %copy-done.3, bf16[1024,128]{1,0:T(8,128)(2,1)S(1)} %get-tuple-element.40.own_queries, bf16[1024,128]{1,0:T(8,128)(2,1)S(1)} %collective-permute-done.2.received, ...), custom_call_target="tpu_custom_call" | custom-call | flops 110000000 | bytes 350000 | tf_op jit(solution)/shard_map/attend_cache/pallas_call | solution.py:246
  58.2 4.1 %attend_new.2 = (f32[2048,128]{1,0:T(8,128)S(1)}, f32[2048,128]{1,0:T(8,128)S(1)}, f32[2048,128]{1,0:T(8,128)S(1)}) custom-call(bf16[1024,128]{1,0:T(8,128)(2,1)S(1)} %get-tuple-element.40.own_queries, bf16[1024,128]{1,0:T(8,128)(2,1)S(1)} %collective-permute-done.2.received, bf16[2048,128]{1,0:T(8,128)(2,1)S(1)} %constant_dynamic-update-slice_fusion.2.refs_0_, ...), custom_call_target="tpu_custom_call" | custom-call | flops 110000000 | bytes 350000 | tf_op jit(solution)/shard_map/attend_new/pallas_call | solution.py:350
  62.3 0.0 collective-permute-done.9.refs_0_
  62.3 0.8 collective-permute-done.10.refs_1_
  63.1 6.0 %attend_new.3 = (f32[2048,128]{1,0:T(8,128)S(1)}, f32[2048,128]{1,0:T(8,128)S(1)}, f32[2048,128]{1,0:T(8,128)S(1)}) custom-call(bf16[1024,128]{1,0:T(8,128)(2,1)S(1)} %get-tuple-element.40.own_queries, bf16[1024,128]{1,0:T(8,128)(2,1)S(1)} %collective-permute-done.2.received, bf16[2048,128]{1,0:T(8,128)(2,1)S(1)} %collective-permute-done.9.refs_0_, ...), custom_call_target="tpu_custom_call" | custom-call | flops 110000000 | bytes 350000 | tf_op jit(solution)/shard_map/attend_new/pallas_call | solution.py:350
  69.1 0.0 collective-permute-done.8.refs_0_
  69.1 3.4 %attend_new_last.1 = (bf16[128,1024]{1,0:T(8,128)(2,1)S(1)}, bf16[128,1024]{1,0:T(8,128)(2,1)S(1)}) custom-call(bf16[1024,128]{1,0:T(8,128)(2,1)S(1)} %get-tuple-element.40.own_queries, bf16[1024,128]{1,0:T(8,128)(2,1)S(1)} %collective-permute-done.2.received, bf16[2048,128]{1,0:T(8,128)(2,1)S(1)} %collective-permute-done.8.refs_0_, ...), custom_call_target="tpu_custom_call" | custom-call | flops 110000000 | bytes 350000 | tf_op jit(solution)/shard_map/attend_new_last/pallas_call | solution.py:350
  72.5 6.4 %collective-permute-start.18 = (bf16[128,1024]{1,0:T(8,128)(2,1)S(1)}, bf16[128,1024]{1,0:T(8,128)(2,1)S(1)}, u32[]{:S(2)}, u32[]{:S(2)}) collective-permute-start(bf16[128,1024]{1,0:T(8,128)(2,1)S(1)} %get-tuple-element.52), channel_id=1, source_target_pairs={{0,4},{4,0},{8,12},{12,8},{16,20},{20,16},{24,28},{28,24},{32,36},... | collective-permute-start | bytes 786440 | tf_op jit(solution)/shard_map/ppermute | solution.py:383
  78.9 1.2 %collective-permute-done.18 = bf16[128,1024]{1,0:T(8,128)(2,1)S(1)} collective-permute-done((bf16[128,1024]{1,0:T(8,128)(2,1)S(1)}, bf16[128,1024]{1,0:T(8,128)(2,1)S(1)}, u32[]{:S(2)}, u32[]{:S(2)}) %collective-permute-start.18) | collective-permute-done | bytes 262176 | tf_op jit(solution)/shard_map/ppermute | solution.py:383
  80.1 0.9 %maximum_select_fusion = bf16[128,2048]{1,0:T(8,128)(2,1)} fusion(bf16[128,1024]{1,0:T(8,128)(2,1)S(1)} %collective-permute-done.18, bf16[128,1024]{1,0:T(8,128)(2,1)S(1)} %get-tuple-element.51, pred[]{:T(512)S(6)} %eq.3), kind=kLoop, calls=%fused_computation | loop fusion | flops 2359296 | bytes 1048577 | tf_op jit(solution)/shard_map/jit(_where)/select_n | solution.py:420
  (13 shorter events, 0.2 us)
Async XLA Ops:
  0.6 24.0 %copy-start.2 = (bf16[128,2048]{1,0:T(8,128)(2,1)S(1)}, bf16[128,2048]{1,0:T(8,128)(2,1)}, u32[]{:S(2)}) copy-start(bf16[128,2048]{1,0:T(8,128)(2,1)} %refs_0_.4) | copy-start | bytes 1572868
  0.6 11.2 %collective-permute-start = (bf16[32,8192]{1,0:T(8,128)(2,1)}, bf16[32,8192]{1,0:T(8,128)(2,1)S(1)}, u32[]{:S(2)}, u32[]{:S(2)}) collective-permute-start(bf16[32,8192]{1,0:T(8,128)(2,1)} %refs_0_.3), channel_id=1, source_target_pairs={{0,1},{1,2},{2,3},{3,0},{4,7},{5,4},{6,5},{7,6},{8,9},{9,10},{10,1... | collective-permute-start | bytes 1572872 | tf_op jit(solution)/shard_map/ppermute | solution.py:390
  3.2 0.8 %copy-start.4 = (bf16[128,256]{1,0:T(8,128)(2,1)S(1)}, bf16[128,256]{1,0:T(8,128)(2,1)}, u32[]{:S(2)}) copy-start(bf16[128,256]{1,0:T(8,128)(2,1)} %refs_0_.2) | copy-start | bytes 196612
  4.0 0.8 %copy-start.5 = (bf16[128,256]{1,0:T(8,128)(2,1)S(1)}, bf16[128,256]{1,0:T(8,128)(2,1)}, u32[]{:S(2)}) copy-start(bf16[128,256]{1,0:T(8,128)(2,1)} %refs_1_.1) | copy-start | bytes 196612
  4.9 12.9 %collective-permute-start.1 = (bf16[32,8192]{1,0:T(8,128)(2,1)}, bf16[32,8192]{1,0:T(8,128)(2,1)S(1)}, u32[]{:S(2)}, u32[]{:S(2)}) collective-permute-start(bf16[32,8192]{1,0:T(8,128)(2,1)} %refs_0_.3), channel_id=1, source_target_pairs={{0,3},{1,0},{2,1},{3,2},{4,5},{5,6},{6,7},{7,4},{8,11},{9,8},{10,9... | collective-permute-start | bytes 1572872 | tf_op jit(solution)/shard_map/ppermute | solution.py:392
  5.0 10.1 %collective-permute-start.11 = (bf16[256,128]{1,0:T(8,128)(2,1)S(1)}, bf16[256,128]{1,0:T(8,128)(2,1)S(1)}, u32[]{:S(2)}, u32[]{:S(2)}) collective-permute-start(bf16[256,128]{1,0:T(8,128)(2,1)S(1)} %get-tuple-element.41), channel_id=1, source_target_pairs={{0,4},{4,0},{8,12},{12,8},{16,20},{20,16},{24,28},{28,24},{32,36},... | collective-permute-start | bytes 196616 | tf_op jit(solution)/shard_map/ppermute | solution.py:383
  11.8 18.8 %collective-permute-start.3 = (bf16[32,8192]{1,0:T(8,128)(2,1)S(1)}, bf16[32,8192]{1,0:T(8,128)(2,1)S(1)}, u32[]{:S(2)}, u32[]{:S(2)}) collective-permute-start(bf16[32,8192]{1,0:T(8,128)(2,1)S(1)} %collective-permute-done.refs_1_), channel_id=1, source_target_pairs={{0,1},{1,2},{2,3},{3,0},{4,7},{5,4},{6,5},{7,6},{8,9},{9,10},{10,1... | collective-permute-start | bytes 1572872 | tf_op jit(solution)/shard_map/ppermute | solution.py:393
  15.1 14.3 %collective-permute-start.12 = (bf16[512,128]{1,0:T(8,128)(2,1)S(1)}, bf16[512,128]{1,0:T(8,128)(2,1)S(1)}, u32[]{:S(2)}, u32[]{:S(2)}) collective-permute-start(bf16[512,128]{1,0:T(8,128)(2,1)S(1)} %get-tuple-element.55), channel_id=1, source_target_pairs={{0,8},{4,36},{8,16},{12,44},{16,24},{20,52},{24,0},{28,60},{32,40}... | collective-permute-start | bytes 393224 | tf_op jit(solution)/shard_map/ppermute | solution.py:374
  15.2 36.7 %copy-start.3 = (s32[32]{0:T(128)S(1)}, s32[32]{0:T(128)}, u32[]{:S(2)}) copy-start(s32[32]{0:T(128)} %kv_blocks.1) | copy-start | bytes 388
  15.3 14.1 %collective-permute-start.13 = (bf16[512,128]{1,0:T(8,128)(2,1)S(1)}, bf16[512,128]{1,0:T(8,128)(2,1)S(1)}, u32[]{:S(2)}, u32[]{:S(2)}) collective-permute-start(bf16[512,128]{1,0:T(8,128)(2,1)S(1)} %get-tuple-element.55), channel_id=1, source_target_pairs={{0,24},{4,100},{8,0},{12,108},{16,8},{20,116},{24,16},{28,124},{32... | collective-permute-start | bytes 393224 | tf_op jit(solution)/shard_map/ppermute | solution.py:374
  16.8 12.7 %collective-permute-start.14 = (bf16[512,128]{1,0:T(8,128)(2,1)S(1)}, bf16[512,128]{1,0:T(8,128)(2,1)S(1)}, u32[]{:S(2)}, u32[]{:S(2)}) collective-permute-start(bf16[512,128]{1,0:T(8,128)(2,1)S(1)} %get-tuple-element.55), channel_id=1, source_target_pairs={{0,16},{4,68},{8,24},{12,76},{16,0},{20,84},{24,8},{28,92},{32,48}... | collective-permute-start | bytes 393224 | tf_op jit(solution)/shard_map/ppermute | solution.py:374
  17.8 3.4 %copy-start = (bf16[2,8192,256]{2,1,0:T(8,128)(2,1)S(1)}, bf16[2,8192,256]{2,1,0:T(8,128)(2,1)}, u32[]{:S(2)}) copy-start(bf16[2,8192,256]{2,1,0:T(8,128)(2,1)} %refs_3_.1) | copy-start | bytes 25165828
  21.2 1.0 %copy-start.1 = (bf16[32,8192]{1,0:T(8,128)(2,1)S(1)}, bf16[32,8192]{1,0:T(8,128)(2,1)}, u32[]{:S(2)}) copy-start(bf16[32,8192]{1,0:T(8,128)(2,1)} %refs_0_.3) | copy-start | bytes 1572868
  24.8 5.7 %collective-permute-start.2 = (bf16[1024,128]{1,0:T(8,128)(2,1)S(1)}, bf16[1024,128]{1,0:T(8,128)(2,1)S(1)}, u32[]{:S(2)}, u32[]{:S(2)}) collective-permute-start(bf16[1024,128]{1,0:T(8,128)(2,1)S(1)} %get-tuple-element.34), channel_id=1, source_target_pairs={{0,4},{4,0},{8,12},{12,8},{16,20},{20,16},{24,28},{28,24},{32,36},... | collective-permute-start | bytes 786440 | tf_op jit(solution)/shard_map/ppermute | solution.py:383
  29.5 20.1 %collective-permute-start.15 = (bf16[2048,128]{1,0:T(8,128)(2,1)S(1)}, bf16[2048,128]{1,0:T(8,128)(2,1)S(1)}, u32[]{:S(2)}, u32[]{:S(2)}) collective-permute-start(bf16[2048,128]{1,0:T(8,128)(2,1)S(1)} %constant_dynamic-update-slice_fusion.9.refs_0_), channel_id=1, source_target_pairs={{0,32},{4,12},{8,40},{12,20},{16,48},{20,28},{24,56},{28,4},{32,64... | collective-permute-start | bytes 1572872 | tf_op jit(solution)/shard_map/ppermute | solution.py:379
  32.8 1.3 %collective-permute-start.4 = (bf16[256,128]{1,0:T(8,128)(2,1)S(1)}, bf16[256,128]{1,0:T(8,128)(2,1)S(1)}, u32[]{:S(2)}, u32[]{:S(2)}) collective-permute-start(bf16[256,128]{1,0:T(8,128)(2,1)S(1)} %get-tuple-element.39), channel_id=1, source_target_pairs={{0,4},{4,0},{8,12},{12,8},{16,20},{20,16},{24,28},{28,24},{32,36},... | collective-permute-start | bytes 196616 | tf_op jit(solution)/shard_map/ppermute | solution.py:383
  34.1 5.6 %collective-permute-start.5 = (bf16[512,128]{1,0:T(8,128)(2,1)S(1)}, bf16[512,128]{1,0:T(8,128)(2,1)S(1)}, u32[]{:S(2)}, u32[]{:S(2)}) collective-permute-start(bf16[512,128]{1,0:T(8,128)(2,1)S(1)} %get-tuple-element.59), channel_id=1, source_target_pairs={{0,8},{4,36},{8,16},{12,44},{16,24},{20,52},{24,0},{28,60},{32,40}... | collective-permute-start | bytes 393224 | tf_op jit(solution)/shard_map/ppermute | solution.py:374
  34.4 6.4 %collective-permute-start.6 = (bf16[512,128]{1,0:T(8,128)(2,1)S(1)}, bf16[512,128]{1,0:T(8,128)(2,1)S(1)}, u32[]{:S(2)}, u32[]{:S(2)}) collective-permute-start(bf16[512,128]{1,0:T(8,128)(2,1)S(1)} %get-tuple-element.59), channel_id=1, source_target_pairs={{0,24},{4,100},{8,0},{12,108},{16,8},{20,116},{24,16},{28,124},{32... | collective-permute-start | bytes 393224 | tf_op jit(solution)/shard_map/ppermute | solution.py:374
  35.7 16.2 %collective-permute-start.16 = (bf16[2048,128]{1,0:T(8,128)(2,1)S(1)}, bf16[2048,128]{1,0:T(8,128)(2,1)S(1)}, u32[]{:S(2)}, u32[]{:S(2)}) collective-permute-start(bf16[2048,128]{1,0:T(8,128)(2,1)S(1)} %constant_dynamic-update-slice_fusion.9.refs_0_), channel_id=1, source_target_pairs={{0,96},{4,28},{8,104},{12,4},{16,112},{20,12},{24,120},{28,20},{32... | collective-permute-start | bytes 1572872 | tf_op jit(solution)/shard_map/ppermute | solution.py:379
  37.3 14.6 %collective-permute-start.17 = (bf16[2048,128]{1,0:T(8,128)(2,1)S(1)}, bf16[2048,128]{1,0:T(8,128)(2,1)S(1)}, u32[]{:S(2)}, u32[]{:S(2)}) collective-permute-start(bf16[2048,128]{1,0:T(8,128)(2,1)S(1)} %constant_dynamic-update-slice_fusion.9.refs_0_), channel_id=1, source_target_pairs={{0,64},{4,20},{8,72},{12,28},{16,80},{20,4},{24,88},{28,12},{32,96... | collective-permute-start | bytes 1572872 | tf_op jit(solution)/shard_map/ppermute | solution.py:379
  39.8 7.1 %collective-permute-start.7 = (bf16[512,128]{1,0:T(8,128)(2,1)S(1)}, bf16[512,128]{1,0:T(8,128)(2,1)S(1)}, u32[]{:S(2)}, u32[]{:S(2)}) collective-permute-start(bf16[512,128]{1,0:T(8,128)(2,1)S(1)} %get-tuple-element.59), channel_id=1, source_target_pairs={{0,16},{4,68},{8,24},{12,76},{16,0},{20,84},{24,8},{28,92},{32,48}... | collective-permute-start | bytes 393224 | tf_op jit(solution)/shard_map/ppermute | solution.py:374
  46.9 15.4 %collective-permute-start.9 = (bf16[2048,128]{1,0:T(8,128)(2,1)S(1)}, bf16[2048,128]{1,0:T(8,128)(2,1)S(1)}, u32[]{:S(2)}, u32[]{:S(2)}) collective-permute-start(bf16[2048,128]{1,0:T(8,128)(2,1)S(1)} %constant_dynamic-update-slice_fusion.2.refs_0_), channel_id=1, source_target_pairs={{0,32},{4,12},{8,40},{12,20},{16,48},{20,28},{24,56},{28,4},{32,64... | collective-permute-start | bytes 1572872 | tf_op jit(solution)/shard_map/ppermute | solution.py:379
  47.7 15.4 %collective-permute-start.10 = (bf16[2048,128]{1,0:T(8,128)(2,1)S(1)}, bf16[2048,128]{1,0:T(8,128)(2,1)S(1)}, u32[]{:S(2)}, u32[]{:S(2)}) collective-permute-start(bf16[2048,128]{1,0:T(8,128)(2,1)S(1)} %constant_dynamic-update-slice_fusion.2.refs_0_), channel_id=1, source_target_pairs={{0,96},{4,28},{8,104},{12,4},{16,112},{20,12},{24,120},{28,20},{32... | collective-permute-start | bytes 1572872 | tf_op jit(solution)/shard_map/ppermute | solution.py:379
  49.6 19.5 %collective-permute-start.8 = (bf16[2048,128]{1,0:T(8,128)(2,1)S(1)}, bf16[2048,128]{1,0:T(8,128)(2,1)S(1)}, u32[]{:S(2)}, u32[]{:S(2)}) collective-permute-start(bf16[2048,128]{1,0:T(8,128)(2,1)S(1)} %constant_dynamic-update-slice_fusion.2.refs_0_), channel_id=1, source_target_pairs={{0,64},{4,20},{8,72},{12,28},{16,80},{20,4},{24,88},{28,12},{32,96... | collective-permute-start | bytes 1572872 | tf_op jit(solution)/shard_map/ppermute | solution.py:379
  72.5 7.5 %collective-permute-start.18 = (bf16[128,1024]{1,0:T(8,128)(2,1)S(1)}, bf16[128,1024]{1,0:T(8,128)(2,1)S(1)}, u32[]{:S(2)}, u32[]{:S(2)}) collective-permute-start(bf16[128,1024]{1,0:T(8,128)(2,1)S(1)} %get-tuple-element.52), channel_id=1, source_target_pairs={{0,4},{4,0},{8,12},{12,8},{16,20},{20,16},{24,28},{28,24},{32,36},... | collective-permute-start | bytes 786440 | tf_op jit(solution)/shard_map/ppermute | solution.py:383

commit v3 on v2

--- a/solution.py
+++ b/solution.py
@@ -79,7 +79,7 @@
                 at += ROWS
 
 
-def heads(width, *arrays):
+def heads(width, microseconds, *arrays):
     rows = len(arrays) * width // HEAD_DIM * ROWS
     tall = jax.ShapeDtypeStruct((rows, HEAD_DIM), BF16)
     return pl.pallas_call(
@@ -87,8 +87,8 @@
         out_shape=(tall, tall),
         in_specs=[VMEM] * len(arrays),
         out_specs=(VMEM,) * 2,
-        compiler_params=pltpu.CompilerParams(vmem_limit_bytes=8 << 20),
-        cost_estimate=cost(0.1),
+        compiler_params=pltpu.CompilerParams(vmem_limit_bytes=4 << 20),
+        cost_estimate=cost(microseconds),
         name="heads",
     )(*arrays)
 
@@ -100,26 +100,17 @@
 
 
 def near_kernel(*refs):
-    pieces, weight, keys_out, values_out, held, rows, sems = refs[:3], *refs[3:]
-    chunks = sems.shape[0]
-    step = held.shape[1] // chunks
-
-    def fetch(i):
-        part = pl.ds(i * step, step)
-        return pltpu.make_async_copy(weight.at[:, part, :], held.at[:, part, :], sems.at[i])
-
-    for i in range(chunks):
-        fetch(i).start()
+    pieces, weight, keys_out, values_out, rows = refs[:3], *refs[3:]
     size = pieces[0].shape[0]
     for i, piece in enumerate(pieces):
         rows[i * size : (i + 1) * size, :] = piece[...]
     keys = jnp.zeros(keys_out.shape, F32)
     values = jnp.zeros(keys_out.shape, F32)
-    for i in range(chunks):
-        fetch(i).wait()
-        part = slice(i * step, (i + 1) * step)
-        keys += jnp.dot(rows[:, part], held[0, part, :], preferred_element_type=F32)
-        values += jnp.dot(rows[:, part], held[1, part, :], preferred_element_type=F32)
+    step = 1024
+    for i in range(0, rows.shape[1], step):
+        part = slice(i, i + step)
+        keys += jnp.dot(rows[:, part], weight[0, part, :], preferred_element_type=F32)
+        values += jnp.dot(rows[:, part], weight[1, part, :], preferred_element_type=F32)
     keys_out[...] = keys
     values_out[...] = values
 
@@ -129,15 +120,12 @@
     wide = jax.ShapeDtypeStruct((count, weight.shape[2]), F32)
     return pl.pallas_call(
         near_kernel,
-        out_shape=(wide, wide, jax.ShapeDtypeStruct(weight.shape, BF16)),
-        in_specs=[VMEM] * 3 + [pl.BlockSpec(memory_space=pltpu.HBM)],
-        out_specs=(VMEM,) * 3,
-        scratch_shapes=[
-            pltpu.VMEM((count, weight.shape[1]), BF16),
-            pltpu.SemaphoreType.DMA((8,)),
-        ],
-        compiler_params=pltpu.CompilerParams(vmem_limit_bytes=32 << 20),
-        cost_estimate=cost(0.1),
+        out_shape=(wide, wide),
+        in_specs=[VMEM] * 4,
+        out_specs=(VMEM,) * 2,
+        scratch_shapes=[pltpu.VMEM((count, weight.shape[1]), BF16)],
+        compiler_params=pltpu.CompilerParams(vmem_limit_bytes=24 << 20),
+        cost_estimate=cost(20),
         name="project_near",
     )(*pieces, weight)
 
@@ -201,7 +189,7 @@
     return raised, den, num
 
 
-TILE = 512
+TILE = 1024
 
 
 def tiles(own_queries, received):
@@ -306,31 +294,27 @@
             pl.when(seen)(keep)
             found = found + seen.astype(jnp.int32)
 
-    def one(i, sources):
-        there = pl.ds(pl.multiple_of(i * size, size), size)
+    def chunk(first, blocks, sources):
+        there = pl.ds(pl.multiple_of(first * size, size), blocks * size)
         visit(turned[:, there], held[there, :], sources)
 
-    def rest(first):
+    def rest(first, sources):
+        left = found - first
+
         def body(i, _):
-            one(i, sums)
+            chunk(first + 4 * i, 4, sources)
             return 0
 
-        lax.fori_loop(first, found, body, 0)
+        lax.fori_loop(0, left // 4, body, 0)
+        pl.when((left & 2) != 0)(lambda: chunk(first + (left // 4) * 4, 2, sources))
+        pl.when((left & 1) != 0)(lambda: chunk(found - 1, 1, sources))
 
     if which[0] == 0:
         visit(*block_of(pieces[0], 0), olds, causal)
-        rest(0)
     else:
-
-        @pl.when(found == 0)
-        def _():
-            for new, old in zip(sums, olds):
-                new[...] = old[...]
-
-        @pl.when(found > 0)
-        def _():
-            one(0, olds)
-            rest(1)
+        for new, old in zip(sums, olds):
+            new[...] = old[...]
+    rest(jnp.int32(0), sums)
 
     if last:
         here, there = outs[:2]
@@ -369,14 +353,17 @@
     return lax.optimization_barrier((value, *others))[0]
 
 
-def first_phase(block):
-    return jnp.concatenate(
-        [block] + [lax.ppermute(block, "group", along(0, d)) for d in (1, 3, 2)], 0
-    )
+def first_phase(block, *others):
+    sent = [lax.ppermute(block, "group", along(0, d)) for d in (1, 3, 2)]
+    return jnp.concatenate([after(block, *others) if others else block] + sent, 0)
 
 
 def second_phase(joined):
-    return [joined] + [lax.ppermute(joined, "group", along(1, d)) for d in (1, 3, 2)]
+    return [joined] + [lax.ppermute(joined, "group", along(1, d)) for d in (1, 3)]
+
+
+def last_phase(joined, *others):
+    return lax.ppermute(after(joined, *others), "group", along(1, 2))
 
 
 def swapped(block):
@@ -388,10 +375,14 @@
     core = lax.rem(group, 2)
     both = ("group", "tensor")
     ahead = lax.ppermute(hidden_rows, both, ring(1))
-    mine, give = heads(HEAD_DIM, cache_keys, cache_values)
+    mine, give = heads(HEAD_DIM, 0.1, cache_keys, cache_values)
     behind = lax.ppermute(after(hidden_rows, mine), both, ring(3))
-    far = lax.ppermute(ahead, both, ring(1))
-    cache = second_phase(first_phase(jnp.concatenate([mine, swapped(give)], 0)))
+    block = jnp.concatenate([mine, swapped(give)], 0)
+    joined = first_phase(block)
+    own_queries, give_queries = heads(SHARE * HEAD_DIM, 20, after(queries, block))
+    received = swapped(give_queries)
+    far = lax.ppermute(after(ahead, own_queries), both, ring(1))
+    cache = second_phase(joined)
 
     live_keys = cache_keys.shape[0] * kv_blocks.shape[0] // 2
     half = HEAD_DIM // 2
@@ -399,21 +390,22 @@
     freq = jnp.exp(jnp.arange(half, dtype=F32) * (-2.0 * math.log(500000.0) / HEAD_DIM))
     angle = positions.astype(F32)[:, None] * freq[None, :]
     cosine, sine = jnp.cos(angle), jnp.sin(angle)
-    near_keys, near_values, weight = project_near((hidden_rows, ahead, behind), kv_weight)
-    own_queries, give_queries = heads(SHARE * HEAD_DIM, after(queries, near_keys))
-    received = swapped(give_queries)
+    near_keys, near_values = project_near((hidden_rows, ahead, behind), kv_weight)
+    cache.append(last_phase(joined, near_keys))
     new_keys, new_values, mine, give = project_far(
         after(far, received),
         near_keys,
         near_values,
-        weight,
+        kv_weight,
         jnp.concatenate([cosine, cosine], 1),
         jnp.concatenate([-sine, sine], 1),
     )
-    joined = first_phase(jnp.concatenate([mine, swapped(give)], 0))
+    block = after(jnp.concatenate([mine, swapped(give)], 0), *cache[:3])
+    states = attend_cache(kv_blocks, after(own_queries, block), received, cache, live_keys)
+    joined = first_phase(block, states[0])
     new = second_phase(joined)
-    states = attend_cache(kv_blocks, after(own_queries, joined), received, cache, live_keys)
     states = attend_new(own_queries, received, (0,), new[:1], states, False)
+    new.append(last_phase(joined, states[0]))
     states = attend_new(own_queries, received, (1, 2), new[1:3], states, False)
     here, there = attend_new(own_queries, received, (3,), new[3:], states, True)
     other = swapped(there)

time: 82.2 us -> 73 us (0.89); the launches traced: 81 us -> 72.7 us
  waiting for transfers between devices: 17.8 us -> 14.4 us
  local copies, waits for them, and re-layouts: 6.29 us -> 2.9 us
  Pallas kernels: 24.7 us -> 22.2 us
  starting transfers between devices: 30 us -> 30.9 us
    ppermute x6 -> x4, waiting for transfers between devices: 2.86 us -> 9.75 us  [second_phase(): lax.ppermute(joined, 'group', along(1, d))]
    ppermute x7 -> x9, waiting for transfers between devices: 7.64 us -> 2.6 us  [the longest x1 1.82 us: shards(): far = lax.ppermute(after(ahead, own_queries), both, ring(1))]
    ppermute x1, waiting for transfers between devices: 5.04 us -> 0.01 us  [shards(): ahead = lax.ppermute(hidden_rows, both, ring(1))]
    unnamed x18 -> x21, local copies, waits for them, and re-layouts: 6.21 us -> 2.86 us
    ppermute x6 -> x4, starting transfers between devices: 6.28 us -> 3.07 us  [second_phase(): lax.ppermute(joined, 'group', along(1, d))]
    ppermute x7 -> x9, starting transfers between devices: 8.38 us -> 11.2 us  [the longest x6 5.24 us: first_phase(): sent = [lax.ppermute(block, 'group', along(0, d)) for d in (1, 3, 2)]]
    ppermute x4, starting transfers between devices: 12.7 us -> 14.1 us  [swapped(): return lax.ppermute(block, 'group', swap_cores())]
    pallas_call x3, Pallas kernels: 13.5 us -> 12.4 us  [attend_new(): pl.pallas_call(functools.partial(new_kernel, which, last), out_shape=(out...]
  transfers between devices with their start and end apart: 19 -> 19, of which waited for: 8 -> 6; matrix products, arithmetic and copies ran while one was open for 1% -> 1% of each run, Pallas kernels for 26% -> 26%
where the time goes in v3:
time: 73 us; the launch traced here: 72.7 us
  starting transfers between devices  30.9 us (42%)
  Pallas kernels  22.2 us (30%)
  waiting for transfers between devices  14.4 us (20%)
  local copies, waits for them, and re-layouts  2.9 us (4%)
  other arithmetic  1.35 us (2%)
  between operations  0.92 us (1%)
    ppermute x4, starting transfers between devices, swapped(): return lax.ppermute(block, 'group', swap_cores())  14.1 us
    pallas_call x3, Pallas kernels, attend_new(): pl.pallas_call(functools.partial(new_kernel, which, last), out_shape=(out...  12.4 us
    ppermute x4, waiting for transfers between devices, second_phase(): lax.ppermute(joined, 'group', along(1, d))  9.75 us
    pallas_call x1, Pallas kernels, attend_cache(): pl.pallas_call(functools.partial(cache_kernel, live_keys), out_shape=(STA...  6.02 us
    ppermute x6, starting transfers between devices, first_phase(): sent = [lax.ppermute(block, 'group', along(0, d)) for d in (1, 3, 2)]  5.24 us
    ppermute x2, starting transfers between devices, last_phase(): return lax.ppermute(after(joined, *others), 'group', along(1, 2))  4.69 us
    ppermute x4, starting transfers between devices, second_phase(): lax.ppermute(joined, 'group', along(1, d))  3.07 us
    unnamed x21, local copies, waits for them, and re-layouts  2.86 us
  transfers between devices with their start and end apart: 19, of which 6 were waited for; matrix products, arithmetic and copies ran while one was open for 1% of the time, Pallas kernels for 26%

profile of v3, /device:TPU:25, one launch (start us, length us, event | category | flops | bytes accessed | tf_op | source)
XLA Modules:
  0.0 72.7 jit_solution(6281736242661750535)
XLA Ops:
  0.6 0.0 copy-start.3
  0.6 0.8 %copy-done.3 = bf16[128,256]{1,0:T(8,128)(2,1)S(1)} copy-done((bf16[128,256]{1,0:T(8,128)(2,1)S(1)}, bf16[128,256]{1,0:T(8,128)(2,1)}, u32[]{:S(2)}) %copy-start.3) | copy-done | bytes 65560
  1.5 0.0 copy-start.4
  1.5 0.8 %copy-done.4 = bf16[128,256]{1,0:T(8,128)(2,1)S(1)} copy-done((bf16[128,256]{1,0:T(8,128)(2,1)S(1)}, bf16[128,256]{1,0:T(8,128)(2,1)}, u32[]{:S(2)}) %copy-start.4) | copy-done | bytes 65560
  2.3 0.8 %collective-permute-start = (bf16[256,128]{1,0:T(8,128)(2,1)S(1)}, bf16[256,128]{1,0:T(8,128)(2,1)S(1)}, u32[]{:S(2)}, u32[]{:S(2)}) collective-permute-start(bf16[256,128]{1,0:T(8,128)(2,1)S(1)} %get-tuple-element.34), channel_id=1, source_target_pairs={{0,4},{4,0},{8,12},{12,8},{16,20},{20,16},{24,28},{28,24},{32,36},... | collective-permute-start | bytes 196616 | tf_op jit(solution)/shard_map/ppermute | solution.py:370
  3.1 2.5 %collective-permute-start.2 = (bf16[32,8192]{1,0:T(8,128)(2,1)}, bf16[32,8192]{1,0:T(8,128)(2,1)S(1)}, u32[]{:S(2)}, u32[]{:S(2)}) collective-permute-start(bf16[32,8192]{1,0:T(8,128)(2,1)} %refs_0_.4), channel_id=1, source_target_pairs={{0,1},{1,2},{2,3},{3,0},{4,7},{5,4},{6,5},{7,6},{8,9},{9,10},{10,1... | collective-permute-start | bytes 1572872 | tf_op jit(solution)/shard_map/ppermute | solution.py:377
  5.6 0.0 collective-permute-start.4
  5.6 0.0 collective-permute-done
  5.7 0.0 slice-start
  5.7 0.0 slice-start.1
  5.7 1.0 %collective-permute-start.8 = (bf16[512,128]{1,0:T(8,128)(2,1)S(1)}, bf16[512,128]{1,0:T(8,128)(2,1)S(1)}, u32[]{:S(2)}, u32[]{:S(2)}) collective-permute-start(bf16[512,128]{1,0:T(8,128)(2,1)S(1)} %get-tuple-element.64), channel_id=1, source_target_pairs={{0,16},{4,68},{8,24},{12,76},{16,0},{20,84},{24,8},{28,92},{32,48}... | collective-permute-start | bytes 393224 | tf_op jit(solution)/shard_map/ppermute | solution.py:357
  6.7 0.0 collective-permute-start.7
  6.7 2.7 %collective-permute-start.6 = (bf16[512,128]{1,0:T(8,128)(2,1)S(1)}, bf16[512,128]{1,0:T(8,128)(2,1)S(1)}, u32[]{:S(2)}, u32[]{:S(2)}) collective-permute-start(bf16[512,128]{1,0:T(8,128)(2,1)S(1)} %get-tuple-element.64), channel_id=1, source_target_pairs={{0,8},{4,36},{8,16},{12,44},{16,24},{20,52},{24,0},{28,60},{32,40}... | collective-permute-start | bytes 393224 | tf_op jit(solution)/shard_map/ppermute | solution.py:357
  9.4 0.0 copy-start.1
  9.4 1.0 %copy-done.1 = bf16[128,2048]{1,0:T(8,128)(2,1)S(1)} copy-done((bf16[128,2048]{1,0:T(8,128)(2,1)S(1)}, bf16[128,2048]{1,0:T(8,128)(2,1)}, u32[]{:S(2)}) %copy-start.1) | copy-done | bytes 524312
  10.4 0.0 copy-start.2
  10.4 0.1 heads.3
  10.6 0.8 %collective-permute-done.6 = bf16[512,128]{1,0:T(8,128)(2,1)S(1)} collective-permute-done((bf16[512,128]{1,0:T(8,128)(2,1)S(1)}, bf16[512,128]{1,0:T(8,128)(2,1)S(1)}, u32[]{:S(2)}, u32[]{:S(2)}) %collective-permute-start.6) | collective-permute-done | bytes 131104 | tf_op jit(solution)/shard_map/ppermute | solution.py:357
  11.3 6.0 %collective-permute-start.1 = (bf16[1024,128]{1,0:T(8,128)(2,1)S(1)}, bf16[1024,128]{1,0:T(8,128)(2,1)S(1)}, u32[]{:S(2)}, u32[]{:S(2)}) collective-permute-start(bf16[1024,128]{1,0:T(8,128)(2,1)S(1)} %get-tuple-element.37), channel_id=1, source_target_pairs={{0,4},{4,0},{8,12},{12,8},{16,20},{20,16},{24,28},{28,24},{32,36},... | collective-permute-start | bytes 786440 | tf_op jit(solution)/shard_map/ppermute | solution.py:370
  17.4 0.0 collective-permute-done.7
  17.4 0.0 collective-permute-done.8
  17.5 0.1 collective-permute-start.10
  17.6 1.5 %collective-permute-start.9 = (bf16[2048,128]{1,0:T(8,128)(2,1)S(1)}, bf16[2048,128]{1,0:T(8,128)(2,1)S(1)}, u32[]{:S(2)}, u32[]{:S(2)}) collective-permute-start(bf16[2048,128]{1,0:T(8,128)(2,1)S(1)} %constant_dynamic-update-slice_fusion.2.refs_0_), channel_id=1, source_target_pairs={{0,32},{4,12},{8,40},{12,20},{16,48},{20,28},{24,56},{28,4},{32,64... | collective-permute-start | bytes 1572872 | tf_op jit(solution)/shard_map/ppermute | solution.py:362
  19.0 0.0 collective-permute-done.2.refs_1_
  19.0 1.3 %collective-permute-start.3 = (bf16[32,8192]{1,0:T(8,128)(2,1)S(1)}, bf16[32,8192]{1,0:T(8,128)(2,1)S(1)}, u32[]{:S(2)}, u32[]{:S(2)}) collective-permute-start(bf16[32,8192]{1,0:T(8,128)(2,1)S(1)} %collective-permute-done.2.refs_1_), channel_id=1, source_target_pairs={{0,1},{1,2},{2,3},{3,0},{4,7},{5,4},{6,5},{7,6},{8,9},{9,10},{10,1... | collective-permute-start | bytes 1572872 | tf_op jit(solution)/shard_map/ppermute | solution.py:384
  20.3 0.0 collective-permute-done.4.refs_2_
  20.3 0.0 slice-done
  20.3 0.0 slice-done.1
  20.3 0.0 copy-done.2
  20.3 1.5 %project_near.1 = (f32[96,256]{1,0:T(8,128)S(1)}, f32[96,256]{1,0:T(8,128)S(1)}) custom-call(bf16[32,8192]{1,0:T(8,128)(2,1)S(1)} %copy-done.2, bf16[32,8192]{1,0:T(8,128)(2,1)S(1)} %collective-permute-done.2.refs_1_, bf16[32,8192]{1,0:T(8,128)(2,1)S(1)} %collective-permute-done.4.refs_2_, bf16[2,8192,256]{2,1,0:T(8,128)(2,1)S(1)} %bitcast.1), custom_call_target="tpu_custom_call" | custom-call | flops 22000001024 | bytes 70000000 | tf_op jit(solution)/shard_map/project_near/pallas_call | solution.py:121
  21.8 0.0 copy-start
  21.8 3.3 %collective-permute-start.11 = (bf16[2048,128]{1,0:T(8,128)(2,1)S(1)}, bf16[2048,128]{1,0:T(8,128)(2,1)S(1)}, u32[]{:S(2)}, u32[]{:S(2)}) collective-permute-start(bf16[2048,128]{1,0:T(8,128)(2,1)S(1)} %constant_dynamic-update-slice_fusion.2.refs_0_), channel_id=1, source_target_pairs={{0,64},{4,20},{8,72},{12,28},{16,80},{20,4},{24,88},{28,12},{32,96... | collective-permute-start | bytes 1572872 | tf_op jit(solution)/shard_map/ppermute | solution.py:366
  25.1 0.3 fusion
  25.4 0.1 pad_maximum_fusion.1
  25.5 0.0 collective-permute-done.1.received
  25.5 1.8 %collective-permute-done.3.piece = bf16[32,8192]{1,0:T(8,128)(2,1)S(1)} collective-permute-done((bf16[32,8192]{1,0:T(8,128)(2,1)S(1)}, bf16[32,8192]{1,0:T(8,128)(2,1)S(1)}, u32[]{:S(2)}, u32[]{:S(2)}) %collective-permute-start.3) | collective-permute-done | bytes 524320 | tf_op jit(solution)/shard_map/ppermute | solution.py:384
  27.3 2.2 %project_far.1 = (bf16[128,256]{1,0:T(8,128)(2,1)}, bf16[128,256]{1,0:T(8,128)(2,1)}, bf16[256,128]{1,0:T(8,128)(2,1)S(1)}, bf16[256,128]{1,0:T(8,128)(2,1)S(1)}) custom-call(bf16[32,8192]{1,0:T(8,128)(2,1)S(1)} %collective-permute-done.3.piece, f32[96,256]{1,0:T(8,128)S(1)} %get-tuple-element.41.near_keys, f32[96,256]{1,0:T(8,128)S(1)} %get-tuple-element.42.near_values, ...), custom_call_target="tpu_custom_call" | custom-call | flops 110000000 | bytes 350000 | tf_op jit(solution)/shard_map/project_far/pallas_call | solution.py:164
  29.6 3.8 %collective-permute-start.5 = (bf16[256,128]{1,0:T(8,128)(2,1)S(1)}, bf16[256,128]{1,0:T(8,128)(2,1)S(1)}, u32[]{:S(2)}, u32[]{:S(2)}) collective-permute-start(bf16[256,128]{1,0:T(8,128)(2,1)S(1)} %get-tuple-element.44), channel_id=1, source_target_pairs={{0,4},{4,0},{8,12},{12,8},{16,20},{20,16},{24,28},{28,24},{32,36},... | collective-permute-start | bytes 196616 | tf_op jit(solution)/shard_map/ppermute | solution.py:370
  33.4 0.9 %collective-permute-done.5 = bf16[256,128]{1,0:T(8,128)(2,1)S(1)} collective-permute-done((bf16[256,128]{1,0:T(8,128)(2,1)S(1)}, bf16[256,128]{1,0:T(8,128)(2,1)S(1)}, u32[]{:S(2)}, u32[]{:S(2)}) %collective-permute-start.5) | collective-permute-done | bytes 65568 | tf_op jit(solution)/shard_map/ppermute | solution.py:370
  34.3 0.0 collective-permute-done.10.refs_2_
  34.3 0.0 collective-permute-done.9.refs_1_
  34.4 0.1 collective-permute-start.12
  34.4 1.0 %collective-permute-start.14 = (bf16[512,128]{1,0:T(8,128)(2,1)S(1)}, bf16[512,128]{1,0:T(8,128)(2,1)S(1)}, u32[]{:S(2)}, u32[]{:S(2)}) collective-permute-start(bf16[512,128]{1,0:T(8,128)(2,1)S(1)} %pad_maximum_fusion), channel_id=1, source_target_pairs={{0,16},{4,68},{8,24},{12,76},{16,0},{20,84},{24,8},{28,92},{32,48}... | collective-permute-start | bytes 393224 | tf_op jit(solution)/shard_map/ppermute | solution.py:357
  35.5 0.4 collective-permute-start.13
  35.9 0.0 collective-permute-done.11.refs_3_
  35.9 0.0 copy-done
  35.9 6.0 %attend_cache.1 = (f32[2048,128]{1,0:T(8,128)S(1)}, f32[2048,128]{1,0:T(8,128)S(1)}, f32[2048,128]{1,0:T(8,128)S(1)}) custom-call(s32[32]{0:T(128)S(1)} %copy-done, bf16[1024,128]{1,0:T(8,128)(2,1)S(1)} %get-tuple-element.46.own_queries, bf16[1024,128]{1,0:T(8,128)(2,1)S(1)} %collective-permute-done.1.received, ...), custom_call_target="tpu_custom_call" | custom-call | flops 110000000 | bytes 350000 | tf_op jit(solution)/shard_map/attend_cache/pallas_call | solution.py:234
  41.9 0.0 collective-permute-done.12
  42.0 0.0 collective-permute-done.13
  42.0 0.0 collective-permute-done.14
  42.1 1.5 %collective-permute-start.17 = (bf16[2048,128]{1,0:T(8,128)(2,1)S(1)}, bf16[2048,128]{1,0:T(8,128)(2,1)S(1)}, u32[]{:S(2)}, u32[]{:S(2)}) collective-permute-start(bf16[2048,128]{1,0:T(8,128)(2,1)S(1)} %constant_dynamic-update-slice_fusion.7.refs_0_), channel_id=1, source_target_pairs={{0,96},{4,28},{8,104},{12,4},{16,112},{20,12},{24,120},{28,20},{32... | collective-permute-start | bytes 1572872 | tf_op jit(solution)/shard_map/ppermute | solution.py:362
  43.6 0.0 collective-permute-start.16
  43.6 4.0 %attend_new.2 = (f32[2048,128]{1,0:T(8,128)S(1)}, f32[2048,128]{1,0:T(8,128)S(1)}, f32[2048,128]{1,0:T(8,128)S(1)}) custom-call(bf16[1024,128]{1,0:T(8,128)(2,1)S(1)} %get-tuple-element.46.own_queries, bf16[1024,128]{1,0:T(8,128)(2,1)S(1)} %collective-permute-done.1.received, bf16[2048,128]{1,0:T(8,128)(2,1)S(1)} %constant_dynamic-update-slice_fusion.7.refs_0_, ...), custom_call_target="tpu_custom_call" | custom-call | flops 110000000 | bytes 350000 | tf_op jit(solution)/shard_map/attend_new/pallas_call | solution.py:334
  47.6 1.4 %collective-permute-start.15 = (bf16[2048,128]{1,0:T(8,128)(2,1)S(1)}, bf16[2048,128]{1,0:T(8,128)(2,1)S(1)}, u32[]{:S(2)}, u32[]{:S(2)}) collective-permute-start(bf16[2048,128]{1,0:T(8,128)(2,1)S(1)} %constant_dynamic-update-slice_fusion.7.refs_0_), channel_id=1, source_target_pairs={{0,64},{4,20},{8,72},{12,28},{16,80},{20,4},{24,88},{28,12},{32,96... | collective-permute-start | bytes 1572872 | tf_op jit(solution)/shard_map/ppermute | solution.py:366
  49.0 1.4 %collective-permute-done.17.refs_1_ = bf16[2048,128]{1,0:T(8,128)(2,1)S(1)} collective-permute-done((bf16[2048,128]{1,0:T(8,128)(2,1)S(1)}, bf16[2048,128]{1,0:T(8,128)(2,1)S(1)}, u32[]{:S(2)}, u32[]{:S(2)}) %collective-permute-start.17) | collective-permute-done | bytes 524320 | tf_op jit(solution)/shard_map/ppermute | solution.py:362
  50.4 8.3 %collective-permute-done.16.refs_0_ = bf16[2048,128]{1,0:T(8,128)(2,1)S(1)} collective-permute-done((bf16[2048,128]{1,0:T(8,128)(2,1)S(1)}, bf16[2048,128]{1,0:T(8,128)(2,1)S(1)}, u32[]{:S(2)}, u32[]{:S(2)}) %collective-permute-start.16) | collective-permute-done | bytes 524320 | tf_op jit(solution)/shard_map/ppermute | solution.py:362
  58.7 5.1 %attend_new.3 = (f32[2048,128]{1,0:T(8,128)S(1)}, f32[2048,128]{1,0:T(8,128)S(1)}, f32[2048,128]{1,0:T(8,128)S(1)}) custom-call(bf16[1024,128]{1,0:T(8,128)(2,1)S(1)} %get-tuple-element.46.own_queries, bf16[1024,128]{1,0:T(8,128)(2,1)S(1)} %collective-permute-done.1.received, bf16[2048,128]{1,0:T(8,128)(2,1)S(1)} %collective-permute-done.16.refs_0_, ...), custom_call_target="tpu_custom_call" | custom-call | flops 110000000 | bytes 350000 | tf_op jit(solution)/shard_map/attend_new/pallas_call | solution.py:334
  63.8 0.0 collective-permute-done.15.refs_0_
  63.8 3.3 %attend_new_last.1 = (bf16[128,1024]{1,0:T(8,128)(2,1)S(1)}, bf16[128,1024]{1,0:T(8,128)(2,1)S(1)}) custom-call(bf16[1024,128]{1,0:T(8,128)(2,1)S(1)} %get-tuple-element.46.own_queries, bf16[1024,128]{1,0:T(8,128)(2,1)S(1)} %collective-permute-done.1.received, bf16[2048,128]{1,0:T(8,128)(2,1)S(1)} %collective-permute-done.15.refs_0_, ...), custom_call_target="tpu_custom_call" | custom-call | flops 110000000 | bytes 350000 | tf_op jit(solution)/shard_map/attend_new_last/pallas_call | solution.py:334
  67.1 3.5 %collective-permute-start.18 = (bf16[128,1024]{1,0:T(8,128)(2,1)S(1)}, bf16[128,1024]{1,0:T(8,128)(2,1)S(1)}, u32[]{:S(2)}, u32[]{:S(2)}) collective-permute-start(bf16[128,1024]{1,0:T(8,128)(2,1)S(1)} %get-tuple-element.60), channel_id=1, source_target_pairs={{0,4},{4,0},{8,12},{12,8},{16,20},{20,16},{24,28},{28,24},{32,36},... | collective-permute-start | bytes 786440 | tf_op jit(solution)/shard_map/ppermute | solution.py:370
  70.7 1.2 %collective-permute-done.18 = bf16[128,1024]{1,0:T(8,128)(2,1)S(1)} collective-permute-done((bf16[128,1024]{1,0:T(8,128)(2,1)S(1)}, bf16[128,1024]{1,0:T(8,128)(2,1)S(1)}, u32[]{:S(2)}, u32[]{:S(2)}) %collective-permute-start.18) | collective-permute-done | bytes 262176 | tf_op jit(solution)/shard_map/ppermute | solution.py:370
  71.8 0.9 %maximum_select_fusion = bf16[128,2048]{1,0:T(8,128)(2,1)} fusion(bf16[128,1024]{1,0:T(8,128)(2,1)S(1)} %collective-permute-done.18, bf16[128,1024]{1,0:T(8,128)(2,1)S(1)} %get-tuple-element.59, pred[]{:T(512)S(6)} %eq.3), kind=kLoop, calls=%fused_computation | loop fusion | flops 2359296 | bytes 1048577 | tf_op jit(solution)/shard_map/jit(_where)/select_n | solution.py:412
  (14 shorter events, 0.2 us)
Async XLA Ops:
  0.6 0.8 %copy-start.3 = (bf16[128,256]{1,0:T(8,128)(2,1)S(1)}, bf16[128,256]{1,0:T(8,128)(2,1)}, u32[]{:S(2)}) copy-start(bf16[128,256]{1,0:T(8,128)(2,1)} %refs_0_.2) | copy-start | bytes 196612
  1.5 0.8 %copy-start.4 = (bf16[128,256]{1,0:T(8,128)(2,1)S(1)}, bf16[128,256]{1,0:T(8,128)(2,1)}, u32[]{:S(2)}) copy-start(bf16[128,256]{1,0:T(8,128)(2,1)} %refs_1_.1) | copy-start | bytes 196612
  2.3 3.3 %collective-permute-start = (bf16[256,128]{1,0:T(8,128)(2,1)S(1)}, bf16[256,128]{1,0:T(8,128)(2,1)S(1)}, u32[]{:S(2)}, u32[]{:S(2)}) collective-permute-start(bf16[256,128]{1,0:T(8,128)(2,1)S(1)} %get-tuple-element.34), channel_id=1, source_target_pairs={{0,4},{4,0},{8,12},{12,8},{16,20},{20,16},{24,28},{28,24},{32,36},... | collective-permute-start | bytes 196616 | tf_op jit(solution)/shard_map/ppermute | solution.py:370
  3.1 15.9 %collective-permute-start.2 = (bf16[32,8192]{1,0:T(8,128)(2,1)}, bf16[32,8192]{1,0:T(8,128)(2,1)S(1)}, u32[]{:S(2)}, u32[]{:S(2)}) collective-permute-start(bf16[32,8192]{1,0:T(8,128)(2,1)} %refs_0_.4), channel_id=1, source_target_pairs={{0,1},{1,2},{2,3},{3,0},{4,7},{5,4},{6,5},{7,6},{8,9},{9,10},{10,1... | collective-permute-start | bytes 1572872 | tf_op jit(solution)/shard_map/ppermute | solution.py:377
  5.6 14.7 %collective-permute-start.4 = (bf16[32,8192]{1,0:T(8,128)(2,1)}, bf16[32,8192]{1,0:T(8,128)(2,1)S(1)}, u32[]{:S(2)}, u32[]{:S(2)}) collective-permute-start(bf16[32,8192]{1,0:T(8,128)(2,1)} %refs_0_.4), channel_id=1, source_target_pairs={{0,3},{1,0},{2,1},{3,2},{4,5},{5,6},{6,7},{7,4},{8,11},{9,8},{10,9... | collective-permute-start | bytes 1572872 | tf_op jit(solution)/shard_map/ppermute | solution.py:379
  5.7 14.6 %slice-start = ((s8[8388608]{0:T(1024)(128)(4,1)}), s8[4194304]{0:T(1024)(128)(4,1)S(1)}, s32[]{:S(2)}) async-start(s8[8388608]{0:T(1024)(128)(4,1)} %bitcast), calls=%async_computation | async-start | bytes 8388608
  5.7 14.6 %slice-start.1 = ((s8[8388608]{0:T(1024)(128)(4,1)}), s8[4194304]{0:T(1024)(128)(4,1)S(1)}, s32[]{:S(2)}) async-start(s8[8388608]{0:T(1024)(128)(4,1)} %bitcast), calls=%async_computation.1 | async-start | bytes 8388608
  5.7 11.7 %collective-permute-start.8 = (bf16[512,128]{1,0:T(8,128)(2,1)S(1)}, bf16[512,128]{1,0:T(8,128)(2,1)S(1)}, u32[]{:S(2)}, u32[]{:S(2)}) collective-permute-start(bf16[512,128]{1,0:T(8,128)(2,1)S(1)} %get-tuple-element.64), channel_id=1, source_target_pairs={{0,16},{4,68},{8,24},{12,76},{16,0},{20,84},{24,8},{28,92},{32,48}... | collective-permute-start | bytes 393224 | tf_op jit(solution)/shard_map/ppermute | solution.py:357
  6.7 10.7 %collective-permute-start.7 = (bf16[512,128]{1,0:T(8,128)(2,1)S(1)}, bf16[512,128]{1,0:T(8,128)(2,1)S(1)}, u32[]{:S(2)}, u32[]{:S(2)}) collective-permute-start(bf16[512,128]{1,0:T(8,128)(2,1)S(1)} %get-tuple-element.64), channel_id=1, source_target_pairs={{0,24},{4,100},{8,0},{12,108},{16,8},{20,116},{24,16},{28,124},{32... | collective-permute-start | bytes 393224 | tf_op jit(solution)/shard_map/ppermute | solution.py:357
  6.7 4.6 %collective-permute-start.6 = (bf16[512,128]{1,0:T(8,128)(2,1)S(1)}, bf16[512,128]{1,0:T(8,128)(2,1)S(1)}, u32[]{:S(2)}, u32[]{:S(2)}) collective-permute-start(bf16[512,128]{1,0:T(8,128)(2,1)S(1)} %get-tuple-element.64), channel_id=1, source_target_pairs={{0,8},{4,36},{8,16},{12,44},{16,24},{20,52},{24,0},{28,60},{32,40}... | collective-permute-start | bytes 393224 | tf_op jit(solution)/shard_map/ppermute | solution.py:357
  9.4 1.0 %copy-start.1 = (bf16[128,2048]{1,0:T(8,128)(2,1)S(1)}, bf16[128,2048]{1,0:T(8,128)(2,1)}, u32[]{:S(2)}) copy-start(bf16[128,2048]{1,0:T(8,128)(2,1)} %refs_0_.3) | copy-start | bytes 1572868
  10.4 9.8 %copy-start.2 = (bf16[32,8192]{1,0:T(8,128)(2,1)S(1)}, bf16[32,8192]{1,0:T(8,128)(2,1)}, u32[]{:S(2)}) copy-start(bf16[32,8192]{1,0:T(8,128)(2,1)} %refs_0_.4) | copy-start | bytes 1572868
  11.3 14.2 %collective-permute-start.1 = (bf16[1024,128]{1,0:T(8,128)(2,1)S(1)}, bf16[1024,128]{1,0:T(8,128)(2,1)S(1)}, u32[]{:S(2)}, u32[]{:S(2)}) collective-permute-start(bf16[1024,128]{1,0:T(8,128)(2,1)S(1)} %get-tuple-element.37), channel_id=1, source_target_pairs={{0,4},{4,0},{8,12},{12,8},{16,20},{20,16},{24,28},{28,24},{32,36},... | collective-permute-start | bytes 786440 | tf_op jit(solution)/shard_map/ppermute | solution.py:370
  17.5 16.9 %collective-permute-start.10 = (bf16[2048,128]{1,0:T(8,128)(2,1)S(1)}, bf16[2048,128]{1,0:T(8,128)(2,1)S(1)}, u32[]{:S(2)}, u32[]{:S(2)}) collective-permute-start(bf16[2048,128]{1,0:T(8,128)(2,1)S(1)} %constant_dynamic-update-slice_fusion.2.refs_0_), channel_id=1, source_target_pairs={{0,96},{4,28},{8,104},{12,4},{16,112},{20,12},{24,120},{28,20},{32... | collective-permute-start | bytes 1572872 | tf_op jit(solution)/shard_map/ppermute | solution.py:362
  17.6 16.8 %collective-permute-start.9 = (bf16[2048,128]{1,0:T(8,128)(2,1)S(1)}, bf16[2048,128]{1,0:T(8,128)(2,1)S(1)}, u32[]{:S(2)}, u32[]{:S(2)}) collective-permute-start(bf16[2048,128]{1,0:T(8,128)(2,1)S(1)} %constant_dynamic-update-slice_fusion.2.refs_0_), channel_id=1, source_target_pairs={{0,32},{4,12},{8,40},{12,20},{16,48},{20,28},{24,56},{28,4},{32,64... | collective-permute-start | bytes 1572872 | tf_op jit(solution)/shard_map/ppermute | solution.py:362
  19.0 8.3 %collective-permute-start.3 = (bf16[32,8192]{1,0:T(8,128)(2,1)S(1)}, bf16[32,8192]{1,0:T(8,128)(2,1)S(1)}, u32[]{:S(2)}, u32[]{:S(2)}) collective-permute-start(bf16[32,8192]{1,0:T(8,128)(2,1)S(1)} %collective-permute-done.2.refs_1_), channel_id=1, source_target_pairs={{0,1},{1,2},{2,3},{3,0},{4,7},{5,4},{6,5},{7,6},{8,9},{9,10},{10,1... | collective-permute-start | bytes 1572872 | tf_op jit(solution)/shard_map/ppermute | solution.py:384
  21.8 14.1 %copy-start = (s32[32]{0:T(128)S(1)}, s32[32]{0:T(128)}, u32[]{:S(2)}) copy-start(s32[32]{0:T(128)} %kv_blocks.1) | copy-start | bytes 388
  21.8 14.1 %collective-permute-start.11 = (bf16[2048,128]{1,0:T(8,128)(2,1)S(1)}, bf16[2048,128]{1,0:T(8,128)(2,1)S(1)}, u32[]{:S(2)}, u32[]{:S(2)}) collective-permute-start(bf16[2048,128]{1,0:T(8,128)(2,1)S(1)} %constant_dynamic-update-slice_fusion.2.refs_0_), channel_id=1, source_target_pairs={{0,64},{4,20},{8,72},{12,28},{16,80},{20,4},{24,88},{28,12},{32,96... | collective-permute-start | bytes 1572872 | tf_op jit(solution)/shard_map/ppermute | solution.py:366
  29.6 4.7 %collective-permute-start.5 = (bf16[256,128]{1,0:T(8,128)(2,1)S(1)}, bf16[256,128]{1,0:T(8,128)(2,1)S(1)}, u32[]{:S(2)}, u32[]{:S(2)}) collective-permute-start(bf16[256,128]{1,0:T(8,128)(2,1)S(1)} %get-tuple-element.44), channel_id=1, source_target_pairs={{0,4},{4,0},{8,12},{12,8},{16,20},{20,16},{24,28},{28,24},{32,36},... | collective-permute-start | bytes 196616 | tf_op jit(solution)/shard_map/ppermute | solution.py:370
  34.4 7.6 %collective-permute-start.12 = (bf16[512,128]{1,0:T(8,128)(2,1)S(1)}, bf16[512,128]{1,0:T(8,128)(2,1)S(1)}, u32[]{:S(2)}, u32[]{:S(2)}) collective-permute-start(bf16[512,128]{1,0:T(8,128)(2,1)S(1)} %pad_maximum_fusion), channel_id=1, source_target_pairs={{0,8},{4,36},{8,16},{12,44},{16,24},{20,52},{24,0},{28,60},{32,40}... | collective-permute-start | bytes 393224 | tf_op jit(solution)/shard_map/ppermute | solution.py:357
  34.4 7.6 %collective-permute-start.14 = (bf16[512,128]{1,0:T(8,128)(2,1)S(1)}, bf16[512,128]{1,0:T(8,128)(2,1)S(1)}, u32[]{:S(2)}, u32[]{:S(2)}) collective-permute-start(bf16[512,128]{1,0:T(8,128)(2,1)S(1)} %pad_maximum_fusion), channel_id=1, source_target_pairs={{0,16},{4,68},{8,24},{12,76},{16,0},{20,84},{24,8},{28,92},{32,48}... | collective-permute-start | bytes 393224 | tf_op jit(solution)/shard_map/ppermute | solution.py:357
  35.5 6.5 %collective-permute-start.13 = (bf16[512,128]{1,0:T(8,128)(2,1)S(1)}, bf16[512,128]{1,0:T(8,128)(2,1)S(1)}, u32[]{:S(2)}, u32[]{:S(2)}) collective-permute-start(bf16[512,128]{1,0:T(8,128)(2,1)S(1)} %pad_maximum_fusion), channel_id=1, source_target_pairs={{0,24},{4,100},{8,0},{12,108},{16,8},{20,116},{24,16},{28,124},{32... | collective-permute-start | bytes 393224 | tf_op jit(solution)/shard_map/ppermute | solution.py:357
  42.1 8.4 %collective-permute-start.17 = (bf16[2048,128]{1,0:T(8,128)(2,1)S(1)}, bf16[2048,128]{1,0:T(8,128)(2,1)S(1)}, u32[]{:S(2)}, u32[]{:S(2)}) collective-permute-start(bf16[2048,128]{1,0:T(8,128)(2,1)S(1)} %constant_dynamic-update-slice_fusion.7.refs_0_), channel_id=1, source_target_pairs={{0,96},{4,28},{8,104},{12,4},{16,112},{20,12},{24,120},{28,20},{32... | collective-permute-start | bytes 1572872 | tf_op jit(solution)/shard_map/ppermute | solution.py:362
  43.6 15.2 %collective-permute-start.16 = (bf16[2048,128]{1,0:T(8,128)(2,1)S(1)}, bf16[2048,128]{1,0:T(8,128)(2,1)S(1)}, u32[]{:S(2)}, u32[]{:S(2)}) collective-permute-start(bf16[2048,128]{1,0:T(8,128)(2,1)S(1)} %constant_dynamic-update-slice_fusion.7.refs_0_), channel_id=1, source_target_pairs={{0,32},{4,12},{8,40},{12,20},{16,48},{20,28},{24,56},{28,4},{32,64... | collective-permute-start | bytes 1572872 | tf_op jit(solution)/shard_map/ppermute | solution.py:362
  47.6 16.2 %collective-permute-start.15 = (bf16[2048,128]{1,0:T(8,128)(2,1)S(1)}, bf16[2048,128]{1,0:T(8,128)(2,1)S(1)}, u32[]{:S(2)}, u32[]{:S(2)}) collective-permute-start(bf16[2048,128]{1,0:T(8,128)(2,1)S(1)} %constant_dynamic-update-slice_fusion.7.refs_0_), channel_id=1, source_target_pairs={{0,64},{4,20},{8,72},{12,28},{16,80},{20,4},{24,88},{28,12},{32,96... | collective-permute-start | bytes 1572872 | tf_op jit(solution)/shard_map/ppermute | solution.py:366
  67.1 4.7 %collective-permute-start.18 = (bf16[128,1024]{1,0:T(8,128)(2,1)S(1)}, bf16[128,1024]{1,0:T(8,128)(2,1)S(1)}, u32[]{:S(2)}, u32[]{:S(2)}) collective-permute-start(bf16[128,1024]{1,0:T(8,128)(2,1)S(1)} %get-tuple-element.60), channel_id=1, source_target_pairs={{0,4},{4,0},{8,12},{12,8},{16,20},{20,16},{24,28},{28,24},{32,36},... | collective-permute-start | bytes 786440 | tf_op jit(solution)/shard_map/ppermute | solution.py:370

commit v4 on v3

--- a/solution.py
+++ b/solution.py
@@ -376,10 +376,10 @@
     both = ("group", "tensor")
     ahead = lax.ppermute(hidden_rows, both, ring(1))
     mine, give = heads(HEAD_DIM, 0.1, cache_keys, cache_values)
-    behind = lax.ppermute(after(hidden_rows, mine), both, ring(3))
     block = jnp.concatenate([mine, swapped(give)], 0)
+    behind = lax.ppermute(after(hidden_rows, block), both, ring(3))
     joined = first_phase(block)
-    own_queries, give_queries = heads(SHARE * HEAD_DIM, 20, after(queries, block))
+    own_queries, give_queries = heads(SHARE * HEAD_DIM, 5, after(queries, block))
     received = swapped(give_queries)
     far = lax.ppermute(after(ahead, own_queries), both, ring(1))
     cache = second_phase(joined)
@@ -405,7 +405,7 @@
     joined = first_phase(block, states[0])
     new = second_phase(joined)
     states = attend_new(own_queries, received, (0,), new[:1], states, False)
-    new.append(last_phase(joined, states[0]))
+    new.append(last_phase(joined, states[0], new[1]))
     states = attend_new(own_queries, received, (1, 2), new[1:3], states, False)
     here, there = attend_new(own_queries, received, (3,), new[3:], states, True)
     other = swapped(there)

time: 73 us -> 69.7 us (0.955)
  waiting for transfers between devices: 14.4 us -> 11.3 us
  starting transfers between devices: 30.9 us -> 30.1 us
    ppermute x4, waiting for transfers between devices: 9.75 us -> 2.84 us  [second_phase(): lax.ppermute(joined, 'group', along(1, d))]
    ppermute x2, waiting for transfers between devices: 0.01 us -> 4.76 us  [last_phase(): return lax.ppermute(after(joined, *others), 'group', along(1, 2))]
    ppermute x4, starting transfers between devices: 14.1 us -> 12.6 us  [swapped(): return lax.ppermute(block, 'group', swap_cores())]
    ppermute x2, starting transfers between devices: 4.69 us -> 3.45 us  [last_phase(): return lax.ppermute(after(joined, *others), 'group', along(1, 2))]
    ppermute x4, starting transfers between devices: 3.07 us -> 4.27 us  [second_phase(): lax.ppermute(joined, 'group', along(1, d))]
    ppermute x1, waiting for transfers between devices: 1.82 us -> 0.85 us  [shards(): far = lax.ppermute(after(ahead, own_queries), both, ring(1))]
    ppermute x1, starting transfers between devices: 1.27 us -> 2.1 us  [shards(): far = lax.ppermute(after(ahead, own_queries), both, ring(1))]
  transfers between devices with their start and end apart: 19 -> 19, of which waited for: 6 -> 6; matrix products, arithmetic and copies ran while one was open for 1% -> 1% of each run, Pallas kernels for 26% -> 27%
where the time goes in v4:
time: 69.7 us; the launch traced here: 68.8 us
  starting transfers between devices  30.1 us (43%)
  Pallas kernels  22.2 us (32%)
  waiting for transfers between devices  11.3 us (16%)
  local copies, waits for them, and re-layouts  2.9 us (4%)
  other arithmetic  1.35 us (2%)
  between operations  0.91 us (1%)
    ppermute x4, starting transfers between devices, swapped(): return lax.ppermute(block, 'group', swap_cores())  12.6 us
    pallas_call x3, Pallas kernels, attend_new(): pl.pallas_call(functools.partial(new_kernel, which, last), out_shape=(out...  12.3 us
    pallas_call x1, Pallas kernels, attend_cache(): pl.pallas_call(functools.partial(cache_kernel, live_keys), out_shape=(STA...  6.02 us
    ppermute x6, starting transfers between devices, first_phase(): sent = [lax.ppermute(block, 'group', along(0, d)) for d in (1, 3, 2)]  5.25 us
    ppermute x2, waiting for transfers between devices, last_phase(): return lax.ppermute(after(joined, *others), 'group', along(1, 2))  4.76 us
    ppermute x4, starting transfers between devices, second_phase(): lax.ppermute(joined, 'group', along(1, d))  4.27 us
    ppermute x2, starting transfers between devices, last_phase(): return lax.ppermute(after(joined, *others), 'group', along(1, 2))  3.45 us
    unnamed x21, local copies, waits for them, and re-layouts  2.86 us
  transfers between devices with their start and end apart: 19, of which 6 were waited for; matrix products, arithmetic and copies ran while one was open for 1% of the time, Pallas kernels for 27%

profile of v4, /device:TPU:25, one launch (start us, length us, event | category | flops | bytes accessed | tf_op | source)
XLA Modules:
  0.0 68.8 jit_solution(6901577053527602948)
XLA Ops:
  0.6 0.0 copy-start.3
  0.6 0.8 %copy-done.3 = bf16[128,256]{1,0:T(8,128)(2,1)S(1)} copy-done((bf16[128,256]{1,0:T(8,128)(2,1)S(1)}, bf16[128,256]{1,0:T(8,128)(2,1)}, u32[]{:S(2)}) %copy-start.3) | copy-done | bytes 65560
  1.5 0.0 copy-start.4
  1.5 0.8 %copy-done.4 = bf16[128,256]{1,0:T(8,128)(2,1)S(1)} copy-done((bf16[128,256]{1,0:T(8,128)(2,1)S(1)}, bf16[128,256]{1,0:T(8,128)(2,1)}, u32[]{:S(2)}) %copy-start.4) | copy-done | bytes 65560
  2.3 0.8 %collective-permute-start = (bf16[256,128]{1,0:T(8,128)(2,1)S(1)}, bf16[256,128]{1,0:T(8,128)(2,1)S(1)}, u32[]{:S(2)}, u32[]{:S(2)}) collective-permute-start(bf16[256,128]{1,0:T(8,128)(2,1)S(1)} %get-tuple-element.34), channel_id=1, source_target_pairs={{0,4},{4,0},{8,12},{12,8},{16,20},{20,16},{24,28},{28,24},{32,36},... | collective-permute-start | bytes 196616 | tf_op jit(solution)/shard_map/ppermute | solution.py:370
  3.1 2.5 %collective-permute-start.2 = (bf16[32,8192]{1,0:T(8,128)(2,1)}, bf16[32,8192]{1,0:T(8,128)(2,1)S(1)}, u32[]{:S(2)}, u32[]{:S(2)}) collective-permute-start(bf16[32,8192]{1,0:T(8,128)(2,1)} %refs_0_.4), channel_id=1, source_target_pairs={{0,1},{1,2},{2,3},{3,0},{4,7},{5,4},{6,5},{7,6},{8,9},{9,10},{10,1... | collective-permute-start | bytes 1572872 | tf_op jit(solution)/shard_map/ppermute | solution.py:377
  5.6 0.0 collective-permute-done
  5.7 0.0 slice-start
  5.7 0.0 slice-start.1
  5.7 1.0 %collective-permute-start.8 = (bf16[512,128]{1,0:T(8,128)(2,1)S(1)}, bf16[512,128]{1,0:T(8,128)(2,1)S(1)}, u32[]{:S(2)}, u32[]{:S(2)}) collective-permute-start(bf16[512,128]{1,0:T(8,128)(2,1)S(1)} %get-tuple-element.64), channel_id=1, source_target_pairs={{0,16},{4,68},{8,24},{12,76},{16,0},{20,84},{24,8},{28,92},{32,48}... | collective-permute-start | bytes 393224 | tf_op jit(solution)/shard_map/ppermute | solution.py:357
  6.7 0.0 collective-permute-start.7
  6.7 2.7 %collective-permute-start.6 = (bf16[512,128]{1,0:T(8,128)(2,1)S(1)}, bf16[512,128]{1,0:T(8,128)(2,1)S(1)}, u32[]{:S(2)}, u32[]{:S(2)}) collective-permute-start(bf16[512,128]{1,0:T(8,128)(2,1)S(1)} %get-tuple-element.64), channel_id=1, source_target_pairs={{0,8},{4,36},{8,16},{12,44},{16,24},{20,52},{24,0},{28,60},{32,40}... | collective-permute-start | bytes 393224 | tf_op jit(solution)/shard_map/ppermute | solution.py:357
  9.4 0.0 collective-permute-start.4
  9.4 0.0 copy-start.1
  9.4 1.0 %copy-done.1 = bf16[128,2048]{1,0:T(8,128)(2,1)S(1)} copy-done((bf16[128,2048]{1,0:T(8,128)(2,1)S(1)}, bf16[128,2048]{1,0:T(8,128)(2,1)}, u32[]{:S(2)}) %copy-start.1) | copy-done | bytes 524312
  10.4 0.0 copy-start.2
  10.4 0.1 heads.3
  10.6 0.8 %collective-permute-done.6 = bf16[512,128]{1,0:T(8,128)(2,1)S(1)} collective-permute-done((bf16[512,128]{1,0:T(8,128)(2,1)S(1)}, bf16[512,128]{1,0:T(8,128)(2,1)S(1)}, u32[]{:S(2)}, u32[]{:S(2)}) %collective-permute-start.6) | collective-permute-done | bytes 131104 | tf_op jit(solution)/shard_map/ppermute | solution.py:357
  11.3 4.3 %collective-permute-start.1 = (bf16[1024,128]{1,0:T(8,128)(2,1)S(1)}, bf16[1024,128]{1,0:T(8,128)(2,1)S(1)}, u32[]{:S(2)}, u32[]{:S(2)}) collective-permute-start(bf16[1024,128]{1,0:T(8,128)(2,1)S(1)} %get-tuple-element.37), channel_id=1, source_target_pairs={{0,4},{4,0},{8,12},{12,8},{16,20},{20,16},{24,28},{28,24},{32,36},... | collective-permute-start | bytes 786440 | tf_op jit(solution)/shard_map/ppermute | solution.py:370
  15.6 0.0 collective-permute-done.7
  15.7 0.0 collective-permute-done.8
  15.7 0.9 %collective-permute-start.10 = (bf16[2048,128]{1,0:T(8,128)(2,1)S(1)}, bf16[2048,128]{1,0:T(8,128)(2,1)S(1)}, u32[]{:S(2)}, u32[]{:S(2)}) collective-permute-start(bf16[2048,128]{1,0:T(8,128)(2,1)S(1)} %constant_dynamic-update-slice_fusion.2.refs_0_), channel_id=1, source_target_pairs={{0,96},{4,28},{8,104},{12,4},{16,112},{20,12},{24,120},{28,20},{32... | collective-permute-start | bytes 1572872 | tf_op jit(solution)/shard_map/ppermute | solution.py:362
  16.7 0.6 collective-permute-start.9
  17.3 0.0 collective-permute-done.2.refs_1_
  17.3 2.1 %collective-permute-start.3 = (bf16[32,8192]{1,0:T(8,128)(2,1)S(1)}, bf16[32,8192]{1,0:T(8,128)(2,1)S(1)}, u32[]{:S(2)}, u32[]{:S(2)}) collective-permute-start(bf16[32,8192]{1,0:T(8,128)(2,1)S(1)} %collective-permute-done.2.refs_1_), channel_id=1, source_target_pairs={{0,1},{1,2},{2,3},{3,0},{4,7},{5,4},{6,5},{7,6},{8,9},{9,10},{10,1... | collective-permute-start | bytes 1572872 | tf_op jit(solution)/shard_map/ppermute | solution.py:384
  19.4 0.0 collective-permute-done.4.refs_2_
  19.4 0.0 slice-done
  19.4 0.0 slice-done.1
  19.4 0.0 copy-done.2
  19.4 1.4 %project_near.1 = (f32[96,256]{1,0:T(8,128)S(1)}, f32[96,256]{1,0:T(8,128)S(1)}) custom-call(bf16[32,8192]{1,0:T(8,128)(2,1)S(1)} %copy-done.2, bf16[32,8192]{1,0:T(8,128)(2,1)S(1)} %collective-permute-done.2.refs_1_, bf16[32,8192]{1,0:T(8,128)(2,1)S(1)} %collective-permute-done.4.refs_2_, bf16[2,8192,256]{2,1,0:T(8,128)(2,1)S(1)} %bitcast.1), custom_call_target="tpu_custom_call" | custom-call | flops 22000001024 | bytes 70000000 | tf_op jit(solution)/shard_map/project_near/pallas_call | solution.py:121
  20.8 0.0 copy-start
  20.9 3.4 %collective-permute-start.11 = (bf16[2048,128]{1,0:T(8,128)(2,1)S(1)}, bf16[2048,128]{1,0:T(8,128)(2,1)S(1)}, u32[]{:S(2)}, u32[]{:S(2)}) collective-permute-start(bf16[2048,128]{1,0:T(8,128)(2,1)S(1)} %constant_dynamic-update-slice_fusion.2.refs_0_), channel_id=1, source_target_pairs={{0,64},{4,20},{8,72},{12,28},{16,80},{20,4},{24,88},{28,12},{32,96... | collective-permute-start | bytes 1572872 | tf_op jit(solution)/shard_map/ppermute | solution.py:366
  24.3 0.3 fusion
  24.6 0.1 pad_maximum_fusion.1
  24.7 0.0 collective-permute-done.1.received
  24.7 0.9 %collective-permute-done.3.piece = bf16[32,8192]{1,0:T(8,128)(2,1)S(1)} collective-permute-done((bf16[32,8192]{1,0:T(8,128)(2,1)S(1)}, bf16[32,8192]{1,0:T(8,128)(2,1)S(1)}, u32[]{:S(2)}, u32[]{:S(2)}) %collective-permute-start.3) | collective-permute-done | bytes 524320 | tf_op jit(solution)/shard_map/ppermute | solution.py:384
  25.6 2.2 %project_far.1 = (bf16[128,256]{1,0:T(8,128)(2,1)}, bf16[128,256]{1,0:T(8,128)(2,1)}, bf16[256,128]{1,0:T(8,128)(2,1)S(1)}, bf16[256,128]{1,0:T(8,128)(2,1)S(1)}) custom-call(bf16[32,8192]{1,0:T(8,128)(2,1)S(1)} %collective-permute-done.3.piece, f32[96,256]{1,0:T(8,128)S(1)} %get-tuple-element.41.near_keys, f32[96,256]{1,0:T(8,128)S(1)} %get-tuple-element.42.near_values, ...), custom_call_target="tpu_custom_call" | custom-call | flops 110000000 | bytes 350000 | tf_op jit(solution)/shard_map/project_far/pallas_call | solution.py:164
  27.8 3.8 %collective-permute-start.5 = (bf16[256,128]{1,0:T(8,128)(2,1)S(1)}, bf16[256,128]{1,0:T(8,128)(2,1)S(1)}, u32[]{:S(2)}, u32[]{:S(2)}) collective-permute-start(bf16[256,128]{1,0:T(8,128)(2,1)S(1)} %get-tuple-element.44), channel_id=1, source_target_pairs={{0,4},{4,0},{8,12},{12,8},{16,20},{20,16},{24,28},{28,24},{32,36},... | collective-permute-start | bytes 196616 | tf_op jit(solution)/shard_map/ppermute | solution.py:370
  31.7 0.9 %collective-permute-done.5 = bf16[256,128]{1,0:T(8,128)(2,1)S(1)} collective-permute-done((bf16[256,128]{1,0:T(8,128)(2,1)S(1)}, bf16[256,128]{1,0:T(8,128)(2,1)S(1)}, u32[]{:S(2)}, u32[]{:S(2)}) %collective-permute-start.5) | collective-permute-done | bytes 65568 | tf_op jit(solution)/shard_map/ppermute | solution.py:370
  32.6 0.0 collective-permute-done.10.refs_2_
  32.6 0.0 collective-permute-done.9.refs_1_
  32.6 0.9 %collective-permute-start.12 = (bf16[512,128]{1,0:T(8,128)(2,1)S(1)}, bf16[512,128]{1,0:T(8,128)(2,1)S(1)}, u32[]{:S(2)}, u32[]{:S(2)}) collective-permute-start(bf16[512,128]{1,0:T(8,128)(2,1)S(1)} %pad_maximum_fusion), channel_id=1, source_target_pairs={{0,8},{4,36},{8,16},{12,44},{16,24},{20,52},{24,0},{28,60},{32,40}... | collective-permute-start | bytes 393224 | tf_op jit(solution)/shard_map/ppermute | solution.py:357
  33.5 0.5 collective-permute-start.14
  34.0 0.2 collective-permute-start.13
  34.1 0.0 collective-permute-done.11.refs_3_
  34.1 0.0 copy-done
  34.1 6.0 %attend_cache.1 = (f32[2048,128]{1,0:T(8,128)S(1)}, f32[2048,128]{1,0:T(8,128)S(1)}, f32[2048,128]{1,0:T(8,128)S(1)}) custom-call(s32[32]{0:T(128)S(1)} %copy-done, bf16[1024,128]{1,0:T(8,128)(2,1)S(1)} %get-tuple-element.46.own_queries, bf16[1024,128]{1,0:T(8,128)(2,1)S(1)} %collective-permute-done.1.received, ...), custom_call_target="tpu_custom_call" | custom-call | flops 110000000 | bytes 350000 | tf_op jit(solution)/shard_map/attend_cache/pallas_call | solution.py:234
  40.2 0.0 collective-permute-done.12
  40.2 0.0 collective-permute-done.13
  40.3 0.0 collective-permute-done.14
  40.3 0.1 collective-permute-start.15
  40.4 2.7 %collective-permute-start.17 = (bf16[2048,128]{1,0:T(8,128)(2,1)S(1)}, bf16[2048,128]{1,0:T(8,128)(2,1)S(1)}, u32[]{:S(2)}, u32[]{:S(2)}) collective-permute-start(bf16[2048,128]{1,0:T(8,128)(2,1)S(1)} %constant_dynamic-update-slice_fusion.7.refs_0_), channel_id=1, source_target_pairs={{0,96},{4,28},{8,104},{12,4},{16,112},{20,12},{24,120},{28,20},{32... | collective-permute-start | bytes 1572872 | tf_op jit(solution)/shard_map/ppermute | solution.py:362
  43.1 4.0 %attend_new.2 = (f32[2048,128]{1,0:T(8,128)S(1)}, f32[2048,128]{1,0:T(8,128)S(1)}, f32[2048,128]{1,0:T(8,128)S(1)}) custom-call(bf16[1024,128]{1,0:T(8,128)(2,1)S(1)} %get-tuple-element.46.own_queries, bf16[1024,128]{1,0:T(8,128)(2,1)S(1)} %collective-permute-done.1.received, bf16[2048,128]{1,0:T(8,128)(2,1)S(1)} %constant_dynamic-update-slice_fusion.7.refs_0_, ...), custom_call_target="tpu_custom_call" | custom-call | flops 110000000 | bytes 350000 | tf_op jit(solution)/shard_map/attend_new/pallas_call | solution.py:334
  47.1 2.8 %collective-permute-done.15.refs_0_ = bf16[2048,128]{1,0:T(8,128)(2,1)S(1)} collective-permute-done((bf16[2048,128]{1,0:T(8,128)(2,1)S(1)}, bf16[2048,128]{1,0:T(8,128)(2,1)S(1)}, u32[]{:S(2)}, u32[]{:S(2)}) %collective-permute-start.15) | collective-permute-done | bytes 524320 | tf_op jit(solution)/shard_map/ppermute | solution.py:362
  49.9 0.0 collective-permute-start.16
  49.9 0.0 collective-permute-done.17.refs_1_
  49.9 5.1 %attend_new.3 = (f32[2048,128]{1,0:T(8,128)S(1)}, f32[2048,128]{1,0:T(8,128)S(1)}, f32[2048,128]{1,0:T(8,128)S(1)}) custom-call(bf16[1024,128]{1,0:T(8,128)(2,1)S(1)} %get-tuple-element.46.own_queries, bf16[1024,128]{1,0:T(8,128)(2,1)S(1)} %collective-permute-done.1.received, bf16[2048,128]{1,0:T(8,128)(2,1)S(1)} %collective-permute-done.15.refs_0_, ...), custom_call_target="tpu_custom_call" | custom-call | flops 110000000 | bytes 350000 | tf_op jit(solution)/shard_map/attend_new/pallas_call | solution.py:334
  55.0 4.8 %collective-permute-done.16.refs_0_ = bf16[2048,128]{1,0:T(8,128)(2,1)S(1)} collective-permute-done((bf16[2048,128]{1,0:T(8,128)(2,1)S(1)}, bf16[2048,128]{1,0:T(8,128)(2,1)S(1)}, u32[]{:S(2)}, u32[]{:S(2)}) %collective-permute-start.16) | collective-permute-done | bytes 524320 | tf_op jit(solution)/shard_map/ppermute | solution.py:366
  59.7 3.3 %attend_new_last.1 = (bf16[128,1024]{1,0:T(8,128)(2,1)S(1)}, bf16[128,1024]{1,0:T(8,128)(2,1)S(1)}) custom-call(bf16[1024,128]{1,0:T(8,128)(2,1)S(1)} %get-tuple-element.46.own_queries, bf16[1024,128]{1,0:T(8,128)(2,1)S(1)} %collective-permute-done.1.received, bf16[2048,128]{1,0:T(8,128)(2,1)S(1)} %collective-permute-done.16.refs_0_, ...), custom_call_target="tpu_custom_call" | custom-call | flops 110000000 | bytes 350000 | tf_op jit(solution)/shard_map/attend_new_last/pallas_call | solution.py:334
  63.0 3.7 %collective-permute-start.18 = (bf16[128,1024]{1,0:T(8,128)(2,1)S(1)}, bf16[128,1024]{1,0:T(8,128)(2,1)S(1)}, u32[]{:S(2)}, u32[]{:S(2)}) collective-permute-start(bf16[128,1024]{1,0:T(8,128)(2,1)S(1)} %get-tuple-element.60), channel_id=1, source_target_pairs={{0,4},{4,0},{8,12},{12,8},{16,20},{20,16},{24,28},{28,24},{32,36},... | collective-permute-start | bytes 786440 | tf_op jit(solution)/shard_map/ppermute | solution.py:370
  66.7 1.2 %collective-permute-done.18 = bf16[128,1024]{1,0:T(8,128)(2,1)S(1)} collective-permute-done((bf16[128,1024]{1,0:T(8,128)(2,1)S(1)}, bf16[128,1024]{1,0:T(8,128)(2,1)S(1)}, u32[]{:S(2)}, u32[]{:S(2)}) %collective-permute-start.18) | collective-permute-done | bytes 262176 | tf_op jit(solution)/shard_map/ppermute | solution.py:370
  67.8 0.9 %maximum_select_fusion = bf16[128,2048]{1,0:T(8,128)(2,1)} fusion(bf16[128,1024]{1,0:T(8,128)(2,1)S(1)} %collective-permute-done.18, bf16[128,1024]{1,0:T(8,128)(2,1)S(1)} %get-tuple-element.59, pred[]{:T(512)S(6)} %eq.3), kind=kLoop, calls=%fused_computation | loop fusion | flops 2359296 | bytes 1048577 | tf_op jit(solution)/shard_map/jit(_where)/select_n | solution.py:412
  (14 shorter events, 0.2 us)
Async XLA Ops:
  0.6 0.8 %copy-start.3 = (bf16[128,256]{1,0:T(8,128)(2,1)S(1)}, bf16[128,256]{1,0:T(8,128)(2,1)}, u32[]{:S(2)}) copy-start(bf16[128,256]{1,0:T(8,128)(2,1)} %refs_0_.2) | copy-start | bytes 196612
  1.5 0.8 %copy-start.4 = (bf16[128,256]{1,0:T(8,128)(2,1)S(1)}, bf16[128,256]{1,0:T(8,128)(2,1)}, u32[]{:S(2)}) copy-start(bf16[128,256]{1,0:T(8,128)(2,1)} %refs_1_.1) | copy-start | bytes 196612
  2.3 3.3 %collective-permute-start = (bf16[256,128]{1,0:T(8,128)(2,1)S(1)}, bf16[256,128]{1,0:T(8,128)(2,1)S(1)}, u32[]{:S(2)}, u32[]{:S(2)}) collective-permute-start(bf16[256,128]{1,0:T(8,128)(2,1)S(1)} %get-tuple-element.34), channel_id=1, source_target_pairs={{0,4},{4,0},{8,12},{12,8},{16,20},{20,16},{24,28},{28,24},{32,36},... | collective-permute-start | bytes 196616 | tf_op jit(solution)/shard_map/ppermute | solution.py:370
  3.1 14.2 %collective-permute-start.2 = (bf16[32,8192]{1,0:T(8,128)(2,1)}, bf16[32,8192]{1,0:T(8,128)(2,1)S(1)}, u32[]{:S(2)}, u32[]{:S(2)}) collective-permute-start(bf16[32,8192]{1,0:T(8,128)(2,1)} %refs_0_.4), channel_id=1, source_target_pairs={{0,1},{1,2},{2,3},{3,0},{4,7},{5,4},{6,5},{7,6},{8,9},{9,10},{10,1... | collective-permute-start | bytes 1572872 | tf_op jit(solution)/shard_map/ppermute | solution.py:377
  5.7 13.7 %slice-start = ((s8[8388608]{0:T(1024)(128)(4,1)}), s8[4194304]{0:T(1024)(128)(4,1)S(1)}, s32[]{:S(2)}) async-start(s8[8388608]{0:T(1024)(128)(4,1)} %bitcast), calls=%async_computation | async-start | bytes 8388608
  5.7 13.7 %slice-start.1 = ((s8[8388608]{0:T(1024)(128)(4,1)}), s8[4194304]{0:T(1024)(128)(4,1)S(1)}, s32[]{:S(2)}) async-start(s8[8388608]{0:T(1024)(128)(4,1)} %bitcast), calls=%async_computation.1 | async-start | bytes 8388608
  5.7 10.0 %collective-permute-start.8 = (bf16[512,128]{1,0:T(8,128)(2,1)S(1)}, bf16[512,128]{1,0:T(8,128)(2,1)S(1)}, u32[]{:S(2)}, u32[]{:S(2)}) collective-permute-start(bf16[512,128]{1,0:T(8,128)(2,1)S(1)} %get-tuple-element.64), channel_id=1, source_target_pairs={{0,16},{4,68},{8,24},{12,76},{16,0},{20,84},{24,8},{28,92},{32,48}... | collective-permute-start | bytes 393224 | tf_op jit(solution)/shard_map/ppermute | solution.py:357
  6.7 8.9 %collective-permute-start.7 = (bf16[512,128]{1,0:T(8,128)(2,1)S(1)}, bf16[512,128]{1,0:T(8,128)(2,1)S(1)}, u32[]{:S(2)}, u32[]{:S(2)}) collective-permute-start(bf16[512,128]{1,0:T(8,128)(2,1)S(1)} %get-tuple-element.64), channel_id=1, source_target_pairs={{0,24},{4,100},{8,0},{12,108},{16,8},{20,116},{24,16},{28,124},{32... | collective-permute-start | bytes 393224 | tf_op jit(solution)/shard_map/ppermute | solution.py:357
  6.7 4.6 %collective-permute-start.6 = (bf16[512,128]{1,0:T(8,128)(2,1)S(1)}, bf16[512,128]{1,0:T(8,128)(2,1)S(1)}, u32[]{:S(2)}, u32[]{:S(2)}) collective-permute-start(bf16[512,128]{1,0:T(8,128)(2,1)S(1)} %get-tuple-element.64), channel_id=1, source_target_pairs={{0,8},{4,36},{8,16},{12,44},{16,24},{20,52},{24,0},{28,60},{32,40}... | collective-permute-start | bytes 393224 | tf_op jit(solution)/shard_map/ppermute | solution.py:357
  9.4 10.0 %collective-permute-start.4 = (bf16[32,8192]{1,0:T(8,128)(2,1)}, bf16[32,8192]{1,0:T(8,128)(2,1)S(1)}, u32[]{:S(2)}, u32[]{:S(2)}) collective-permute-start(bf16[32,8192]{1,0:T(8,128)(2,1)} %refs_0_.4), channel_id=1, source_target_pairs={{0,3},{1,0},{2,1},{3,2},{4,5},{5,6},{6,7},{7,4},{8,11},{9,8},{10,9... | collective-permute-start | bytes 1572872 | tf_op jit(solution)/shard_map/ppermute | solution.py:380
  9.4 1.0 %copy-start.1 = (bf16[128,2048]{1,0:T(8,128)(2,1)S(1)}, bf16[128,2048]{1,0:T(8,128)(2,1)}, u32[]{:S(2)}) copy-start(bf16[128,2048]{1,0:T(8,128)(2,1)} %refs_0_.3) | copy-start | bytes 1572868
  10.4 8.9 %copy-start.2 = (bf16[32,8192]{1,0:T(8,128)(2,1)S(1)}, bf16[32,8192]{1,0:T(8,128)(2,1)}, u32[]{:S(2)}) copy-start(bf16[32,8192]{1,0:T(8,128)(2,1)} %refs_0_.4) | copy-start | bytes 1572868
  11.3 13.4 %collective-permute-start.1 = (bf16[1024,128]{1,0:T(8,128)(2,1)S(1)}, bf16[1024,128]{1,0:T(8,128)(2,1)S(1)}, u32[]{:S(2)}, u32[]{:S(2)}) collective-permute-start(bf16[1024,128]{1,0:T(8,128)(2,1)S(1)} %get-tuple-element.37), channel_id=1, source_target_pairs={{0,4},{4,0},{8,12},{12,8},{16,20},{20,16},{24,28},{28,24},{32,36},... | collective-permute-start | bytes 786440 | tf_op jit(solution)/shard_map/ppermute | solution.py:370
  15.7 16.9 %collective-permute-start.10 = (bf16[2048,128]{1,0:T(8,128)(2,1)S(1)}, bf16[2048,128]{1,0:T(8,128)(2,1)S(1)}, u32[]{:S(2)}, u32[]{:S(2)}) collective-permute-start(bf16[2048,128]{1,0:T(8,128)(2,1)S(1)} %constant_dynamic-update-slice_fusion.2.refs_0_), channel_id=1, source_target_pairs={{0,96},{4,28},{8,104},{12,4},{16,112},{20,12},{24,120},{28,20},{32... | collective-permute-start | bytes 1572872 | tf_op jit(solution)/shard_map/ppermute | solution.py:362
  16.7 15.9 %collective-permute-start.9 = (bf16[2048,128]{1,0:T(8,128)(2,1)S(1)}, bf16[2048,128]{1,0:T(8,128)(2,1)S(1)}, u32[]{:S(2)}, u32[]{:S(2)}) collective-permute-start(bf16[2048,128]{1,0:T(8,128)(2,1)S(1)} %constant_dynamic-update-slice_fusion.2.refs_0_), channel_id=1, source_target_pairs={{0,32},{4,12},{8,40},{12,20},{16,48},{20,28},{24,56},{28,4},{32,64... | collective-permute-start | bytes 1572872 | tf_op jit(solution)/shard_map/ppermute | solution.py:362
  17.3 8.3 %collective-permute-start.3 = (bf16[32,8192]{1,0:T(8,128)(2,1)S(1)}, bf16[32,8192]{1,0:T(8,128)(2,1)S(1)}, u32[]{:S(2)}, u32[]{:S(2)}) collective-permute-start(bf16[32,8192]{1,0:T(8,128)(2,1)S(1)} %collective-permute-done.2.refs_1_), channel_id=1, source_target_pairs={{0,1},{1,2},{2,3},{3,0},{4,7},{5,4},{6,5},{7,6},{8,9},{9,10},{10,1... | collective-permute-start | bytes 1572872 | tf_op jit(solution)/shard_map/ppermute | solution.py:384
  20.8 13.3 %copy-start = (s32[32]{0:T(128)S(1)}, s32[32]{0:T(128)}, u32[]{:S(2)}) copy-start(s32[32]{0:T(128)} %kv_blocks.1) | copy-start | bytes 388
  20.9 13.3 %collective-permute-start.11 = (bf16[2048,128]{1,0:T(8,128)(2,1)S(1)}, bf16[2048,128]{1,0:T(8,128)(2,1)S(1)}, u32[]{:S(2)}, u32[]{:S(2)}) collective-permute-start(bf16[2048,128]{1,0:T(8,128)(2,1)S(1)} %constant_dynamic-update-slice_fusion.2.refs_0_), channel_id=1, source_target_pairs={{0,64},{4,20},{8,72},{12,28},{16,80},{20,4},{24,88},{28,12},{32,96... | collective-permute-start | bytes 1572872 | tf_op jit(solution)/shard_map/ppermute | solution.py:366
  27.8 4.7 %collective-permute-start.5 = (bf16[256,128]{1,0:T(8,128)(2,1)S(1)}, bf16[256,128]{1,0:T(8,128)(2,1)S(1)}, u32[]{:S(2)}, u32[]{:S(2)}) collective-permute-start(bf16[256,128]{1,0:T(8,128)(2,1)S(1)} %get-tuple-element.44), channel_id=1, source_target_pairs={{0,4},{4,0},{8,12},{12,8},{16,20},{20,16},{24,28},{28,24},{32,36},... | collective-permute-start | bytes 196616 | tf_op jit(solution)/shard_map/ppermute | solution.py:370
  32.6 7.6 %collective-permute-start.12 = (bf16[512,128]{1,0:T(8,128)(2,1)S(1)}, bf16[512,128]{1,0:T(8,128)(2,1)S(1)}, u32[]{:S(2)}, u32[]{:S(2)}) collective-permute-start(bf16[512,128]{1,0:T(8,128)(2,1)S(1)} %pad_maximum_fusion), channel_id=1, source_target_pairs={{0,8},{4,36},{8,16},{12,44},{16,24},{20,52},{24,0},{28,60},{32,40}... | collective-permute-start | bytes 393224 | tf_op jit(solution)/shard_map/ppermute | solution.py:357
  33.5 6.8 %collective-permute-start.14 = (bf16[512,128]{1,0:T(8,128)(2,1)S(1)}, bf16[512,128]{1,0:T(8,128)(2,1)S(1)}, u32[]{:S(2)}, u32[]{:S(2)}) collective-permute-start(bf16[512,128]{1,0:T(8,128)(2,1)S(1)} %pad_maximum_fusion), channel_id=1, source_target_pairs={{0,16},{4,68},{8,24},{12,76},{16,0},{20,84},{24,8},{28,92},{32,48}... | collective-permute-start | bytes 393224 | tf_op jit(solution)/shard_map/ppermute | solution.py:357
  34.0 6.3 %collective-permute-start.13 = (bf16[512,128]{1,0:T(8,128)(2,1)S(1)}, bf16[512,128]{1,0:T(8,128)(2,1)S(1)}, u32[]{:S(2)}, u32[]{:S(2)}) collective-permute-start(bf16[512,128]{1,0:T(8,128)(2,1)S(1)} %pad_maximum_fusion), channel_id=1, source_target_pairs={{0,24},{4,100},{8,0},{12,108},{16,8},{20,116},{24,16},{28,124},{32... | collective-permute-start | bytes 393224 | tf_op jit(solution)/shard_map/ppermute | solution.py:357
  40.3 9.6 %collective-permute-start.15 = (bf16[2048,128]{1,0:T(8,128)(2,1)S(1)}, bf16[2048,128]{1,0:T(8,128)(2,1)S(1)}, u32[]{:S(2)}, u32[]{:S(2)}) collective-permute-start(bf16[2048,128]{1,0:T(8,128)(2,1)S(1)} %constant_dynamic-update-slice_fusion.7.refs_0_), channel_id=1, source_target_pairs={{0,32},{4,12},{8,40},{12,20},{16,48},{20,28},{24,56},{28,4},{32,64... | collective-permute-start | bytes 1572872 | tf_op jit(solution)/shard_map/ppermute | solution.py:362
  40.4 9.5 %collective-permute-start.17 = (bf16[2048,128]{1,0:T(8,128)(2,1)S(1)}, bf16[2048,128]{1,0:T(8,128)(2,1)S(1)}, u32[]{:S(2)}, u32[]{:S(2)}) collective-permute-start(bf16[2048,128]{1,0:T(8,128)(2,1)S(1)} %constant_dynamic-update-slice_fusion.7.refs_0_), channel_id=1, source_target_pairs={{0,96},{4,28},{8,104},{12,4},{16,112},{20,12},{24,120},{28,20},{32... | collective-permute-start | bytes 1572872 | tf_op jit(solution)/shard_map/ppermute | solution.py:362
  49.9 9.8 %collective-permute-start.16 = (bf16[2048,128]{1,0:T(8,128)(2,1)S(1)}, bf16[2048,128]{1,0:T(8,128)(2,1)S(1)}, u32[]{:S(2)}, u32[]{:S(2)}) collective-permute-start(bf16[2048,128]{1,0:T(8,128)(2,1)S(1)} %constant_dynamic-update-slice_fusion.7.refs_0_), channel_id=1, source_target_pairs={{0,64},{4,20},{8,72},{12,28},{16,80},{20,4},{24,88},{28,12},{32,96... | collective-permute-start | bytes 1572872 | tf_op jit(solution)/shard_map/ppermute | solution.py:366
  63.0 4.8 %collective-permute-start.18 = (bf16[128,1024]{1,0:T(8,128)(2,1)S(1)}, bf16[128,1024]{1,0:T(8,128)(2,1)S(1)}, u32[]{:S(2)}, u32[]{:S(2)}) collective-permute-start(bf16[128,1024]{1,0:T(8,128)(2,1)S(1)} %get-tuple-element.60), channel_id=1, source_target_pairs={{0,4},{4,0},{8,12},{12,8},{16,20},{20,16},{24,28},{28,24},{32,36},... | collective-permute-start | bytes 786440 | tf_op jit(solution)/shard_map/ppermute | solution.py:370

commit v5 on v4

--- a/solution.py
+++ b/solution.py
@@ -349,6 +349,42 @@
     )(own_queries, received, *pieces, *states)
 
 
+def finish_kernel(here, other, keys, values, attended, keys_out, values_out, sems):
+    core, _, _ = place()
+    width = here.shape[1]
+
+    def half(i):
+        return attended.at[:, pl.ds(pl.multiple_of(i * width, width), width)]
+
+    copies = [
+        pltpu.make_async_copy(source, target, sems.at[i])
+        for i, (source, target) in enumerate(
+            ((here, half(core)), (other, half(1 - core)), (keys, keys_out), (values, values_out))
+        )
+    ]
+    for copy in copies:
+        copy.start()
+    for copy in copies:
+        copy.wait()
+
+
+def finish(here, other, keys, values):
+    rows, width = here.shape
+    hbm = pl.BlockSpec(memory_space=pltpu.HBM)
+    return pl.pallas_call(
+        finish_kernel,
+        out_shape=tuple(
+            jax.ShapeDtypeStruct(shape, BF16) for shape in ((rows, 2 * width), keys.shape, values.shape)
+        ),
+        in_specs=[VMEM] * 4,
+        out_specs=(hbm,) * 3,
+        scratch_shapes=[pltpu.SemaphoreType.DMA((4,))],
+        compiler_params=pltpu.CompilerParams(vmem_limit_bytes=4 << 20),
+        cost_estimate=cost(0.1),
+        name="finish",
+    )(here, other, keys, values)
+
+
 def after(value, *others):
     return lax.optimization_barrier((value, *others))[0]
 
@@ -400,7 +436,7 @@
         jnp.concatenate([cosine, cosine], 1),
         jnp.concatenate([-sine, sine], 1),
     )
-    block = after(jnp.concatenate([mine, swapped(give)], 0), *cache[:3])
+    block = jnp.concatenate([mine, swapped(give)], 0)
     states = attend_cache(kv_blocks, after(own_queries, block), received, cache, live_keys)
     joined = first_phase(block, states[0])
     new = second_phase(joined)
@@ -409,10 +445,7 @@
     states = attend_new(own_queries, received, (1, 2), new[1:3], states, False)
     here, there = attend_new(own_queries, received, (3,), new[3:], states, True)
     other = swapped(there)
-    attended = jnp.where(
-        core == 0, jnp.concatenate([here, other], 1), jnp.concatenate([other, here], 1)
-    )
-    return (attended, new_keys, new_values)
+    return finish(here, other, new_keys, new_values)
 
 
 def solution(mesh):

time: 69.7 us -> 68.6 us (0.984)
  other arithmetic: 1.35 us -> 0.42 us
    select_n x1 -> x0, other arithmetic: 0.92 us -> none  [shards(): jnp.where(core == 0, jnp.concatenate([here, other], 1), jnp.concatenate([...]
    pallas_call x0 -> x1, Pallas kernels: none -> 0.86 us  [finish(): pl.pallas_call(finish_kernel, out_shape=tuple((jax.ShapeDtypeStruct(shape...]
    unnamed x21 -> x22, local copies, waits for them, and re-layouts: 2.86 us -> 2.86 us
where the time goes in v5:
time: 68.6 us; the launch traced here: 68.3 us
  starting transfers between devices  30.2 us (44%)
  Pallas kernels  22.4 us (33%)
  waiting for transfers between devices  11.3 us (16%)
  local copies, waits for them, and re-layouts  2.92 us (4%)
  between operations  1.09 us (2%)
    ppermute x4, starting transfers between devices, swapped(): return lax.ppermute(block, 'group', swap_cores())  12.6 us
    pallas_call x3, Pallas kernels, attend_new(): pl.pallas_call(functools.partial(new_kernel, which, last), out_shape=(out...  12.3 us
    pallas_call x1, Pallas kernels, attend_cache(): pl.pallas_call(functools.partial(cache_kernel, live_keys), out_shape=(STA...  6.02 us
    ppermute x6, starting transfers between devices, first_phase(): sent = [lax.ppermute(block, 'group', along(0, d)) for d in (1, 3, 2)]  5.24 us
    ppermute x2, waiting for transfers between devices, last_phase(): return lax.ppermute(after(joined, *others), 'group', along(1, 2))  4.75 us
    ppermute x4, starting transfers between devices, second_phase(): lax.ppermute(joined, 'group', along(1, d))  4.27 us
    ppermute x2, starting transfers between devices, last_phase(): return lax.ppermute(after(joined, *others), 'group', along(1, 2))  3.45 us
    unnamed x22, local copies, waits for them, and re-layouts  2.86 us
  transfers between devices with their start and end apart: 19, of which 6 were waited for; matrix products, arithmetic and copies ran while one was open for 1% of the time, Pallas kernels for 27%

profile of v5, /device:TPU:25, one launch (start us, length us, event | category | flops | bytes accessed | tf_op | source)
XLA Modules:
  0.0 68.3 jit_solution(2576332841436955363)
XLA Ops:
  0.6 0.0 copy-start.3
  0.6 0.8 %copy-done.3 = bf16[128,256]{1,0:T(8,128)(2,1)S(1)} copy-done((bf16[128,256]{1,0:T(8,128)(2,1)S(1)}, bf16[128,256]{1,0:T(8,128)(2,1)}, u32[]{:S(2)}) %copy-start.3) | copy-done | bytes 65560
  1.5 0.0 copy-start.4
  1.5 0.8 %copy-done.4 = bf16[128,256]{1,0:T(8,128)(2,1)S(1)} copy-done((bf16[128,256]{1,0:T(8,128)(2,1)S(1)}, bf16[128,256]{1,0:T(8,128)(2,1)}, u32[]{:S(2)}) %copy-start.4) | copy-done | bytes 65560
  2.3 0.8 %collective-permute-start = (bf16[256,128]{1,0:T(8,128)(2,1)S(1)}, bf16[256,128]{1,0:T(8,128)(2,1)S(1)}, u32[]{:S(2)}, u32[]{:S(2)}) collective-permute-start(bf16[256,128]{1,0:T(8,128)(2,1)S(1)} %get-tuple-element.33), channel_id=1, source_target_pairs={{0,4},{4,0},{8,12},{12,8},{16,20},{20,16},{24,28},{28,24},{32,36},... | collective-permute-start | bytes 196616 | tf_op jit(solution)/shard_map/ppermute | solution.py:406
  3.1 2.5 %collective-permute-start.2 = (bf16[32,8192]{1,0:T(8,128)(2,1)}, bf16[32,8192]{1,0:T(8,128)(2,1)S(1)}, u32[]{:S(2)}, u32[]{:S(2)}) collective-permute-start(bf16[32,8192]{1,0:T(8,128)(2,1)} %refs_0_.4), channel_id=1, source_target_pairs={{0,1},{1,2},{2,3},{3,0},{4,7},{5,4},{6,5},{7,6},{8,9},{9,10},{10,1... | collective-permute-start | bytes 1572872 | tf_op jit(solution)/shard_map/ppermute | solution.py:413
  5.6 0.0 collective-permute-done
  5.7 0.0 slice-start
  5.7 0.0 slice-start.1
  5.7 1.0 %collective-permute-start.8 = (bf16[512,128]{1,0:T(8,128)(2,1)S(1)}, bf16[512,128]{1,0:T(8,128)(2,1)S(1)}, u32[]{:S(2)}, u32[]{:S(2)}) collective-permute-start(bf16[512,128]{1,0:T(8,128)(2,1)S(1)} %get-tuple-element.62), channel_id=1, source_target_pairs={{0,16},{4,68},{8,24},{12,76},{16,0},{20,84},{24,8},{28,92},{32,48}... | collective-permute-start | bytes 393224 | tf_op jit(solution)/shard_map/ppermute | solution.py:393
  6.7 0.0 collective-permute-start.7
  6.7 2.7 %collective-permute-start.6 = (bf16[512,128]{1,0:T(8,128)(2,1)S(1)}, bf16[512,128]{1,0:T(8,128)(2,1)S(1)}, u32[]{:S(2)}, u32[]{:S(2)}) collective-permute-start(bf16[512,128]{1,0:T(8,128)(2,1)S(1)} %get-tuple-element.62), channel_id=1, source_target_pairs={{0,8},{4,36},{8,16},{12,44},{16,24},{20,52},{24,0},{28,60},{32,40}... | collective-permute-start | bytes 393224 | tf_op jit(solution)/shard_map/ppermute | solution.py:393
  9.4 0.0 collective-permute-start.4
  9.4 0.0 copy-start.1
  9.4 1.0 %copy-done.1 = bf16[128,2048]{1,0:T(8,128)(2,1)S(1)} copy-done((bf16[128,2048]{1,0:T(8,128)(2,1)S(1)}, bf16[128,2048]{1,0:T(8,128)(2,1)}, u32[]{:S(2)}) %copy-start.1) | copy-done | bytes 524312
  10.4 0.0 copy-start.2
  10.4 0.1 heads.3
  10.6 0.8 %collective-permute-done.6 = bf16[512,128]{1,0:T(8,128)(2,1)S(1)} collective-permute-done((bf16[512,128]{1,0:T(8,128)(2,1)S(1)}, bf16[512,128]{1,0:T(8,128)(2,1)S(1)}, u32[]{:S(2)}, u32[]{:S(2)}) %collective-permute-start.6) | collective-permute-done | bytes 131104 | tf_op jit(solution)/shard_map/ppermute | solution.py:393
  11.3 4.3 %collective-permute-start.1 = (bf16[1024,128]{1,0:T(8,128)(2,1)S(1)}, bf16[1024,128]{1,0:T(8,128)(2,1)S(1)}, u32[]{:S(2)}, u32[]{:S(2)}) collective-permute-start(bf16[1024,128]{1,0:T(8,128)(2,1)S(1)} %get-tuple-element.36), channel_id=1, source_target_pairs={{0,4},{4,0},{8,12},{12,8},{16,20},{20,16},{24,28},{28,24},{32,36},... | collective-permute-start | bytes 786440 | tf_op jit(solution)/shard_map/ppermute | solution.py:406
  15.6 0.0 collective-permute-done.7
  15.7 0.0 collective-permute-done.8
  15.7 0.9 %collective-permute-start.10 = (bf16[2048,128]{1,0:T(8,128)(2,1)S(1)}, bf16[2048,128]{1,0:T(8,128)(2,1)S(1)}, u32[]{:S(2)}, u32[]{:S(2)}) collective-permute-start(bf16[2048,128]{1,0:T(8,128)(2,1)S(1)} %constant_dynamic-update-slice_fusion.4.refs_0_), channel_id=1, source_target_pairs={{0,96},{4,28},{8,104},{12,4},{16,112},{20,12},{24,120},{28,20},{32... | collective-permute-start | bytes 1572872 | tf_op jit(solution)/shard_map/ppermute | solution.py:398
  16.7 0.6 collective-permute-start.9
  17.3 0.0 collective-permute-done.2.refs_1_
  17.3 2.1 %collective-permute-start.3 = (bf16[32,8192]{1,0:T(8,128)(2,1)S(1)}, bf16[32,8192]{1,0:T(8,128)(2,1)S(1)}, u32[]{:S(2)}, u32[]{:S(2)}) collective-permute-start(bf16[32,8192]{1,0:T(8,128)(2,1)S(1)} %collective-permute-done.2.refs_1_), channel_id=1, source_target_pairs={{0,1},{1,2},{2,3},{3,0},{4,7},{5,4},{6,5},{7,6},{8,9},{9,10},{10,1... | collective-permute-start | bytes 1572872 | tf_op jit(solution)/shard_map/ppermute | solution.py:420
  19.4 0.0 collective-permute-done.4.refs_2_
  19.4 0.0 slice-done
  19.4 0.0 slice-done.1
  19.4 0.0 copy-done.2
  19.4 1.4 %project_near.1 = (f32[96,256]{1,0:T(8,128)S(1)}, f32[96,256]{1,0:T(8,128)S(1)}) custom-call(bf16[32,8192]{1,0:T(8,128)(2,1)S(1)} %copy-done.2, bf16[32,8192]{1,0:T(8,128)(2,1)S(1)} %collective-permute-done.2.refs_1_, bf16[32,8192]{1,0:T(8,128)(2,1)S(1)} %collective-permute-done.4.refs_2_, bf16[2,8192,256]{2,1,0:T(8,128)(2,1)S(1)} %bitcast.1), custom_call_target="tpu_custom_call" | custom-call | flops 22000001024 | bytes 70000000 | tf_op jit(solution)/shard_map/project_near/pallas_call | solution.py:121
  20.8 0.0 copy-start
  20.9 3.4 %collective-permute-start.11 = (bf16[2048,128]{1,0:T(8,128)(2,1)S(1)}, bf16[2048,128]{1,0:T(8,128)(2,1)S(1)}, u32[]{:S(2)}, u32[]{:S(2)}) collective-permute-start(bf16[2048,128]{1,0:T(8,128)(2,1)S(1)} %constant_dynamic-update-slice_fusion.4.refs_0_), channel_id=1, source_target_pairs={{0,64},{4,20},{8,72},{12,28},{16,80},{20,4},{24,88},{28,12},{32,96... | collective-permute-start | bytes 1572872 | tf_op jit(solution)/shard_map/ppermute | solution.py:402
  24.3 0.3 fusion
  24.6 0.1 pad_maximum_fusion
  24.7 0.0 collective-permute-done.1.received
  24.7 0.9 %collective-permute-done.3.piece = bf16[32,8192]{1,0:T(8,128)(2,1)S(1)} collective-permute-done((bf16[32,8192]{1,0:T(8,128)(2,1)S(1)}, bf16[32,8192]{1,0:T(8,128)(2,1)S(1)}, u32[]{:S(2)}, u32[]{:S(2)}) %collective-permute-start.3) | collective-permute-done | bytes 524320 | tf_op jit(solution)/shard_map/ppermute | solution.py:420
  25.6 1.6 %project_far.1 = (bf16[128,256]{1,0:T(8,128)(2,1)S(1)}, bf16[128,256]{1,0:T(8,128)(2,1)S(1)}, bf16[256,128]{1,0:T(8,128)(2,1)S(1)}, bf16[256,128]{1,0:T(8,128)(2,1)S(1)}) custom-call(bf16[32,8192]{1,0:T(8,128)(2,1)S(1)} %collective-permute-done.3.piece, f32[96,256]{1,0:T(8,128)S(1)} %get-tuple-element.40.near_keys, ...), custom_call_target="tpu_custom_call" | custom-call | flops 110000000 | bytes 350000 | tf_op jit(solution)/shard_map/project_far/pallas_call | solution.py:164
  27.2 3.9 %collective-permute-start.5 = (bf16[256,128]{1,0:T(8,128)(2,1)S(1)}, bf16[256,128]{1,0:T(8,128)(2,1)S(1)}, u32[]{:S(2)}, u32[]{:S(2)}) collective-permute-start(bf16[256,128]{1,0:T(8,128)(2,1)S(1)} %get-tuple-element.43), channel_id=1, source_target_pairs={{0,4},{4,0},{8,12},{12,8},{16,20},{20,16},{24,28},{28,24},{32,36},... | collective-permute-start | bytes 196616 | tf_op jit(solution)/shard_map/ppermute | solution.py:406
  31.1 0.9 %collective-permute-done.5 = bf16[256,128]{1,0:T(8,128)(2,1)S(1)} collective-permute-done((bf16[256,128]{1,0:T(8,128)(2,1)S(1)}, bf16[256,128]{1,0:T(8,128)(2,1)S(1)}, u32[]{:S(2)}, u32[]{:S(2)}) %collective-permute-start.5) | collective-permute-done | bytes 65568 | tf_op jit(solution)/shard_map/ppermute | solution.py:406
  32.0 0.1 collective-permute-start.12
  32.1 1.0 %collective-permute-start.14 = (bf16[512,128]{1,0:T(8,128)(2,1)S(1)}, bf16[512,128]{1,0:T(8,128)(2,1)S(1)}, u32[]{:S(2)}, u32[]{:S(2)}) collective-permute-start(bf16[512,128]{1,0:T(8,128)(2,1)S(1)} %constant_dynamic-update-slice_fusion.2), channel_id=1, source_target_pairs={{0,16},{4,68},{8,24},{12,76},{16,0},{20,84},{24,8},{28,92},{32,48}... | collective-permute-start | bytes 393224 | tf_op jit(solution)/shard_map/ppermute | solution.py:393
  33.2 0.0 collective-permute-done.10.refs_2_
  33.2 0.4 collective-permute-start.13
  33.6 0.0 collective-permute-done.9.refs_1_
  33.6 0.0 collective-permute-done.11.refs_3_
  33.6 0.0 copy-done
  33.6 6.0 %attend_cache.1 = (f32[2048,128]{1,0:T(8,128)S(1)}, f32[2048,128]{1,0:T(8,128)S(1)}, f32[2048,128]{1,0:T(8,128)S(1)}) custom-call(s32[32]{0:T(128)S(1)} %copy-done, bf16[1024,128]{1,0:T(8,128)(2,1)S(1)} %get-tuple-element.44.own_queries, bf16[1024,128]{1,0:T(8,128)(2,1)S(1)} %collective-permute-done.1.received, ...), custom_call_target="tpu_custom_call" | custom-call | flops 110000000 | bytes 350000 | tf_op jit(solution)/shard_map/attend_cache/pallas_call | solution.py:234
  39.6 0.0 collective-permute-done.12
  39.7 0.0 collective-permute-done.13
  39.7 0.0 collective-permute-done.14
  39.8 0.1 collective-permute-start.15
  39.8 2.7 %collective-permute-start.17 = (bf16[2048,128]{1,0:T(8,128)(2,1)S(1)}, bf16[2048,128]{1,0:T(8,128)(2,1)S(1)}, u32[]{:S(2)}, u32[]{:S(2)}) collective-permute-start(bf16[2048,128]{1,0:T(8,128)(2,1)S(1)} %constant_dynamic-update-slice_fusion.9.refs_0_), channel_id=1, source_target_pairs={{0,96},{4,28},{8,104},{12,4},{16,112},{20,12},{24,120},{28,20},{32... | collective-permute-start | bytes 1572872 | tf_op jit(solution)/shard_map/ppermute | solution.py:398
  42.5 4.0 %attend_new.2 = (f32[2048,128]{1,0:T(8,128)S(1)}, f32[2048,128]{1,0:T(8,128)S(1)}, f32[2048,128]{1,0:T(8,128)S(1)}) custom-call(bf16[1024,128]{1,0:T(8,128)(2,1)S(1)} %get-tuple-element.44.own_queries, bf16[1024,128]{1,0:T(8,128)(2,1)S(1)} %collective-permute-done.1.received, bf16[2048,128]{1,0:T(8,128)(2,1)S(1)} %constant_dynamic-update-slice_fusion.9.refs_0_, ...), custom_call_target="tpu_custom_call" | custom-call | flops 110000000 | bytes 350000 | tf_op jit(solution)/shard_map/attend_new/pallas_call | solution.py:334
  46.5 2.8 %collective-permute-done.15.refs_0_ = bf16[2048,128]{1,0:T(8,128)(2,1)S(1)} collective-permute-done((bf16[2048,128]{1,0:T(8,128)(2,1)S(1)}, bf16[2048,128]{1,0:T(8,128)(2,1)S(1)}, u32[]{:S(2)}, u32[]{:S(2)}) %collective-permute-start.15) | collective-permute-done | bytes 524320 | tf_op jit(solution)/shard_map/ppermute | solution.py:398
  49.4 0.0 collective-permute-start.16
  49.4 0.0 collective-permute-done.17.refs_1_
  49.4 5.1 %attend_new.3 = (f32[2048,128]{1,0:T(8,128)S(1)}, f32[2048,128]{1,0:T(8,128)S(1)}, f32[2048,128]{1,0:T(8,128)S(1)}) custom-call(bf16[1024,128]{1,0:T(8,128)(2,1)S(1)} %get-tuple-element.44.own_queries, bf16[1024,128]{1,0:T(8,128)(2,1)S(1)} %collective-permute-done.1.received, bf16[2048,128]{1,0:T(8,128)(2,1)S(1)} %collective-permute-done.15.refs_0_, ...), custom_call_target="tpu_custom_call" | custom-call | flops 110000000 | bytes 350000 | tf_op jit(solution)/shard_map/attend_new/pallas_call | solution.py:334
  54.5 4.7 %collective-permute-done.16.refs_0_ = bf16[2048,128]{1,0:T(8,128)(2,1)S(1)} collective-permute-done((bf16[2048,128]{1,0:T(8,128)(2,1)S(1)}, bf16[2048,128]{1,0:T(8,128)(2,1)S(1)}, u32[]{:S(2)}, u32[]{:S(2)}) %collective-permute-start.16) | collective-permute-done | bytes 524320 | tf_op jit(solution)/shard_map/ppermute | solution.py:402
  59.2 3.2 %attend_new_last.1 = (bf16[128,1024]{1,0:T(8,128)(2,1)S(1)}, bf16[128,1024]{1,0:T(8,128)(2,1)S(1)}) custom-call(bf16[1024,128]{1,0:T(8,128)(2,1)S(1)} %get-tuple-element.44.own_queries, bf16[1024,128]{1,0:T(8,128)(2,1)S(1)} %collective-permute-done.1.received, bf16[2048,128]{1,0:T(8,128)(2,1)S(1)} %collective-permute-done.16.refs_0_, ...), custom_call_target="tpu_custom_call" | custom-call | flops 110000000 | bytes 350000 | tf_op jit(solution)/shard_map/attend_new_last/pallas_call | solution.py:334
  62.5 3.7 %collective-permute-start.18 = (bf16[128,1024]{1,0:T(8,128)(2,1)S(1)}, bf16[128,1024]{1,0:T(8,128)(2,1)S(1)}, u32[]{:S(2)}, u32[]{:S(2)}) collective-permute-start(bf16[128,1024]{1,0:T(8,128)(2,1)S(1)} %get-tuple-element.58), channel_id=1, source_target_pairs={{0,4},{4,0},{8,12},{12,8},{16,20},{20,16},{24,28},{28,24},{32,36},... | collective-permute-start | bytes 786440 | tf_op jit(solution)/shard_map/ppermute | solution.py:406
  66.1 1.2 %collective-permute-done.18.other = bf16[128,1024]{1,0:T(8,128)(2,1)S(1)} collective-permute-done((bf16[128,1024]{1,0:T(8,128)(2,1)S(1)}, bf16[128,1024]{1,0:T(8,128)(2,1)S(1)}, u32[]{:S(2)}, u32[]{:S(2)}) %collective-permute-start.18) | collective-permute-done | bytes 262176 | tf_op jit(solution)/shard_map/ppermute | solution.py:406
  67.3 0.9 %finish.1 = (bf16[128,2048]{1,0:T(8,128)(2,1)}, bf16[128,256]{1,0:T(8,128)(2,1)}, bf16[128,256]{1,0:T(8,128)(2,1)}) custom-call(bf16[128,1024]{1,0:T(8,128)(2,1)S(1)} %get-tuple-element.57.here, bf16[128,1024]{1,0:T(8,128)(2,1)S(1)} %collective-permute-done.18.other, bf16[128,256]{1,0:T(8,128)(2,1)S(1)} %get-tuple-element.59.keys, ...), custom_call_target="tpu_custom_call" | custom-call | flops 110000000 | bytes 350000 | tf_op jit(solution)/shard_map/finish/pallas_call | solution.py:374
  (15 shorter events, 0.2 us)
Async XLA Ops:
  0.6 0.8 %copy-start.3 = (bf16[128,256]{1,0:T(8,128)(2,1)S(1)}, bf16[128,256]{1,0:T(8,128)(2,1)}, u32[]{:S(2)}) copy-start(bf16[128,256]{1,0:T(8,128)(2,1)} %refs_0_.2) | copy-start | bytes 196612
  1.5 0.8 %copy-start.4 = (bf16[128,256]{1,0:T(8,128)(2,1)S(1)}, bf16[128,256]{1,0:T(8,128)(2,1)}, u32[]{:S(2)}) copy-start(bf16[128,256]{1,0:T(8,128)(2,1)} %refs_1_.1) | copy-start | bytes 196612
  2.3 3.3 %collective-permute-start = (bf16[256,128]{1,0:T(8,128)(2,1)S(1)}, bf16[256,128]{1,0:T(8,128)(2,1)S(1)}, u32[]{:S(2)}, u32[]{:S(2)}) collective-permute-start(bf16[256,128]{1,0:T(8,128)(2,1)S(1)} %get-tuple-element.33), channel_id=1, source_target_pairs={{0,4},{4,0},{8,12},{12,8},{16,20},{20,16},{24,28},{28,24},{32,36},... | collective-permute-start | bytes 196616 | tf_op jit(solution)/shard_map/ppermute | solution.py:406
  3.1 14.2 %collective-permute-start.2 = (bf16[32,8192]{1,0:T(8,128)(2,1)}, bf16[32,8192]{1,0:T(8,128)(2,1)S(1)}, u32[]{:S(2)}, u32[]{:S(2)}) collective-permute-start(bf16[32,8192]{1,0:T(8,128)(2,1)} %refs_0_.4), channel_id=1, source_target_pairs={{0,1},{1,2},{2,3},{3,0},{4,7},{5,4},{6,5},{7,6},{8,9},{9,10},{10,1... | collective-permute-start | bytes 1572872 | tf_op jit(solution)/shard_map/ppermute | solution.py:413
  5.7 13.7 %slice-start = ((s8[8388608]{0:T(1024)(128)(4,1)}), s8[4194304]{0:T(1024)(128)(4,1)S(1)}, s32[]{:S(2)}) async-start(s8[8388608]{0:T(1024)(128)(4,1)} %bitcast), calls=%async_computation | async-start | bytes 8388608
  5.7 13.7 %slice-start.1 = ((s8[8388608]{0:T(1024)(128)(4,1)}), s8[4194304]{0:T(1024)(128)(4,1)S(1)}, s32[]{:S(2)}) async-start(s8[8388608]{0:T(1024)(128)(4,1)} %bitcast), calls=%async_computation.1 | async-start | bytes 8388608
  5.7 10.0 %collective-permute-start.8 = (bf16[512,128]{1,0:T(8,128)(2,1)S(1)}, bf16[512,128]{1,0:T(8,128)(2,1)S(1)}, u32[]{:S(2)}, u32[]{:S(2)}) collective-permute-start(bf16[512,128]{1,0:T(8,128)(2,1)S(1)} %get-tuple-element.62), channel_id=1, source_target_pairs={{0,16},{4,68},{8,24},{12,76},{16,0},{20,84},{24,8},{28,92},{32,48}... | collective-permute-start | bytes 393224 | tf_op jit(solution)/shard_map/ppermute | solution.py:393
  6.7 8.9 %collective-permute-start.7 = (bf16[512,128]{1,0:T(8,128)(2,1)S(1)}, bf16[512,128]{1,0:T(8,128)(2,1)S(1)}, u32[]{:S(2)}, u32[]{:S(2)}) collective-permute-start(bf16[512,128]{1,0:T(8,128)(2,1)S(1)} %get-tuple-element.62), channel_id=1, source_target_pairs={{0,24},{4,100},{8,0},{12,108},{16,8},{20,116},{24,16},{28,124},{32... | collective-permute-start | bytes 393224 | tf_op jit(solution)/shard_map/ppermute | solution.py:393
  6.7 4.6 %collective-permute-start.6 = (bf16[512,128]{1,0:T(8,128)(2,1)S(1)}, bf16[512,128]{1,0:T(8,128)(2,1)S(1)}, u32[]{:S(2)}, u32[]{:S(2)}) collective-permute-start(bf16[512,128]{1,0:T(8,128)(2,1)S(1)} %get-tuple-element.62), channel_id=1, source_target_pairs={{0,8},{4,36},{8,16},{12,44},{16,24},{20,52},{24,0},{28,60},{32,40}... | collective-permute-start | bytes 393224 | tf_op jit(solution)/shard_map/ppermute | solution.py:393
  9.4 10.0 %collective-permute-start.4 = (bf16[32,8192]{1,0:T(8,128)(2,1)}, bf16[32,8192]{1,0:T(8,128)(2,1)S(1)}, u32[]{:S(2)}, u32[]{:S(2)}) collective-permute-start(bf16[32,8192]{1,0:T(8,128)(2,1)} %refs_0_.4), channel_id=1, source_target_pairs={{0,3},{1,0},{2,1},{3,2},{4,5},{5,6},{6,7},{7,4},{8,11},{9,8},{10,9... | collective-permute-start | bytes 1572872 | tf_op jit(solution)/shard_map/ppermute | solution.py:416
  9.4 1.0 %copy-start.1 = (bf16[128,2048]{1,0:T(8,128)(2,1)S(1)}, bf16[128,2048]{1,0:T(8,128)(2,1)}, u32[]{:S(2)}) copy-start(bf16[128,2048]{1,0:T(8,128)(2,1)} %refs_0_.3) | copy-start | bytes 1572868
  10.4 8.9 %copy-start.2 = (bf16[32,8192]{1,0:T(8,128)(2,1)S(1)}, bf16[32,8192]{1,0:T(8,128)(2,1)}, u32[]{:S(2)}) copy-start(bf16[32,8192]{1,0:T(8,128)(2,1)} %refs_0_.4) | copy-start | bytes 1572868
  11.3 13.4 %collective-permute-start.1 = (bf16[1024,128]{1,0:T(8,128)(2,1)S(1)}, bf16[1024,128]{1,0:T(8,128)(2,1)S(1)}, u32[]{:S(2)}, u32[]{:S(2)}) collective-permute-start(bf16[1024,128]{1,0:T(8,128)(2,1)S(1)} %get-tuple-element.36), channel_id=1, source_target_pairs={{0,4},{4,0},{8,12},{12,8},{16,20},{20,16},{24,28},{28,24},{32,36},... | collective-permute-start | bytes 786440 | tf_op jit(solution)/shard_map/ppermute | solution.py:406
  15.7 17.4 %collective-permute-start.10 = (bf16[2048,128]{1,0:T(8,128)(2,1)S(1)}, bf16[2048,128]{1,0:T(8,128)(2,1)S(1)}, u32[]{:S(2)}, u32[]{:S(2)}) collective-permute-start(bf16[2048,128]{1,0:T(8,128)(2,1)S(1)} %constant_dynamic-update-slice_fusion.4.refs_0_), channel_id=1, source_target_pairs={{0,96},{4,28},{8,104},{12,4},{16,112},{20,12},{24,120},{28,20},{32... | collective-permute-start | bytes 1572872 | tf_op jit(solution)/shard_map/ppermute | solution.py:398
  16.7 16.9 %collective-permute-start.9 = (bf16[2048,128]{1,0:T(8,128)(2,1)S(1)}, bf16[2048,128]{1,0:T(8,128)(2,1)S(1)}, u32[]{:S(2)}, u32[]{:S(2)}) collective-permute-start(bf16[2048,128]{1,0:T(8,128)(2,1)S(1)} %constant_dynamic-update-slice_fusion.4.refs_0_), channel_id=1, source_target_pairs={{0,32},{4,12},{8,40},{12,20},{16,48},{20,28},{24,56},{28,4},{32,64... | collective-permute-start | bytes 1572872 | tf_op jit(solution)/shard_map/ppermute | solution.py:398
  17.3 8.3 %collective-permute-start.3 = (bf16[32,8192]{1,0:T(8,128)(2,1)S(1)}, bf16[32,8192]{1,0:T(8,128)(2,1)S(1)}, u32[]{:S(2)}, u32[]{:S(2)}) collective-permute-start(bf16[32,8192]{1,0:T(8,128)(2,1)S(1)} %collective-permute-done.2.refs_1_), channel_id=1, source_target_pairs={{0,1},{1,2},{2,3},{3,0},{4,7},{5,4},{6,5},{7,6},{8,9},{9,10},{10,1... | collective-permute-start | bytes 1572872 | tf_op jit(solution)/shard_map/ppermute | solution.py:420
  20.8 12.8 %copy-start = (s32[32]{0:T(128)S(1)}, s32[32]{0:T(128)}, u32[]{:S(2)}) copy-start(s32[32]{0:T(128)} %kv_blocks.1) | copy-start | bytes 388
  20.9 12.7 %collective-permute-start.11 = (bf16[2048,128]{1,0:T(8,128)(2,1)S(1)}, bf16[2048,128]{1,0:T(8,128)(2,1)S(1)}, u32[]{:S(2)}, u32[]{:S(2)}) collective-permute-start(bf16[2048,128]{1,0:T(8,128)(2,1)S(1)} %constant_dynamic-update-slice_fusion.4.refs_0_), channel_id=1, source_target_pairs={{0,64},{4,20},{8,72},{12,28},{16,80},{20,4},{24,88},{28,12},{32,96... | collective-permute-start | bytes 1572872 | tf_op jit(solution)/shard_map/ppermute | solution.py:402
  27.2 4.8 %collective-permute-start.5 = (bf16[256,128]{1,0:T(8,128)(2,1)S(1)}, bf16[256,128]{1,0:T(8,128)(2,1)S(1)}, u32[]{:S(2)}, u32[]{:S(2)}) collective-permute-start(bf16[256,128]{1,0:T(8,128)(2,1)S(1)} %get-tuple-element.43), channel_id=1, source_target_pairs={{0,4},{4,0},{8,12},{12,8},{16,20},{20,16},{24,28},{28,24},{32,36},... | collective-permute-start | bytes 196616 | tf_op jit(solution)/shard_map/ppermute | solution.py:406
  32.0 7.6 %collective-permute-start.12 = (bf16[512,128]{1,0:T(8,128)(2,1)S(1)}, bf16[512,128]{1,0:T(8,128)(2,1)S(1)}, u32[]{:S(2)}, u32[]{:S(2)}) collective-permute-start(bf16[512,128]{1,0:T(8,128)(2,1)S(1)} %constant_dynamic-update-slice_fusion.2), channel_id=1, source_target_pairs={{0,8},{4,36},{8,16},{12,44},{16,24},{20,52},{24,0},{28,60},{32,40}... | collective-permute-start | bytes 393224 | tf_op jit(solution)/shard_map/ppermute | solution.py:393
  32.1 7.6 %collective-permute-start.14 = (bf16[512,128]{1,0:T(8,128)(2,1)S(1)}, bf16[512,128]{1,0:T(8,128)(2,1)S(1)}, u32[]{:S(2)}, u32[]{:S(2)}) collective-permute-start(bf16[512,128]{1,0:T(8,128)(2,1)S(1)} %constant_dynamic-update-slice_fusion.2), channel_id=1, source_target_pairs={{0,16},{4,68},{8,24},{12,76},{16,0},{20,84},{24,8},{28,92},{32,48}... | collective-permute-start | bytes 393224 | tf_op jit(solution)/shard_map/ppermute | solution.py:393
  33.2 6.5 %collective-permute-start.13 = (bf16[512,128]{1,0:T(8,128)(2,1)S(1)}, bf16[512,128]{1,0:T(8,128)(2,1)S(1)}, u32[]{:S(2)}, u32[]{:S(2)}) collective-permute-start(bf16[512,128]{1,0:T(8,128)(2,1)S(1)} %constant_dynamic-update-slice_fusion.2), channel_id=1, source_target_pairs={{0,24},{4,100},{8,0},{12,108},{16,8},{20,116},{24,16},{28,124},{32... | collective-permute-start | bytes 393224 | tf_op jit(solution)/shard_map/ppermute | solution.py:393
  39.8 9.6 %collective-permute-start.15 = (bf16[2048,128]{1,0:T(8,128)(2,1)S(1)}, bf16[2048,128]{1,0:T(8,128)(2,1)S(1)}, u32[]{:S(2)}, u32[]{:S(2)}) collective-permute-start(bf16[2048,128]{1,0:T(8,128)(2,1)S(1)} %constant_dynamic-update-slice_fusion.9.refs_0_), channel_id=1, source_target_pairs={{0,32},{4,12},{8,40},{12,20},{16,48},{20,28},{24,56},{28,4},{32,64... | collective-permute-start | bytes 1572872 | tf_op jit(solution)/shard_map/ppermute | solution.py:398
  39.8 9.5 %collective-permute-start.17 = (bf16[2048,128]{1,0:T(8,128)(2,1)S(1)}, bf16[2048,128]{1,0:T(8,128)(2,1)S(1)}, u32[]{:S(2)}, u32[]{:S(2)}) collective-permute-start(bf16[2048,128]{1,0:T(8,128)(2,1)S(1)} %constant_dynamic-update-slice_fusion.9.refs_0_), channel_id=1, source_target_pairs={{0,96},{4,28},{8,104},{12,4},{16,112},{20,12},{24,120},{28,20},{32... | collective-permute-start | bytes 1572872 | tf_op jit(solution)/shard_map/ppermute | solution.py:398
  49.4 9.8 %collective-permute-start.16 = (bf16[2048,128]{1,0:T(8,128)(2,1)S(1)}, bf16[2048,128]{1,0:T(8,128)(2,1)S(1)}, u32[]{:S(2)}, u32[]{:S(2)}) collective-permute-start(bf16[2048,128]{1,0:T(8,128)(2,1)S(1)} %constant_dynamic-update-slice_fusion.9.refs_0_), channel_id=1, source_target_pairs={{0,64},{4,20},{8,72},{12,28},{16,80},{20,4},{24,88},{28,12},{32,96... | collective-permute-start | bytes 1572872 | tf_op jit(solution)/shard_map/ppermute | solution.py:402
  62.5 4.9 %collective-permute-start.18 = (bf16[128,1024]{1,0:T(8,128)(2,1)S(1)}, bf16[128,1024]{1,0:T(8,128)(2,1)S(1)}, u32[]{:S(2)}, u32[]{:S(2)}) collective-permute-start(bf16[128,1024]{1,0:T(8,128)(2,1)S(1)} %get-tuple-element.58), channel_id=1, source_target_pairs={{0,4},{4,0},{8,12},{12,8},{16,20},{20,16},{24,28},{28,24},{32,36},... | collective-permute-start | bytes 786440 | tf_op jit(solution)/shard_map/ppermute | solution.py:406

commit v6 on v5

--- a/solution.py
+++ b/solution.py
@@ -206,7 +206,8 @@
 
 
 def cache_kernel(live_keys, kv_blocks, own_queries, received, *refs):
-    pieces, states, (keys, values, turned) = refs[:4], refs[4:7], refs[7:]
+    pieces, states, (turned, rest), (keys, values) = refs[:4], refs[4:7], refs[7:9], refs[9:]
+    first = live_keys - rest.shape[0]
     core, _, _ = place()
     at = jnp.int32(0)
     for piece in range(SIDE):
@@ -221,26 +222,54 @@
                 at = at + kv_blocks[group] * BLOCK
     for i in range(0, live_keys, 256):
         turned[:, i : i + 256] = keys[i : i + 256, :].T
+    rest[...] = values[first:live_keys, :]
     for _, start, query in tiles(own_queries, received):
         zero = jnp.zeros((TILE, HEAD_DIM), F32)
         state = (jnp.full((TILE, HEAD_DIM), -1e30, F32), zero, zero)
-        state = absorb(query(), turned[...], values[:live_keys, :], state)
+        state = absorb(query(), turned[:, :first], values[:first, :], state)
         for ref, value in zip(states, state):
             ref[start : start + TILE, :] = value
 
 
-def attend_cache(kv_blocks, own_queries, received, pieces, live_keys):
+def attend_cache(kv_blocks, own_queries, received, pieces, live_keys, later):
     held = pltpu.VMEM((live_keys + ROWS, HEAD_DIM), BF16)
     return pl.pallas_call(
         functools.partial(cache_kernel, live_keys),
-        out_shape=(STATE,) * 3,
+        out_shape=(STATE,) * 3
+        + (
+            jax.ShapeDtypeStruct((HEAD_DIM, live_keys), BF16),
+            jax.ShapeDtypeStruct((later, HEAD_DIM), BF16),
+        ),
         in_specs=[SMEM] + [VMEM] * 6,
-        out_specs=(VMEM,) * 3,
-        scratch_shapes=[held, held, pltpu.VMEM((HEAD_DIM, live_keys), BF16)],
+        out_specs=(VMEM,) * 5,
+        scratch_shapes=[held, held],
         compiler_params=pltpu.CompilerParams(vmem_limit_bytes=24 << 20),
         cost_estimate=cost(0.1),
         name="attend_cache",
     )(kv_blocks, own_queries, received, *pieces)
+
+
+def later_kernel(own_queries, received, turned, values, *refs):
+    olds, states = refs[:3], refs[3:]
+    first = turned.shape[1] - values.shape[0]
+    for _, start, query in tiles(own_queries, received):
+        rows = slice(start, start + TILE)
+        state = tuple(old[rows, :] for old in olds)
+        state = absorb(query(), turned[:, first:], values[...], state)
+        for ref, value in zip(states, state):
+            ref[rows, :] = value
+
+
+def attend_later(own_queries, received, turned, values, states):
+    return pl.pallas_call(
+        later_kernel,
+        out_shape=(STATE,) * 3,
+        in_specs=[VMEM] * 7,
+        out_specs=(VMEM,) * 3,
+        compiler_params=pltpu.CompilerParams(vmem_limit_bytes=24 << 20),
+        cost_estimate=cost(0.1),
+        name="attend_later",
+    )(own_queries, received, turned, values, *states)
 
 
 def new_kernel(which, last, own_queries, received, *refs):
@@ -437,10 +466,13 @@
         jnp.concatenate([-sine, sine], 1),
     )
     block = jnp.concatenate([mine, swapped(give)], 0)
-    states = attend_cache(kv_blocks, after(own_queries, block), received, cache, live_keys)
+    *states, turned, values = attend_cache(
+        kv_blocks, after(own_queries, block), received, cache, live_keys, live_keys // 2
+    )
     joined = first_phase(block, states[0])
     new = second_phase(joined)
     states = attend_new(own_queries, received, (0,), new[:1], states, False)
+    states = attend_later(own_queries, received, turned, values, states)
     new.append(last_phase(joined, states[0], new[1]))
     states = attend_new(own_queries, received, (1, 2), new[1:3], states, False)
     here, there = attend_new(own_queries, received, (3,), new[3:], states, True)

time: 68.6 us -> 67.1 us (0.978)
  waiting for transfers between devices: 11.3 us -> 9.91 us
  starting transfers between devices: 30.2 us -> 29.4 us
  Pallas kernels: 22.4 us -> 23.1 us
    pallas_call x0 -> x1, Pallas kernels: none -> 2.85 us  [attend_later(): pl.pallas_call(later_kernel, out_shape=(STATE,) * 3, in_specs=[VMEM] * 7,...]
    ppermute x4, waiting for transfers between devices: 2.85 us -> 0.15 us  [second_phase(): lax.ppermute(joined, 'group', along(1, d))]
    pallas_call x1, Pallas kernels: 6.02 us -> 3.82 us  [attend_cache(): pl.pallas_call(functools.partial(cache_kernel, live_keys), out_shape=(STA...]
    ppermute x6, waiting for transfers between devices: 0.77 us -> 2.52 us  [first_phase(): sent = [lax.ppermute(block, 'group', along(0, d)) for d in (1, 3, 2)]]
    ppermute x4, starting transfers between devices: 12.6 us -> 11.6 us  [swapped(): return lax.ppermute(block, 'group', swap_cores())]
  transfers between devices with their start and end apart: 19 -> 19, of which waited for: 6 -> 7; matrix products, arithmetic and copies ran while one was open for 1% -> 1% of each run, Pallas kernels for 27% -> 28%
where the time goes in v6:
time: 67.1 us; the launch traced here: 66.9 us
  starting transfers between devices  29.4 us (44%)
  Pallas kernels  23.1 us (34%)
  waiting for transfers between devices  9.91 us (15%)
  local copies, waits for them, and re-layouts  2.91 us (4%)
  between operations  1.08 us (2%)
    pallas_call x3, Pallas kernels, attend_new(): pl.pallas_call(functools.partial(new_kernel, which, last), out_shape=(out...  12.4 us
    ppermute x4, starting transfers between devices, swapped(): return lax.ppermute(block, 'group', swap_cores())  11.6 us
    ppermute x6, starting transfers between devices, first_phase(): sent = [lax.ppermute(block, 'group', along(0, d)) for d in (1, 3, 2)]  5.24 us
    ppermute x2, waiting for transfers between devices, last_phase(): return lax.ppermute(after(joined, *others), 'group', along(1, 2))  4.31 us
    ppermute x4, starting transfers between devices, second_phase(): lax.ppermute(joined, 'group', along(1, d))  4.27 us
    pallas_call x1, Pallas kernels, attend_cache(): pl.pallas_call(functools.partial(cache_kernel, live_keys), out_shape=(STA...  3.82 us
    ppermute x2, starting transfers between devices, last_phase(): return lax.ppermute(after(joined, *others), 'group', along(1, 2))  3.68 us
    unnamed x22, local copies, waits for them, and re-layouts  2.86 us
  transfers between devices with their start and end apart: 19, of which 7 were waited for; matrix products, arithmetic and copies ran while one was open for 1% of the time, Pallas kernels for 28%

profile of v6, /device:TPU:25, one launch (start us, length us, event | category | flops | bytes accessed | tf_op | source)
XLA Modules:
  0.0 66.9 jit_solution(15580295543771671893)
XLA Ops:
  0.6 0.0 copy-start.3
  0.6 0.8 %copy-done.3 = bf16[128,256]{1,0:T(8,128)(2,1)S(1)} copy-done((bf16[128,256]{1,0:T(8,128)(2,1)S(1)}, bf16[128,256]{1,0:T(8,128)(2,1)}, u32[]{:S(2)}) %copy-start.3) | copy-done | bytes 65560
  1.5 0.0 copy-start.4
  1.5 0.8 %copy-done.4 = bf16[128,256]{1,0:T(8,128)(2,1)S(1)} copy-done((bf16[128,256]{1,0:T(8,128)(2,1)S(1)}, bf16[128,256]{1,0:T(8,128)(2,1)}, u32[]{:S(2)}) %copy-start.4) | copy-done | bytes 65560
  2.3 0.8 %collective-permute-start = (bf16[256,128]{1,0:T(8,128)(2,1)S(1)}, bf16[256,128]{1,0:T(8,128)(2,1)S(1)}, u32[]{:S(2)}, u32[]{:S(2)}) collective-permute-start(bf16[256,128]{1,0:T(8,128)(2,1)S(1)} %get-tuple-element.38), channel_id=1, source_target_pairs={{0,4},{4,0},{8,12},{12,8},{16,20},{20,16},{24,28},{28,24},{32,36},... | collective-permute-start | bytes 196616 | tf_op jit(solution)/shard_map/ppermute | solution.py:435
  3.1 2.5 %collective-permute-start.2 = (bf16[32,8192]{1,0:T(8,128)(2,1)}, bf16[32,8192]{1,0:T(8,128)(2,1)S(1)}, u32[]{:S(2)}, u32[]{:S(2)}) collective-permute-start(bf16[32,8192]{1,0:T(8,128)(2,1)} %refs_0_.4), channel_id=1, source_target_pairs={{0,1},{1,2},{2,3},{3,0},{4,7},{5,4},{6,5},{7,6},{8,9},{9,10},{10,1... | collective-permute-start | bytes 1572872 | tf_op jit(solution)/shard_map/ppermute | solution.py:442
  5.6 0.0 collective-permute-done
  5.7 0.0 slice-start
  5.7 0.0 slice-start.1
  5.7 1.0 %collective-permute-start.8 = (bf16[512,128]{1,0:T(8,128)(2,1)S(1)}, bf16[512,128]{1,0:T(8,128)(2,1)S(1)}, u32[]{:S(2)}, u32[]{:S(2)}) collective-permute-start(bf16[512,128]{1,0:T(8,128)(2,1)S(1)} %get-tuple-element.72), channel_id=1, source_target_pairs={{0,16},{4,68},{8,24},{12,76},{16,0},{20,84},{24,8},{28,92},{32,48}... | collective-permute-start | bytes 393224 | tf_op jit(solution)/shard_map/ppermute | solution.py:422
  6.7 0.0 collective-permute-start.7
  6.7 2.7 %collective-permute-start.6 = (bf16[512,128]{1,0:T(8,128)(2,1)S(1)}, bf16[512,128]{1,0:T(8,128)(2,1)S(1)}, u32[]{:S(2)}, u32[]{:S(2)}) collective-permute-start(bf16[512,128]{1,0:T(8,128)(2,1)S(1)} %get-tuple-element.72), channel_id=1, source_target_pairs={{0,8},{4,36},{8,16},{12,44},{16,24},{20,52},{24,0},{28,60},{32,40}... | collective-permute-start | bytes 393224 | tf_op jit(solution)/shard_map/ppermute | solution.py:422
  9.4 0.0 collective-permute-start.4
  9.4 0.0 copy-start.1
  9.4 1.0 %copy-done.1 = bf16[128,2048]{1,0:T(8,128)(2,1)S(1)} copy-done((bf16[128,2048]{1,0:T(8,128)(2,1)S(1)}, bf16[128,2048]{1,0:T(8,128)(2,1)}, u32[]{:S(2)}) %copy-start.1) | copy-done | bytes 524312
  10.4 0.0 copy-start.2
  10.4 0.1 heads.3
  10.6 0.8 %collective-permute-done.6 = bf16[512,128]{1,0:T(8,128)(2,1)S(1)} collective-permute-done((bf16[512,128]{1,0:T(8,128)(2,1)S(1)}, bf16[512,128]{1,0:T(8,128)(2,1)S(1)}, u32[]{:S(2)}, u32[]{:S(2)}) %collective-permute-start.6) | collective-permute-done | bytes 131104 | tf_op jit(solution)/shard_map/ppermute | solution.py:422
  11.3 4.3 %collective-permute-start.1 = (bf16[1024,128]{1,0:T(8,128)(2,1)S(1)}, bf16[1024,128]{1,0:T(8,128)(2,1)S(1)}, u32[]{:S(2)}, u32[]{:S(2)}) collective-permute-start(bf16[1024,128]{1,0:T(8,128)(2,1)S(1)} %get-tuple-element.41), channel_id=1, source_target_pairs={{0,4},{4,0},{8,12},{12,8},{16,20},{20,16},{24,28},{28,24},{32,36},... | collective-permute-start | bytes 786440 | tf_op jit(solution)/shard_map/ppermute | solution.py:435
  15.6 0.0 collective-permute-done.7
  15.7 0.0 collective-permute-done.8
  15.7 0.9 %collective-permute-start.10 = (bf16[2048,128]{1,0:T(8,128)(2,1)S(1)}, bf16[2048,128]{1,0:T(8,128)(2,1)S(1)}, u32[]{:S(2)}, u32[]{:S(2)}) collective-permute-start(bf16[2048,128]{1,0:T(8,128)(2,1)S(1)} %constant_dynamic-update-slice_fusion.4.refs_0_), channel_id=1, source_target_pairs={{0,96},{4,28},{8,104},{12,4},{16,112},{20,12},{24,120},{28,20},{32... | collective-permute-start | bytes 1572872 | tf_op jit(solution)/shard_map/ppermute | solution.py:427
  16.7 0.6 collective-permute-start.9
  17.3 0.0 collective-permute-done.2.refs_1_
  17.3 2.1 %collective-permute-start.3 = (bf16[32,8192]{1,0:T(8,128)(2,1)S(1)}, bf16[32,8192]{1,0:T(8,128)(2,1)S(1)}, u32[]{:S(2)}, u32[]{:S(2)}) collective-permute-start(bf16[32,8192]{1,0:T(8,128)(2,1)S(1)} %collective-permute-done.2.refs_1_), channel_id=1, source_target_pairs={{0,1},{1,2},{2,3},{3,0},{4,7},{5,4},{6,5},{7,6},{8,9},{9,10},{10,1... | collective-permute-start | bytes 1572872 | tf_op jit(solution)/shard_map/ppermute | solution.py:449
  19.4 0.0 collective-permute-done.4.refs_2_
  19.4 0.0 slice-done
  19.4 0.0 slice-done.1
  19.4 0.0 copy-done.2
  19.4 1.4 %project_near.1 = (f32[96,256]{1,0:T(8,128)S(1)}, f32[96,256]{1,0:T(8,128)S(1)}) custom-call(bf16[32,8192]{1,0:T(8,128)(2,1)S(1)} %copy-done.2, bf16[32,8192]{1,0:T(8,128)(2,1)S(1)} %collective-permute-done.2.refs_1_, bf16[32,8192]{1,0:T(8,128)(2,1)S(1)} %collective-permute-done.4.refs_2_, bf16[2,8192,256]{2,1,0:T(8,128)(2,1)S(1)} %bitcast.1), custom_call_target="tpu_custom_call" | custom-call | flops 22000001024 | bytes 70000000 | tf_op jit(solution)/shard_map/project_near/pallas_call | solution.py:121
  20.8 0.0 copy-start
  20.9 3.4 %collective-permute-start.11 = (bf16[2048,128]{1,0:T(8,128)(2,1)S(1)}, bf16[2048,128]{1,0:T(8,128)(2,1)S(1)}, u32[]{:S(2)}, u32[]{:S(2)}) collective-permute-start(bf16[2048,128]{1,0:T(8,128)(2,1)S(1)} %constant_dynamic-update-slice_fusion.4.refs_0_), channel_id=1, source_target_pairs={{0,64},{4,20},{8,72},{12,28},{16,80},{20,4},{24,88},{28,12},{32,96... | collective-permute-start | bytes 1572872 | tf_op jit(solution)/shard_map/ppermute | solution.py:431
  24.3 0.3 fusion
  24.6 0.1 pad_maximum_fusion
  24.7 0.0 collective-permute-done.1.received
  24.7 0.9 %collective-permute-done.3.piece = bf16[32,8192]{1,0:T(8,128)(2,1)S(1)} collective-permute-done((bf16[32,8192]{1,0:T(8,128)(2,1)S(1)}, bf16[32,8192]{1,0:T(8,128)(2,1)S(1)}, u32[]{:S(2)}, u32[]{:S(2)}) %collective-permute-start.3) | collective-permute-done | bytes 524320 | tf_op jit(solution)/shard_map/ppermute | solution.py:449
  25.6 1.6 %project_far.1 = (bf16[128,256]{1,0:T(8,128)(2,1)S(1)}, bf16[128,256]{1,0:T(8,128)(2,1)S(1)}, bf16[256,128]{1,0:T(8,128)(2,1)S(1)}, bf16[256,128]{1,0:T(8,128)(2,1)S(1)}) custom-call(bf16[32,8192]{1,0:T(8,128)(2,1)S(1)} %collective-permute-done.3.piece, f32[96,256]{1,0:T(8,128)S(1)} %get-tuple-element.45.near_keys, ...), custom_call_target="tpu_custom_call" | custom-call | flops 110000000 | bytes 350000 | tf_op jit(solution)/shard_map/project_far/pallas_call | solution.py:164
  27.2 3.9 %collective-permute-start.5 = (bf16[256,128]{1,0:T(8,128)(2,1)S(1)}, bf16[256,128]{1,0:T(8,128)(2,1)S(1)}, u32[]{:S(2)}, u32[]{:S(2)}) collective-permute-start(bf16[256,128]{1,0:T(8,128)(2,1)S(1)} %get-tuple-element.48), channel_id=1, source_target_pairs={{0,4},{4,0},{8,12},{12,8},{16,20},{20,16},{24,28},{28,24},{32,36},... | collective-permute-start | bytes 196616 | tf_op jit(solution)/shard_map/ppermute | solution.py:435
  31.1 0.9 %collective-permute-done.5 = bf16[256,128]{1,0:T(8,128)(2,1)S(1)} collective-permute-done((bf16[256,128]{1,0:T(8,128)(2,1)S(1)}, bf16[256,128]{1,0:T(8,128)(2,1)S(1)}, u32[]{:S(2)}, u32[]{:S(2)}) %collective-permute-start.5) | collective-permute-done | bytes 65568 | tf_op jit(solution)/shard_map/ppermute | solution.py:435
  32.0 0.1 collective-permute-start.12
  32.1 1.0 %collective-permute-start.14 = (bf16[512,128]{1,0:T(8,128)(2,1)S(1)}, bf16[512,128]{1,0:T(8,128)(2,1)S(1)}, u32[]{:S(2)}, u32[]{:S(2)}) collective-permute-start(bf16[512,128]{1,0:T(8,128)(2,1)S(1)} %constant_dynamic-update-slice_fusion.2), channel_id=1, source_target_pairs={{0,16},{4,68},{8,24},{12,76},{16,0},{20,84},{24,8},{28,92},{32,48}... | collective-permute-start | bytes 393224 | tf_op jit(solution)/shard_map/ppermute | solution.py:422
  33.2 0.0 collective-permute-done.10.refs_2_
  33.2 0.4 collective-permute-start.13
  33.6 0.0 collective-permute-done.9.refs_1_
  33.6 0.0 collective-permute-done.11.refs_3_
  33.6 0.0 copy-done
  33.6 3.8 %attend_cache.1 = (f32[2048,128]{1,0:T(8,128)S(1)}, f32[2048,128]{1,0:T(8,128)S(1)}, f32[2048,128]{1,0:T(8,128)S(1)}, bf16[128,2048]{1,0:T(8,128)(2,1)S(1)}, bf16[1024,128]{1,0:T(8,128)(2,1)S(1)}) custom-call(s32[32]{0:T(128)S(1)} %copy-done, bf16[1024,128]{1,0:T(8,128)(2,1)S(1)} %get-tuple-element.49.own_queries, ...), custom_call_target="tpu_custom_call" | custom-call | flops 110000000 | bytes 350000 | tf_op jit(solution)/shard_map/attend_cache/pallas_call | solution.py:236
  37.4 0.0 collective-permute-done.12
  37.5 1.7 %collective-permute-done.13 = bf16[512,128]{1,0:T(8,128)(2,1)S(1)} collective-permute-done((bf16[512,128]{1,0:T(8,128)(2,1)S(1)}, bf16[512,128]{1,0:T(8,128)(2,1)S(1)}, u32[]{:S(2)}, u32[]{:S(2)}) %collective-permute-start.13) | collective-permute-done | bytes 131104 | tf_op jit(solution)/shard_map/ppermute | solution.py:422
  39.3 0.0 collective-permute-done.14
  39.3 0.1 collective-permute-start.15
  39.4 2.7 %collective-permute-start.17 = (bf16[2048,128]{1,0:T(8,128)(2,1)S(1)}, bf16[2048,128]{1,0:T(8,128)(2,1)S(1)}, u32[]{:S(2)}, u32[]{:S(2)}) collective-permute-start(bf16[2048,128]{1,0:T(8,128)(2,1)S(1)} %constant_dynamic-update-slice_fusion.9.refs_0_), channel_id=1, source_target_pairs={{0,96},{4,28},{8,104},{12,4},{16,112},{20,12},{24,120},{28,20},{32... | collective-permute-start | bytes 1572872 | tf_op jit(solution)/shard_map/ppermute | solution.py:427
  42.0 3.9 %attend_new.2 = (f32[2048,128]{1,0:T(8,128)S(1)}, f32[2048,128]{1,0:T(8,128)S(1)}, f32[2048,128]{1,0:T(8,128)S(1)}) custom-call(bf16[1024,128]{1,0:T(8,128)(2,1)S(1)} %get-tuple-element.49.own_queries, bf16[1024,128]{1,0:T(8,128)(2,1)S(1)} %collective-permute-done.1.received, bf16[2048,128]{1,0:T(8,128)(2,1)S(1)} %constant_dynamic-update-slice_fusion.9.refs_0_, ...), custom_call_target="tpu_custom_call" | custom-call | flops 110000000 | bytes 350000 | tf_op jit(solution)/shard_map/attend_new/pallas_call | solution.py:363
  45.9 2.9 %attend_later.1 = (f32[2048,128]{1,0:T(8,128)S(1)}, f32[2048,128]{1,0:T(8,128)S(1)}, f32[2048,128]{1,0:T(8,128)S(1)}) custom-call(bf16[1024,128]{1,0:T(8,128)(2,1)S(1)} %get-tuple-element.49.own_queries, bf16[1024,128]{1,0:T(8,128)(2,1)S(1)} %collective-permute-done.1.received, bf16[128,2048]{1,0:T(8,128)(2,1)S(1)} %get-tuple-element.53.turned, ...), custom_call_target="tpu_custom_call" | custom-call | flops 110000000 | bytes 350000 | tf_op jit(solution)/shard_map/attend_later/pallas_call | solution.py:264
  48.8 0.1 collective-permute-done.15.refs_0_
  48.9 0.2 collective-permute-start.16
  49.1 0.0 collective-permute-done.17.refs_1_
  49.1 5.3 %attend_new.3 = (f32[2048,128]{1,0:T(8,128)S(1)}, f32[2048,128]{1,0:T(8,128)S(1)}, f32[2048,128]{1,0:T(8,128)S(1)}) custom-call(bf16[1024,128]{1,0:T(8,128)(2,1)S(1)} %get-tuple-element.49.own_queries, bf16[1024,128]{1,0:T(8,128)(2,1)S(1)} %collective-permute-done.1.received, bf16[2048,128]{1,0:T(8,128)(2,1)S(1)} %collective-permute-done.15.refs_0_, ...), custom_call_target="tpu_custom_call" | custom-call | flops 110000000 | bytes 350000 | tf_op jit(solution)/shard_map/attend_new/pallas_call | solution.py:363
  54.4 4.3 %collective-permute-done.16.refs_0_ = bf16[2048,128]{1,0:T(8,128)(2,1)S(1)} collective-permute-done((bf16[2048,128]{1,0:T(8,128)(2,1)S(1)}, bf16[2048,128]{1,0:T(8,128)(2,1)S(1)}, u32[]{:S(2)}, u32[]{:S(2)}) %collective-permute-start.16) | collective-permute-done | bytes 524320 | tf_op jit(solution)/shard_map/ppermute | solution.py:431
  58.7 3.3 %attend_new_last.1 = (bf16[128,1024]{1,0:T(8,128)(2,1)S(1)}, bf16[128,1024]{1,0:T(8,128)(2,1)S(1)}) custom-call(bf16[1024,128]{1,0:T(8,128)(2,1)S(1)} %get-tuple-element.49.own_queries, bf16[1024,128]{1,0:T(8,128)(2,1)S(1)} %collective-permute-done.1.received, bf16[2048,128]{1,0:T(8,128)(2,1)S(1)} %collective-permute-done.16.refs_0_, ...), custom_call_target="tpu_custom_call" | custom-call | flops 110000000 | bytes 350000 | tf_op jit(solution)/shard_map/attend_new_last/pallas_call | solution.py:363
  62.0 2.7 %collective-permute-start.18 = (bf16[128,1024]{1,0:T(8,128)(2,1)S(1)}, bf16[128,1024]{1,0:T(8,128)(2,1)S(1)}, u32[]{:S(2)}, u32[]{:S(2)}) collective-permute-start(bf16[128,1024]{1,0:T(8,128)(2,1)S(1)} %get-tuple-element.68), channel_id=1, source_target_pairs={{0,4},{4,0},{8,12},{12,8},{16,20},{20,16},{24,28},{28,24},{32,36},... | collective-permute-start | bytes 786440 | tf_op jit(solution)/shard_map/ppermute | solution.py:435
  64.7 1.2 %collective-permute-done.18.other = bf16[128,1024]{1,0:T(8,128)(2,1)S(1)} collective-permute-done((bf16[128,1024]{1,0:T(8,128)(2,1)S(1)}, bf16[128,1024]{1,0:T(8,128)(2,1)S(1)}, u32[]{:S(2)}, u32[]{:S(2)}) %collective-permute-start.18) | collective-permute-done | bytes 262176 | tf_op jit(solution)/shard_map/ppermute | solution.py:435
  65.8 0.9 %finish.1 = (bf16[128,2048]{1,0:T(8,128)(2,1)}, bf16[128,256]{1,0:T(8,128)(2,1)}, bf16[128,256]{1,0:T(8,128)(2,1)}) custom-call(bf16[128,1024]{1,0:T(8,128)(2,1)S(1)} %get-tuple-element.67.here, bf16[128,1024]{1,0:T(8,128)(2,1)S(1)} %collective-permute-done.18.other, bf16[128,256]{1,0:T(8,128)(2,1)S(1)} %get-tuple-element.69.keys, ...), custom_call_target="tpu_custom_call" | custom-call | flops 110000000 | bytes 350000 | tf_op jit(solution)/shard_map/finish/pallas_call | solution.py:403
  (15 shorter events, 0.2 us)
Async XLA Ops:
  0.6 0.8 %copy-start.3 = (bf16[128,256]{1,0:T(8,128)(2,1)S(1)}, bf16[128,256]{1,0:T(8,128)(2,1)}, u32[]{:S(2)}) copy-start(bf16[128,256]{1,0:T(8,128)(2,1)} %refs_0_.2) | copy-start | bytes 196612
  1.5 0.8 %copy-start.4 = (bf16[128,256]{1,0:T(8,128)(2,1)S(1)}, bf16[128,256]{1,0:T(8,128)(2,1)}, u32[]{:S(2)}) copy-start(bf16[128,256]{1,0:T(8,128)(2,1)} %refs_1_.1) | copy-start | bytes 196612
  2.3 3.3 %collective-permute-start = (bf16[256,128]{1,0:T(8,128)(2,1)S(1)}, bf16[256,128]{1,0:T(8,128)(2,1)S(1)}, u32[]{:S(2)}, u32[]{:S(2)}) collective-permute-start(bf16[256,128]{1,0:T(8,128)(2,1)S(1)} %get-tuple-element.38), channel_id=1, source_target_pairs={{0,4},{4,0},{8,12},{12,8},{16,20},{20,16},{24,28},{28,24},{32,36},... | collective-permute-start | bytes 196616 | tf_op jit(solution)/shard_map/ppermute | solution.py:435
  3.1 14.2 %collective-permute-start.2 = (bf16[32,8192]{1,0:T(8,128)(2,1)}, bf16[32,8192]{1,0:T(8,128)(2,1)S(1)}, u32[]{:S(2)}, u32[]{:S(2)}) collective-permute-start(bf16[32,8192]{1,0:T(8,128)(2,1)} %refs_0_.4), channel_id=1, source_target_pairs={{0,1},{1,2},{2,3},{3,0},{4,7},{5,4},{6,5},{7,6},{8,9},{9,10},{10,1... | collective-permute-start | bytes 1572872 | tf_op jit(solution)/shard_map/ppermute | solution.py:442
  5.7 13.7 %slice-start = ((s8[8388608]{0:T(1024)(128)(4,1)}), s8[4194304]{0:T(1024)(128)(4,1)S(1)}, s32[]{:S(2)}) async-start(s8[8388608]{0:T(1024)(128)(4,1)} %bitcast), calls=%async_computation | async-start | bytes 8388608
  5.7 13.7 %slice-start.1 = ((s8[8388608]{0:T(1024)(128)(4,1)}), s8[4194304]{0:T(1024)(128)(4,1)S(1)}, s32[]{:S(2)}) async-start(s8[8388608]{0:T(1024)(128)(4,1)} %bitcast), calls=%async_computation.1 | async-start | bytes 8388608
  5.7 10.0 %collective-permute-start.8 = (bf16[512,128]{1,0:T(8,128)(2,1)S(1)}, bf16[512,128]{1,0:T(8,128)(2,1)S(1)}, u32[]{:S(2)}, u32[]{:S(2)}) collective-permute-start(bf16[512,128]{1,0:T(8,128)(2,1)S(1)} %get-tuple-element.72), channel_id=1, source_target_pairs={{0,16},{4,68},{8,24},{12,76},{16,0},{20,84},{24,8},{28,92},{32,48}... | collective-permute-start | bytes 393224 | tf_op jit(solution)/shard_map/ppermute | solution.py:422
  6.7 8.9 %collective-permute-start.7 = (bf16[512,128]{1,0:T(8,128)(2,1)S(1)}, bf16[512,128]{1,0:T(8,128)(2,1)S(1)}, u32[]{:S(2)}, u32[]{:S(2)}) collective-permute-start(bf16[512,128]{1,0:T(8,128)(2,1)S(1)} %get-tuple-element.72), channel_id=1, source_target_pairs={{0,24},{4,100},{8,0},{12,108},{16,8},{20,116},{24,16},{28,124},{32... | collective-permute-start | bytes 393224 | tf_op jit(solution)/shard_map/ppermute | solution.py:422
  6.7 4.6 %collective-permute-start.6 = (bf16[512,128]{1,0:T(8,128)(2,1)S(1)}, bf16[512,128]{1,0:T(8,128)(2,1)S(1)}, u32[]{:S(2)}, u32[]{:S(2)}) collective-permute-start(bf16[512,128]{1,0:T(8,128)(2,1)S(1)} %get-tuple-element.72), channel_id=1, source_target_pairs={{0,8},{4,36},{8,16},{12,44},{16,24},{20,52},{24,0},{28,60},{32,40}... | collective-permute-start | bytes 393224 | tf_op jit(solution)/shard_map/ppermute | solution.py:422
  9.4 10.0 %collective-permute-start.4 = (bf16[32,8192]{1,0:T(8,128)(2,1)}, bf16[32,8192]{1,0:T(8,128)(2,1)S(1)}, u32[]{:S(2)}, u32[]{:S(2)}) collective-permute-start(bf16[32,8192]{1,0:T(8,128)(2,1)} %refs_0_.4), channel_id=1, source_target_pairs={{0,3},{1,0},{2,1},{3,2},{4,5},{5,6},{6,7},{7,4},{8,11},{9,8},{10,9... | collective-permute-start | bytes 1572872 | tf_op jit(solution)/shard_map/ppermute | solution.py:445
  9.4 1.0 %copy-start.1 = (bf16[128,2048]{1,0:T(8,128)(2,1)S(1)}, bf16[128,2048]{1,0:T(8,128)(2,1)}, u32[]{:S(2)}) copy-start(bf16[128,2048]{1,0:T(8,128)(2,1)} %refs_0_.3) | copy-start | bytes 1572868
  10.4 8.9 %copy-start.2 = (bf16[32,8192]{1,0:T(8,128)(2,1)S(1)}, bf16[32,8192]{1,0:T(8,128)(2,1)}, u32[]{:S(2)}) copy-start(bf16[32,8192]{1,0:T(8,128)(2,1)} %refs_0_.4) | copy-start | bytes 1572868
  11.3 13.4 %collective-permute-start.1 = (bf16[1024,128]{1,0:T(8,128)(2,1)S(1)}, bf16[1024,128]{1,0:T(8,128)(2,1)S(1)}, u32[]{:S(2)}, u32[]{:S(2)}) collective-permute-start(bf16[1024,128]{1,0:T(8,128)(2,1)S(1)} %get-tuple-element.41), channel_id=1, source_target_pairs={{0,4},{4,0},{8,12},{12,8},{16,20},{20,16},{24,28},{28,24},{32,36},... | collective-permute-start | bytes 786440 | tf_op jit(solution)/shard_map/ppermute | solution.py:435
  15.7 17.4 %collective-permute-start.10 = (bf16[2048,128]{1,0:T(8,128)(2,1)S(1)}, bf16[2048,128]{1,0:T(8,128)(2,1)S(1)}, u32[]{:S(2)}, u32[]{:S(2)}) collective-permute-start(bf16[2048,128]{1,0:T(8,128)(2,1)S(1)} %constant_dynamic-update-slice_fusion.4.refs_0_), channel_id=1, source_target_pairs={{0,96},{4,28},{8,104},{12,4},{16,112},{20,12},{24,120},{28,20},{32... | collective-permute-start | bytes 1572872 | tf_op jit(solution)/shard_map/ppermute | solution.py:427
  16.7 16.9 %collective-permute-start.9 = (bf16[2048,128]{1,0:T(8,128)(2,1)S(1)}, bf16[2048,128]{1,0:T(8,128)(2,1)S(1)}, u32[]{:S(2)}, u32[]{:S(2)}) collective-permute-start(bf16[2048,128]{1,0:T(8,128)(2,1)S(1)} %constant_dynamic-update-slice_fusion.4.refs_0_), channel_id=1, source_target_pairs={{0,32},{4,12},{8,40},{12,20},{16,48},{20,28},{24,56},{28,4},{32,64... | collective-permute-start | bytes 1572872 | tf_op jit(solution)/shard_map/ppermute | solution.py:427
  17.3 8.3 %collective-permute-start.3 = (bf16[32,8192]{1,0:T(8,128)(2,1)S(1)}, bf16[32,8192]{1,0:T(8,128)(2,1)S(1)}, u32[]{:S(2)}, u32[]{:S(2)}) collective-permute-start(bf16[32,8192]{1,0:T(8,128)(2,1)S(1)} %collective-permute-done.2.refs_1_), channel_id=1, source_target_pairs={{0,1},{1,2},{2,3},{3,0},{4,7},{5,4},{6,5},{7,6},{8,9},{9,10},{10,1... | collective-permute-start | bytes 1572872 | tf_op jit(solution)/shard_map/ppermute | solution.py:449
  20.8 12.8 %copy-start = (s32[32]{0:T(128)S(1)}, s32[32]{0:T(128)}, u32[]{:S(2)}) copy-start(s32[32]{0:T(128)} %kv_blocks.1) | copy-start | bytes 388
  20.9 12.7 %collective-permute-start.11 = (bf16[2048,128]{1,0:T(8,128)(2,1)S(1)}, bf16[2048,128]{1,0:T(8,128)(2,1)S(1)}, u32[]{:S(2)}, u32[]{:S(2)}) collective-permute-start(bf16[2048,128]{1,0:T(8,128)(2,1)S(1)} %constant_dynamic-update-slice_fusion.4.refs_0_), channel_id=1, source_target_pairs={{0,64},{4,20},{8,72},{12,28},{16,80},{20,4},{24,88},{28,12},{32,96... | collective-permute-start | bytes 1572872 | tf_op jit(solution)/shard_map/ppermute | solution.py:431
  27.2 4.8 %collective-permute-start.5 = (bf16[256,128]{1,0:T(8,128)(2,1)S(1)}, bf16[256,128]{1,0:T(8,128)(2,1)S(1)}, u32[]{:S(2)}, u32[]{:S(2)}) collective-permute-start(bf16[256,128]{1,0:T(8,128)(2,1)S(1)} %get-tuple-element.48), channel_id=1, source_target_pairs={{0,4},{4,0},{8,12},{12,8},{16,20},{20,16},{24,28},{28,24},{32,36},... | collective-permute-start | bytes 196616 | tf_op jit(solution)/shard_map/ppermute | solution.py:435
  32.0 5.4 %collective-permute-start.12 = (bf16[512,128]{1,0:T(8,128)(2,1)S(1)}, bf16[512,128]{1,0:T(8,128)(2,1)S(1)}, u32[]{:S(2)}, u32[]{:S(2)}) collective-permute-start(bf16[512,128]{1,0:T(8,128)(2,1)S(1)} %constant_dynamic-update-slice_fusion.2), channel_id=1, source_target_pairs={{0,8},{4,36},{8,16},{12,44},{16,24},{20,52},{24,0},{28,60},{32,40}... | collective-permute-start | bytes 393224 | tf_op jit(solution)/shard_map/ppermute | solution.py:422
  32.1 7.1 %collective-permute-start.14 = (bf16[512,128]{1,0:T(8,128)(2,1)S(1)}, bf16[512,128]{1,0:T(8,128)(2,1)S(1)}, u32[]{:S(2)}, u32[]{:S(2)}) collective-permute-start(bf16[512,128]{1,0:T(8,128)(2,1)S(1)} %constant_dynamic-update-slice_fusion.2), channel_id=1, source_target_pairs={{0,16},{4,68},{8,24},{12,76},{16,0},{20,84},{24,8},{28,92},{32,48}... | collective-permute-start | bytes 393224 | tf_op jit(solution)/shard_map/ppermute | solution.py:422
  33.2 6.1 %collective-permute-start.13 = (bf16[512,128]{1,0:T(8,128)(2,1)S(1)}, bf16[512,128]{1,0:T(8,128)(2,1)S(1)}, u32[]{:S(2)}, u32[]{:S(2)}) collective-permute-start(bf16[512,128]{1,0:T(8,128)(2,1)S(1)} %constant_dynamic-update-slice_fusion.2), channel_id=1, source_target_pairs={{0,24},{4,100},{8,0},{12,108},{16,8},{20,116},{24,16},{28,124},{32... | collective-permute-start | bytes 393224 | tf_op jit(solution)/shard_map/ppermute | solution.py:422
  39.3 9.6 %collective-permute-start.15 = (bf16[2048,128]{1,0:T(8,128)(2,1)S(1)}, bf16[2048,128]{1,0:T(8,128)(2,1)S(1)}, u32[]{:S(2)}, u32[]{:S(2)}) collective-permute-start(bf16[2048,128]{1,0:T(8,128)(2,1)S(1)} %constant_dynamic-update-slice_fusion.9.refs_0_), channel_id=1, source_target_pairs={{0,32},{4,12},{8,40},{12,20},{16,48},{20,28},{24,56},{28,4},{32,64... | collective-permute-start | bytes 1572872 | tf_op jit(solution)/shard_map/ppermute | solution.py:427
  39.4 9.8 %collective-permute-start.17 = (bf16[2048,128]{1,0:T(8,128)(2,1)S(1)}, bf16[2048,128]{1,0:T(8,128)(2,1)S(1)}, u32[]{:S(2)}, u32[]{:S(2)}) collective-permute-start(bf16[2048,128]{1,0:T(8,128)(2,1)S(1)} %constant_dynamic-update-slice_fusion.9.refs_0_), channel_id=1, source_target_pairs={{0,96},{4,28},{8,104},{12,4},{16,112},{20,12},{24,120},{28,20},{32... | collective-permute-start | bytes 1572872 | tf_op jit(solution)/shard_map/ppermute | solution.py:427
  48.9 9.8 %collective-permute-start.16 = (bf16[2048,128]{1,0:T(8,128)(2,1)S(1)}, bf16[2048,128]{1,0:T(8,128)(2,1)S(1)}, u32[]{:S(2)}, u32[]{:S(2)}) collective-permute-start(bf16[2048,128]{1,0:T(8,128)(2,1)S(1)} %constant_dynamic-update-slice_fusion.9.refs_0_), channel_id=1, source_target_pairs={{0,64},{4,20},{8,72},{12,28},{16,80},{20,4},{24,88},{28,12},{32,96... | collective-permute-start | bytes 1572872 | tf_op jit(solution)/shard_map/ppermute | solution.py:431
  62.0 3.9 %collective-permute-start.18 = (bf16[128,1024]{1,0:T(8,128)(2,1)S(1)}, bf16[128,1024]{1,0:T(8,128)(2,1)S(1)}, u32[]{:S(2)}, u32[]{:S(2)}) collective-permute-start(bf16[128,1024]{1,0:T(8,128)(2,1)S(1)} %get-tuple-element.68), channel_id=1, source_target_pairs={{0,4},{4,0},{8,12},{12,8},{16,20},{20,16},{24,28},{28,24},{32,36},... | collective-permute-start | bytes 786440 | tf_op jit(solution)/shard_map/ppermute | solution.py:435

commit v7 on v6

--- a/solution.py
+++ b/solution.py
@@ -467,7 +467,7 @@
     )
     block = jnp.concatenate([mine, swapped(give)], 0)
     *states, turned, values = attend_cache(
-        kv_blocks, after(own_queries, block), received, cache, live_keys, live_keys // 2
+        kv_blocks, after(own_queries, block), received, cache, live_keys, live_keys // 8 * 5
     )
     joined = first_phase(block, states[0])
     new = second_phase(joined)

time: 67.1 us -> 67.1 us (level)
  starting transfers between devices: 29.4 us -> 28.6 us
    ppermute x4, starting transfers between devices: 11.6 us -> 10.7 us  [swapped(): return lax.ppermute(block, 'group', swap_cores())]
    pallas_call x1, Pallas kernels: 2.85 us -> 3.71 us  [attend_later(): pl.pallas_call(later_kernel, out_shape=(STATE,) * 3, in_specs=[VMEM] * 7,...]
  transfers between devices with their start and end apart: 19 -> 19, of which waited for: 7 -> 6; matrix products, arithmetic and copies ran while one was open for 1% -> 1% of each run, Pallas kernels for 28% -> 29%
where the time goes in v7:
time: 67.1 us; the launch traced here: 66.9 us
  starting transfers between devices  28.6 us (43%)
  Pallas kernels  23.7 us (35%)
  waiting for transfers between devices  10.2 us (15%)
  local copies, waits for them, and re-layouts  2.91 us (4%)
  between operations  1.09 us (2%)
    pallas_call x3, Pallas kernels, attend_new(): pl.pallas_call(functools.partial(new_kernel, which, last), out_shape=(out...  12.6 us
    ppermute x4, starting transfers between devices, swapped(): return lax.ppermute(block, 'group', swap_cores())  10.7 us
    ppermute x6, starting transfers between devices, first_phase(): sent = [lax.ppermute(block, 'group', along(0, d)) for d in (1, 3, 2)]  5.24 us
    ppermute x4, starting transfers between devices, second_phase(): lax.ppermute(joined, 'group', along(1, d))  4.27 us
    ppermute x2, waiting for transfers between devices, last_phase(): return lax.ppermute(after(joined, *others), 'group', along(1, 2))  4.27 us
    ppermute x2, starting transfers between devices, last_phase(): return lax.ppermute(after(joined, *others), 'group', along(1, 2))  3.79 us
    pallas_call x1, Pallas kernels, attend_later(): pl.pallas_call(later_kernel, out_shape=(STATE,) * 3, in_specs=[VMEM] * 7,...  3.71 us
    pallas_call x1, Pallas kernels, attend_cache(): pl.pallas_call(functools.partial(cache_kernel, live_keys), out_shape=(STA...  3.31 us
  transfers between devices with their start and end apart: 19, of which 6 were waited for; matrix products, arithmetic and copies ran while one was open for 1% of the time, Pallas kernels for 29%

profile of v7, /device:TPU:25, one launch (start us, length us, event | category | flops | bytes accessed | tf_op | source)
XLA Modules:
  0.0 66.9 jit_solution(14887488855389114779)
XLA Ops:
  0.6 0.0 copy-start.3
  0.6 0.8 %copy-done.3 = bf16[128,256]{1,0:T(8,128)(2,1)S(1)} copy-done((bf16[128,256]{1,0:T(8,128)(2,1)S(1)}, bf16[128,256]{1,0:T(8,128)(2,1)}, u32[]{:S(2)}) %copy-start.3) | copy-done | bytes 65560
  1.5 0.0 copy-start.4
  1.5 0.8 %copy-done.4 = bf16[128,256]{1,0:T(8,128)(2,1)S(1)} copy-done((bf16[128,256]{1,0:T(8,128)(2,1)S(1)}, bf16[128,256]{1,0:T(8,128)(2,1)}, u32[]{:S(2)}) %copy-start.4) | copy-done | bytes 65560
  2.3 0.8 %collective-permute-start = (bf16[256,128]{1,0:T(8,128)(2,1)S(1)}, bf16[256,128]{1,0:T(8,128)(2,1)S(1)}, u32[]{:S(2)}, u32[]{:S(2)}) collective-permute-start(bf16[256,128]{1,0:T(8,128)(2,1)S(1)} %get-tuple-element.38), channel_id=1, source_target_pairs={{0,4},{4,0},{8,12},{12,8},{16,20},{20,16},{24,28},{28,24},{32,36},... | collective-permute-start | bytes 196616 | tf_op jit(solution)/shard_map/ppermute | solution.py:435
  3.1 2.5 %collective-permute-start.2 = (bf16[32,8192]{1,0:T(8,128)(2,1)}, bf16[32,8192]{1,0:T(8,128)(2,1)S(1)}, u32[]{:S(2)}, u32[]{:S(2)}) collective-permute-start(bf16[32,8192]{1,0:T(8,128)(2,1)} %refs_0_.4), channel_id=1, source_target_pairs={{0,1},{1,2},{2,3},{3,0},{4,7},{5,4},{6,5},{7,6},{8,9},{9,10},{10,1... | collective-permute-start | bytes 1572872 | tf_op jit(solution)/shard_map/ppermute | solution.py:442
  5.6 0.0 collective-permute-done
  5.7 0.0 slice-start
  5.7 0.0 slice-start.1
  5.7 1.0 %collective-permute-start.8 = (bf16[512,128]{1,0:T(8,128)(2,1)S(1)}, bf16[512,128]{1,0:T(8,128)(2,1)S(1)}, u32[]{:S(2)}, u32[]{:S(2)}) collective-permute-start(bf16[512,128]{1,0:T(8,128)(2,1)S(1)} %get-tuple-element.72), channel_id=1, source_target_pairs={{0,16},{4,68},{8,24},{12,76},{16,0},{20,84},{24,8},{28,92},{32,48}... | collective-permute-start | bytes 393224 | tf_op jit(solution)/shard_map/ppermute | solution.py:422
  6.7 0.0 collective-permute-start.7
  6.7 2.7 %collective-permute-start.6 = (bf16[512,128]{1,0:T(8,128)(2,1)S(1)}, bf16[512,128]{1,0:T(8,128)(2,1)S(1)}, u32[]{:S(2)}, u32[]{:S(2)}) collective-permute-start(bf16[512,128]{1,0:T(8,128)(2,1)S(1)} %get-tuple-element.72), channel_id=1, source_target_pairs={{0,8},{4,36},{8,16},{12,44},{16,24},{20,52},{24,0},{28,60},{32,40}... | collective-permute-start | bytes 393224 | tf_op jit(solution)/shard_map/ppermute | solution.py:422
  9.4 0.0 collective-permute-start.4
  9.4 0.0 copy-start.1
  9.4 1.0 %copy-done.1 = bf16[128,2048]{1,0:T(8,128)(2,1)S(1)} copy-done((bf16[128,2048]{1,0:T(8,128)(2,1)S(1)}, bf16[128,2048]{1,0:T(8,128)(2,1)}, u32[]{:S(2)}) %copy-start.1) | copy-done | bytes 524312
  10.4 0.0 copy-start.2
  10.4 0.1 heads.3
  10.6 0.8 %collective-permute-done.6 = bf16[512,128]{1,0:T(8,128)(2,1)S(1)} collective-permute-done((bf16[512,128]{1,0:T(8,128)(2,1)S(1)}, bf16[512,128]{1,0:T(8,128)(2,1)S(1)}, u32[]{:S(2)}, u32[]{:S(2)}) %collective-permute-start.6) | collective-permute-done | bytes 131104 | tf_op jit(solution)/shard_map/ppermute | solution.py:422
  11.3 4.3 %collective-permute-start.1 = (bf16[1024,128]{1,0:T(8,128)(2,1)S(1)}, bf16[1024,128]{1,0:T(8,128)(2,1)S(1)}, u32[]{:S(2)}, u32[]{:S(2)}) collective-permute-start(bf16[1024,128]{1,0:T(8,128)(2,1)S(1)} %get-tuple-element.41), channel_id=1, source_target_pairs={{0,4},{4,0},{8,12},{12,8},{16,20},{20,16},{24,28},{28,24},{32,36},... | collective-permute-start | bytes 786440 | tf_op jit(solution)/shard_map/ppermute | solution.py:435
  15.6 0.0 collective-permute-done.7
  15.7 0.0 collective-permute-done.8
  15.7 0.9 %collective-permute-start.10 = (bf16[2048,128]{1,0:T(8,128)(2,1)S(1)}, bf16[2048,128]{1,0:T(8,128)(2,1)S(1)}, u32[]{:S(2)}, u32[]{:S(2)}) collective-permute-start(bf16[2048,128]{1,0:T(8,128)(2,1)S(1)} %constant_dynamic-update-slice_fusion.4.refs_0_), channel_id=1, source_target_pairs={{0,96},{4,28},{8,104},{12,4},{16,112},{20,12},{24,120},{28,20},{32... | collective-permute-start | bytes 1572872 | tf_op jit(solution)/shard_map/ppermute | solution.py:427
  16.7 0.6 collective-permute-start.9
  17.3 0.0 collective-permute-done.2.refs_1_
  17.3 2.1 %collective-permute-start.3 = (bf16[32,8192]{1,0:T(8,128)(2,1)S(1)}, bf16[32,8192]{1,0:T(8,128)(2,1)S(1)}, u32[]{:S(2)}, u32[]{:S(2)}) collective-permute-start(bf16[32,8192]{1,0:T(8,128)(2,1)S(1)} %collective-permute-done.2.refs_1_), channel_id=1, source_target_pairs={{0,1},{1,2},{2,3},{3,0},{4,7},{5,4},{6,5},{7,6},{8,9},{9,10},{10,1... | collective-permute-start | bytes 1572872 | tf_op jit(solution)/shard_map/ppermute | solution.py:449
  19.4 0.0 collective-permute-done.4.refs_2_
  19.4 0.0 slice-done
  19.4 0.0 slice-done.1
  19.4 0.0 copy-done.2
  19.4 1.4 %project_near.1 = (f32[96,256]{1,0:T(8,128)S(1)}, f32[96,256]{1,0:T(8,128)S(1)}) custom-call(bf16[32,8192]{1,0:T(8,128)(2,1)S(1)} %copy-done.2, bf16[32,8192]{1,0:T(8,128)(2,1)S(1)} %collective-permute-done.2.refs_1_, bf16[32,8192]{1,0:T(8,128)(2,1)S(1)} %collective-permute-done.4.refs_2_, bf16[2,8192,256]{2,1,0:T(8,128)(2,1)S(1)} %bitcast.1), custom_call_target="tpu_custom_call" | custom-call | flops 22000001024 | bytes 70000000 | tf_op jit(solution)/shard_map/project_near/pallas_call | solution.py:121
  20.8 0.0 copy-start
  20.9 3.4 %collective-permute-start.11 = (bf16[2048,128]{1,0:T(8,128)(2,1)S(1)}, bf16[2048,128]{1,0:T(8,128)(2,1)S(1)}, u32[]{:S(2)}, u32[]{:S(2)}) collective-permute-start(bf16[2048,128]{1,0:T(8,128)(2,1)S(1)} %constant_dynamic-update-slice_fusion.4.refs_0_), channel_id=1, source_target_pairs={{0,64},{4,20},{8,72},{12,28},{16,80},{20,4},{24,88},{28,12},{32,96... | collective-permute-start | bytes 1572872 | tf_op jit(solution)/shard_map/ppermute | solution.py:431
  24.3 0.3 fusion
  24.6 0.1 pad_maximum_fusion
  24.7 0.0 collective-permute-done.1.received
  24.7 0.9 %collective-permute-done.3.piece = bf16[32,8192]{1,0:T(8,128)(2,1)S(1)} collective-permute-done((bf16[32,8192]{1,0:T(8,128)(2,1)S(1)}, bf16[32,8192]{1,0:T(8,128)(2,1)S(1)}, u32[]{:S(2)}, u32[]{:S(2)}) %collective-permute-start.3) | collective-permute-done | bytes 524320 | tf_op jit(solution)/shard_map/ppermute | solution.py:449
  25.6 1.6 %project_far.1 = (bf16[128,256]{1,0:T(8,128)(2,1)S(1)}, bf16[128,256]{1,0:T(8,128)(2,1)S(1)}, bf16[256,128]{1,0:T(8,128)(2,1)S(1)}, bf16[256,128]{1,0:T(8,128)(2,1)S(1)}) custom-call(bf16[32,8192]{1,0:T(8,128)(2,1)S(1)} %collective-permute-done.3.piece, f32[96,256]{1,0:T(8,128)S(1)} %get-tuple-element.45.near_keys, ...), custom_call_target="tpu_custom_call" | custom-call | flops 110000000 | bytes 350000 | tf_op jit(solution)/shard_map/project_far/pallas_call | solution.py:164
  27.2 3.9 %collective-permute-start.5 = (bf16[256,128]{1,0:T(8,128)(2,1)S(1)}, bf16[256,128]{1,0:T(8,128)(2,1)S(1)}, u32[]{:S(2)}, u32[]{:S(2)}) collective-permute-start(bf16[256,128]{1,0:T(8,128)(2,1)S(1)} %get-tuple-element.48), channel_id=1, source_target_pairs={{0,4},{4,0},{8,12},{12,8},{16,20},{20,16},{24,28},{28,24},{32,36},... | collective-permute-start | bytes 196616 | tf_op jit(solution)/shard_map/ppermute | solution.py:435
  31.1 0.9 %collective-permute-done.5 = bf16[256,128]{1,0:T(8,128)(2,1)S(1)} collective-permute-done((bf16[256,128]{1,0:T(8,128)(2,1)S(1)}, bf16[256,128]{1,0:T(8,128)(2,1)S(1)}, u32[]{:S(2)}, u32[]{:S(2)}) %collective-permute-start.5) | collective-permute-done | bytes 65568 | tf_op jit(solution)/shard_map/ppermute | solution.py:435
  32.0 0.1 collective-permute-start.12
  32.1 1.0 %collective-permute-start.14 = (bf16[512,128]{1,0:T(8,128)(2,1)S(1)}, bf16[512,128]{1,0:T(8,128)(2,1)S(1)}, u32[]{:S(2)}, u32[]{:S(2)}) collective-permute-start(bf16[512,128]{1,0:T(8,128)(2,1)S(1)} %constant_dynamic-update-slice_fusion.2), channel_id=1, source_target_pairs={{0,16},{4,68},{8,24},{12,76},{16,0},{20,84},{24,8},{28,92},{32,48}... | collective-permute-start | bytes 393224 | tf_op jit(solution)/shard_map/ppermute | solution.py:422
  33.2 0.0 collective-permute-done.10.refs_2_
  33.2 0.4 collective-permute-start.13
  33.6 0.0 collective-permute-done.9.refs_1_
  33.6 0.0 collective-permute-done.11.refs_3_
  33.6 0.0 copy-done
  33.6 3.3 %attend_cache.1 = (f32[2048,128]{1,0:T(8,128)S(1)}, f32[2048,128]{1,0:T(8,128)S(1)}, f32[2048,128]{1,0:T(8,128)S(1)}, bf16[128,2048]{1,0:T(8,128)(2,1)S(1)}, bf16[1280,128]{1,0:T(8,128)(2,1)S(1)}) custom-call(s32[32]{0:T(128)S(1)} %copy-done, bf16[1024,128]{1,0:T(8,128)(2,1)S(1)} %get-tuple-element.49.own_queries, ...), custom_call_target="tpu_custom_call" | custom-call | flops 110000000 | bytes 350000 | tf_op jit(solution)/shard_map/attend_cache/pallas_call | solution.py:236
  36.9 0.0 collective-permute-done.12
  37.0 2.3 %collective-permute-done.13 = bf16[512,128]{1,0:T(8,128)(2,1)S(1)} collective-permute-done((bf16[512,128]{1,0:T(8,128)(2,1)S(1)}, bf16[512,128]{1,0:T(8,128)(2,1)S(1)}, u32[]{:S(2)}, u32[]{:S(2)}) %collective-permute-start.13) | collective-permute-done | bytes 131104 | tf_op jit(solution)/shard_map/ppermute | solution.py:422
  39.3 0.0 collective-permute-done.14
  39.3 0.1 collective-permute-start.15
  39.4 2.7 %collective-permute-start.17 = (bf16[2048,128]{1,0:T(8,128)(2,1)S(1)}, bf16[2048,128]{1,0:T(8,128)(2,1)S(1)}, u32[]{:S(2)}, u32[]{:S(2)}) collective-permute-start(bf16[2048,128]{1,0:T(8,128)(2,1)S(1)} %constant_dynamic-update-slice_fusion.9.refs_0_), channel_id=1, source_target_pairs={{0,96},{4,28},{8,104},{12,4},{16,112},{20,12},{24,120},{28,20},{32... | collective-permute-start | bytes 1572872 | tf_op jit(solution)/shard_map/ppermute | solution.py:427
  42.0 4.0 %attend_new.2 = (f32[2048,128]{1,0:T(8,128)S(1)}, f32[2048,128]{1,0:T(8,128)S(1)}, f32[2048,128]{1,0:T(8,128)S(1)}) custom-call(bf16[1024,128]{1,0:T(8,128)(2,1)S(1)} %get-tuple-element.49.own_queries, bf16[1024,128]{1,0:T(8,128)(2,1)S(1)} %collective-permute-done.1.received, bf16[2048,128]{1,0:T(8,128)(2,1)S(1)} %constant_dynamic-update-slice_fusion.9.refs_0_, ...), custom_call_target="tpu_custom_call" | custom-call | flops 110000000 | bytes 350000 | tf_op jit(solution)/shard_map/attend_new/pallas_call | solution.py:363
  46.1 3.7 %attend_later.1 = (f32[2048,128]{1,0:T(8,128)S(1)}, f32[2048,128]{1,0:T(8,128)S(1)}, f32[2048,128]{1,0:T(8,128)S(1)}) custom-call(bf16[1024,128]{1,0:T(8,128)(2,1)S(1)} %get-tuple-element.49.own_queries, bf16[1024,128]{1,0:T(8,128)(2,1)S(1)} %collective-permute-done.1.received, bf16[128,2048]{1,0:T(8,128)(2,1)S(1)} %get-tuple-element.53.turned, ...), custom_call_target="tpu_custom_call" | custom-call | flops 110000000 | bytes 350000 | tf_op jit(solution)/shard_map/attend_later/pallas_call | solution.py:264
  49.8 0.0 collective-permute-done.15.refs_0_
  49.8 0.3 collective-permute-start.16
  50.1 0.0 collective-permute-done.17.refs_1_
  50.1 5.3 %attend_new.3 = (f32[2048,128]{1,0:T(8,128)S(1)}, f32[2048,128]{1,0:T(8,128)S(1)}, f32[2048,128]{1,0:T(8,128)S(1)}) custom-call(bf16[1024,128]{1,0:T(8,128)(2,1)S(1)} %get-tuple-element.49.own_queries, bf16[1024,128]{1,0:T(8,128)(2,1)S(1)} %collective-permute-done.1.received, bf16[2048,128]{1,0:T(8,128)(2,1)S(1)} %collective-permute-done.15.refs_0_, ...), custom_call_target="tpu_custom_call" | custom-call | flops 110000000 | bytes 350000 | tf_op jit(solution)/shard_map/attend_new/pallas_call | solution.py:363
  55.4 4.3 %collective-permute-done.16.refs_0_ = bf16[2048,128]{1,0:T(8,128)(2,1)S(1)} collective-permute-done((bf16[2048,128]{1,0:T(8,128)(2,1)S(1)}, bf16[2048,128]{1,0:T(8,128)(2,1)S(1)}, u32[]{:S(2)}, u32[]{:S(2)}) %collective-permute-start.16) | collective-permute-done | bytes 524320 | tf_op jit(solution)/shard_map/ppermute | solution.py:431
  59.7 3.2 %attend_new_last.1 = (bf16[128,1024]{1,0:T(8,128)(2,1)S(1)}, bf16[128,1024]{1,0:T(8,128)(2,1)S(1)}) custom-call(bf16[1024,128]{1,0:T(8,128)(2,1)S(1)} %get-tuple-element.49.own_queries, bf16[1024,128]{1,0:T(8,128)(2,1)S(1)} %collective-permute-done.1.received, bf16[2048,128]{1,0:T(8,128)(2,1)S(1)} %collective-permute-done.16.refs_0_, ...), custom_call_target="tpu_custom_call" | custom-call | flops 110000000 | bytes 350000 | tf_op jit(solution)/shard_map/attend_new_last/pallas_call | solution.py:363
  62.9 1.7 %collective-permute-start.18 = (bf16[128,1024]{1,0:T(8,128)(2,1)S(1)}, bf16[128,1024]{1,0:T(8,128)(2,1)S(1)}, u32[]{:S(2)}, u32[]{:S(2)}) collective-permute-start(bf16[128,1024]{1,0:T(8,128)(2,1)S(1)} %get-tuple-element.68), channel_id=1, source_target_pairs={{0,4},{4,0},{8,12},{12,8},{16,20},{20,16},{24,28},{28,24},{32,36},... | collective-permute-start | bytes 786440 | tf_op jit(solution)/shard_map/ppermute | solution.py:435
  64.7 1.2 %collective-permute-done.18.other = bf16[128,1024]{1,0:T(8,128)(2,1)S(1)} collective-permute-done((bf16[128,1024]{1,0:T(8,128)(2,1)S(1)}, bf16[128,1024]{1,0:T(8,128)(2,1)S(1)}, u32[]{:S(2)}, u32[]{:S(2)}) %collective-permute-start.18) | collective-permute-done | bytes 262176 | tf_op jit(solution)/shard_map/ppermute | solution.py:435
  65.8 0.9 %finish.1 = (bf16[128,2048]{1,0:T(8,128)(2,1)}, bf16[128,256]{1,0:T(8,128)(2,1)}, bf16[128,256]{1,0:T(8,128)(2,1)}) custom-call(bf16[128,1024]{1,0:T(8,128)(2,1)S(1)} %get-tuple-element.67.here, bf16[128,1024]{1,0:T(8,128)(2,1)S(1)} %collective-permute-done.18.other, bf16[128,256]{1,0:T(8,128)(2,1)S(1)} %get-tuple-element.69.keys, ...), custom_call_target="tpu_custom_call" | custom-call | flops 110000000 | bytes 350000 | tf_op jit(solution)/shard_map/finish/pallas_call | solution.py:403
  (15 shorter events, 0.2 us)
Async XLA Ops:
  0.6 0.8 %copy-start.3 = (bf16[128,256]{1,0:T(8,128)(2,1)S(1)}, bf16[128,256]{1,0:T(8,128)(2,1)}, u32[]{:S(2)}) copy-start(bf16[128,256]{1,0:T(8,128)(2,1)} %refs_0_.2) | copy-start | bytes 196612
  1.5 0.8 %copy-start.4 = (bf16[128,256]{1,0:T(8,128)(2,1)S(1)}, bf16[128,256]{1,0:T(8,128)(2,1)}, u32[]{:S(2)}) copy-start(bf16[128,256]{1,0:T(8,128)(2,1)} %refs_1_.1) | copy-start | bytes 196612
  2.3 3.3 %collective-permute-start = (bf16[256,128]{1,0:T(8,128)(2,1)S(1)}, bf16[256,128]{1,0:T(8,128)(2,1)S(1)}, u32[]{:S(2)}, u32[]{:S(2)}) collective-permute-start(bf16[256,128]{1,0:T(8,128)(2,1)S(1)} %get-tuple-element.38), channel_id=1, source_target_pairs={{0,4},{4,0},{8,12},{12,8},{16,20},{20,16},{24,28},{28,24},{32,36},... | collective-permute-start | bytes 196616 | tf_op jit(solution)/shard_map/ppermute | solution.py:435
  3.1 14.2 %collective-permute-start.2 = (bf16[32,8192]{1,0:T(8,128)(2,1)}, bf16[32,8192]{1,0:T(8,128)(2,1)S(1)}, u32[]{:S(2)}, u32[]{:S(2)}) collective-permute-start(bf16[32,8192]{1,0:T(8,128)(2,1)} %refs_0_.4), channel_id=1, source_target_pairs={{0,1},{1,2},{2,3},{3,0},{4,7},{5,4},{6,5},{7,6},{8,9},{9,10},{10,1... | collective-permute-start | bytes 1572872 | tf_op jit(solution)/shard_map/ppermute | solution.py:442
  5.7 13.7 %slice-start = ((s8[8388608]{0:T(1024)(128)(4,1)}), s8[4194304]{0:T(1024)(128)(4,1)S(1)}, s32[]{:S(2)}) async-start(s8[8388608]{0:T(1024)(128)(4,1)} %bitcast), calls=%async_computation | async-start | bytes 8388608
  5.7 13.7 %slice-start.1 = ((s8[8388608]{0:T(1024)(128)(4,1)}), s8[4194304]{0:T(1024)(128)(4,1)S(1)}, s32[]{:S(2)}) async-start(s8[8388608]{0:T(1024)(128)(4,1)} %bitcast), calls=%async_computation.1 | async-start | bytes 8388608
  5.7 10.0 %collective-permute-start.8 = (bf16[512,128]{1,0:T(8,128)(2,1)S(1)}, bf16[512,128]{1,0:T(8,128)(2,1)S(1)}, u32[]{:S(2)}, u32[]{:S(2)}) collective-permute-start(bf16[512,128]{1,0:T(8,128)(2,1)S(1)} %get-tuple-element.72), channel_id=1, source_target_pairs={{0,16},{4,68},{8,24},{12,76},{16,0},{20,84},{24,8},{28,92},{32,48}... | collective-permute-start | bytes 393224 | tf_op jit(solution)/shard_map/ppermute | solution.py:422
  6.7 8.9 %collective-permute-start.7 = (bf16[512,128]{1,0:T(8,128)(2,1)S(1)}, bf16[512,128]{1,0:T(8,128)(2,1)S(1)}, u32[]{:S(2)}, u32[]{:S(2)}) collective-permute-start(bf16[512,128]{1,0:T(8,128)(2,1)S(1)} %get-tuple-element.72), channel_id=1, source_target_pairs={{0,24},{4,100},{8,0},{12,108},{16,8},{20,116},{24,16},{28,124},{32... | collective-permute-start | bytes 393224 | tf_op jit(solution)/shard_map/ppermute | solution.py:422
  6.7 4.6 %collective-permute-start.6 = (bf16[512,128]{1,0:T(8,128)(2,1)S(1)}, bf16[512,128]{1,0:T(8,128)(2,1)S(1)}, u32[]{:S(2)}, u32[]{:S(2)}) collective-permute-start(bf16[512,128]{1,0:T(8,128)(2,1)S(1)} %get-tuple-element.72), channel_id=1, source_target_pairs={{0,8},{4,36},{8,16},{12,44},{16,24},{20,52},{24,0},{28,60},{32,40}... | collective-permute-start | bytes 393224 | tf_op jit(solution)/shard_map/ppermute | solution.py:422
  9.4 10.0 %collective-permute-start.4 = (bf16[32,8192]{1,0:T(8,128)(2,1)}, bf16[32,8192]{1,0:T(8,128)(2,1)S(1)}, u32[]{:S(2)}, u32[]{:S(2)}) collective-permute-start(bf16[32,8192]{1,0:T(8,128)(2,1)} %refs_0_.4), channel_id=1, source_target_pairs={{0,3},{1,0},{2,1},{3,2},{4,5},{5,6},{6,7},{7,4},{8,11},{9,8},{10,9... | collective-permute-start | bytes 1572872 | tf_op jit(solution)/shard_map/ppermute | solution.py:445
  9.4 1.0 %copy-start.1 = (bf16[128,2048]{1,0:T(8,128)(2,1)S(1)}, bf16[128,2048]{1,0:T(8,128)(2,1)}, u32[]{:S(2)}) copy-start(bf16[128,2048]{1,0:T(8,128)(2,1)} %refs_0_.3) | copy-start | bytes 1572868
  10.4 8.9 %copy-start.2 = (bf16[32,8192]{1,0:T(8,128)(2,1)S(1)}, bf16[32,8192]{1,0:T(8,128)(2,1)}, u32[]{:S(2)}) copy-start(bf16[32,8192]{1,0:T(8,128)(2,1)} %refs_0_.4) | copy-start | bytes 1572868
  11.3 13.4 %collective-permute-start.1 = (bf16[1024,128]{1,0:T(8,128)(2,1)S(1)}, bf16[1024,128]{1,0:T(8,128)(2,1)S(1)}, u32[]{:S(2)}, u32[]{:S(2)}) collective-permute-start(bf16[1024,128]{1,0:T(8,128)(2,1)S(1)} %get-tuple-element.41), channel_id=1, source_target_pairs={{0,4},{4,0},{8,12},{12,8},{16,20},{20,16},{24,28},{28,24},{32,36},... | collective-permute-start | bytes 786440 | tf_op jit(solution)/shard_map/ppermute | solution.py:435
  15.7 17.4 %collective-permute-start.10 = (bf16[2048,128]{1,0:T(8,128)(2,1)S(1)}, bf16[2048,128]{1,0:T(8,128)(2,1)S(1)}, u32[]{:S(2)}, u32[]{:S(2)}) collective-permute-start(bf16[2048,128]{1,0:T(8,128)(2,1)S(1)} %constant_dynamic-update-slice_fusion.4.refs_0_), channel_id=1, source_target_pairs={{0,96},{4,28},{8,104},{12,4},{16,112},{20,12},{24,120},{28,20},{32... | collective-permute-start | bytes 1572872 | tf_op jit(solution)/shard_map/ppermute | solution.py:427
  16.7 16.9 %collective-permute-start.9 = (bf16[2048,128]{1,0:T(8,128)(2,1)S(1)}, bf16[2048,128]{1,0:T(8,128)(2,1)S(1)}, u32[]{:S(2)}, u32[]{:S(2)}) collective-permute-start(bf16[2048,128]{1,0:T(8,128)(2,1)S(1)} %constant_dynamic-update-slice_fusion.4.refs_0_), channel_id=1, source_target_pairs={{0,32},{4,12},{8,40},{12,20},{16,48},{20,28},{24,56},{28,4},{32,64... | collective-permute-start | bytes 1572872 | tf_op jit(solution)/shard_map/ppermute | solution.py:427
  17.3 8.3 %collective-permute-start.3 = (bf16[32,8192]{1,0:T(8,128)(2,1)S(1)}, bf16[32,8192]{1,0:T(8,128)(2,1)S(1)}, u32[]{:S(2)}, u32[]{:S(2)}) collective-permute-start(bf16[32,8192]{1,0:T(8,128)(2,1)S(1)} %collective-permute-done.2.refs_1_), channel_id=1, source_target_pairs={{0,1},{1,2},{2,3},{3,0},{4,7},{5,4},{6,5},{7,6},{8,9},{9,10},{10,1... | collective-permute-start | bytes 1572872 | tf_op jit(solution)/shard_map/ppermute | solution.py:449
  20.8 12.8 %copy-start = (s32[32]{0:T(128)S(1)}, s32[32]{0:T(128)}, u32[]{:S(2)}) copy-start(s32[32]{0:T(128)} %kv_blocks.1) | copy-start | bytes 388
  20.9 12.7 %collective-permute-start.11 = (bf16[2048,128]{1,0:T(8,128)(2,1)S(1)}, bf16[2048,128]{1,0:T(8,128)(2,1)S(1)}, u32[]{:S(2)}, u32[]{:S(2)}) collective-permute-start(bf16[2048,128]{1,0:T(8,128)(2,1)S(1)} %constant_dynamic-update-slice_fusion.4.refs_0_), channel_id=1, source_target_pairs={{0,64},{4,20},{8,72},{12,28},{16,80},{20,4},{24,88},{28,12},{32,96... | collective-permute-start | bytes 1572872 | tf_op jit(solution)/shard_map/ppermute | solution.py:431
  27.2 4.8 %collective-permute-start.5 = (bf16[256,128]{1,0:T(8,128)(2,1)S(1)}, bf16[256,128]{1,0:T(8,128)(2,1)S(1)}, u32[]{:S(2)}, u32[]{:S(2)}) collective-permute-start(bf16[256,128]{1,0:T(8,128)(2,1)S(1)} %get-tuple-element.48), channel_id=1, source_target_pairs={{0,4},{4,0},{8,12},{12,8},{16,20},{20,16},{24,28},{28,24},{32,36},... | collective-permute-start | bytes 196616 | tf_op jit(solution)/shard_map/ppermute | solution.py:435
  32.0 4.9 %collective-permute-start.12 = (bf16[512,128]{1,0:T(8,128)(2,1)S(1)}, bf16[512,128]{1,0:T(8,128)(2,1)S(1)}, u32[]{:S(2)}, u32[]{:S(2)}) collective-permute-start(bf16[512,128]{1,0:T(8,128)(2,1)S(1)} %constant_dynamic-update-slice_fusion.2), channel_id=1, source_target_pairs={{0,8},{4,36},{8,16},{12,44},{16,24},{20,52},{24,0},{28,60},{32,40}... | collective-permute-start | bytes 393224 | tf_op jit(solution)/shard_map/ppermute | solution.py:422
  32.1 7.1 %collective-permute-start.14 = (bf16[512,128]{1,0:T(8,128)(2,1)S(1)}, bf16[512,128]{1,0:T(8,128)(2,1)S(1)}, u32[]{:S(2)}, u32[]{:S(2)}) collective-permute-start(bf16[512,128]{1,0:T(8,128)(2,1)S(1)} %constant_dynamic-update-slice_fusion.2), channel_id=1, source_target_pairs={{0,16},{4,68},{8,24},{12,76},{16,0},{20,84},{24,8},{28,92},{32,48}... | collective-permute-start | bytes 393224 | tf_op jit(solution)/shard_map/ppermute | solution.py:422
  33.2 6.1 %collective-permute-start.13 = (bf16[512,128]{1,0:T(8,128)(2,1)S(1)}, bf16[512,128]{1,0:T(8,128)(2,1)S(1)}, u32[]{:S(2)}, u32[]{:S(2)}) collective-permute-start(bf16[512,128]{1,0:T(8,128)(2,1)S(1)} %constant_dynamic-update-slice_fusion.2), channel_id=1, source_target_pairs={{0,24},{4,100},{8,0},{12,108},{16,8},{20,116},{24,16},{28,124},{32... | collective-permute-start | bytes 393224 | tf_op jit(solution)/shard_map/ppermute | solution.py:422
  39.3 10.5 %collective-permute-start.15 = (bf16[2048,128]{1,0:T(8,128)(2,1)S(1)}, bf16[2048,128]{1,0:T(8,128)(2,1)S(1)}, u32[]{:S(2)}, u32[]{:S(2)}) collective-permute-start(bf16[2048,128]{1,0:T(8,128)(2,1)S(1)} %constant_dynamic-update-slice_fusion.9.refs_0_), channel_id=1, source_target_pairs={{0,32},{4,12},{8,40},{12,20},{16,48},{20,28},{24,56},{28,4},{32,64... | collective-permute-start | bytes 1572872 | tf_op jit(solution)/shard_map/ppermute | solution.py:427
  39.4 10.8 %collective-permute-start.17 = (bf16[2048,128]{1,0:T(8,128)(2,1)S(1)}, bf16[2048,128]{1,0:T(8,128)(2,1)S(1)}, u32[]{:S(2)}, u32[]{:S(2)}) collective-permute-start(bf16[2048,128]{1,0:T(8,128)(2,1)S(1)} %constant_dynamic-update-slice_fusion.9.refs_0_), channel_id=1, source_target_pairs={{0,96},{4,28},{8,104},{12,4},{16,112},{20,12},{24,120},{28,20},{32... | collective-permute-start | bytes 1572872 | tf_op jit(solution)/shard_map/ppermute | solution.py:427
  49.8 9.9 %collective-permute-start.16 = (bf16[2048,128]{1,0:T(8,128)(2,1)S(1)}, bf16[2048,128]{1,0:T(8,128)(2,1)S(1)}, u32[]{:S(2)}, u32[]{:S(2)}) collective-permute-start(bf16[2048,128]{1,0:T(8,128)(2,1)S(1)} %constant_dynamic-update-slice_fusion.9.refs_0_), channel_id=1, source_target_pairs={{0,64},{4,20},{8,72},{12,28},{16,80},{20,4},{24,88},{28,12},{32,96... | collective-permute-start | bytes 1572872 | tf_op jit(solution)/shard_map/ppermute | solution.py:431
  62.9 2.9 %collective-permute-start.18 = (bf16[128,1024]{1,0:T(8,128)(2,1)S(1)}, bf16[128,1024]{1,0:T(8,128)(2,1)S(1)}, u32[]{:S(2)}, u32[]{:S(2)}) collective-permute-start(bf16[128,1024]{1,0:T(8,128)(2,1)S(1)} %get-tuple-element.68), channel_id=1, source_target_pairs={{0,4},{4,0},{8,12},{12,8},{16,20},{20,16},{24,28},{28,24},{32,36},... | collective-permute-start | bytes 786440 | tf_op jit(solution)/shard_map/ppermute | solution.py:435
